TPU v7x, 32 devices: a whole 2x2x4 slice. The times are simulated.
32 devices in a mesh: dp: 8 (over y, x, core), tensor: 4 (over z).
Axes of the slice: x: 2, y: 2, z: 4, core: 2. Of those that a mesh axis runs over, the one named last changes fastest.
Arguments:
- tokens: bfloat16 [8, 1024, 1024], P('dp', 'tensor'), may hold values from -6 to 6
- segment_ids: int32 [8, 1024], P('dp'), may hold values from 0 to 7, as said below
- norm1_gain: float32 [1024], replicated, may hold values from 0.25 to 1.75
- norm1_bias: float32 [1024], replicated, may hold values from -1.75 to 1.75
- proj_weight: bfloat16 [1024, 3, 1024], P(None, None, 'tensor'), may hold values from -0.1875 to 0.1875
- proj_bias: float32 [3, 1024], P(None, 'tensor'), may hold values from -1.75 to 1.75
- short_weight: float32 [3, 3, 1024], P(None, None, 'tensor'), may hold values from -3.5 to 3.5
- short_bias: float32 [3, 1024], P(None, 'tensor'), may hold values from -1.75 to 1.75
- embed_weight: float32 [33, 64], replicated, may hold values from -1 to 1
- embed_bias: float32 [64], replicated, may hold values from -3 to 3
- sine_freq: float32 [3, 64], replicated, may hold values from 0.5 to 2
- inner_weight: float32 [2, 64, 64], replicated, may hold values from -0.75 to 0.75
- inner_bias: float32 [2, 64], replicated, may hold values from -3 to 3
- filter_weight: float32 [64, 1024], P(None, 'tensor'), may hold values from -0.09375 to 0.09375
- decay_rate: float32 [1024], P('tensor'), may hold values from 0.5 to 64
- skip_gain: float32 [1024], P('tensor'), may hold values from -6 to 6
- out_weight: bfloat16 [1024, 1024], P('tensor'), may hold values from -0.1875 to 0.1875
- out_bias: float32 [1024], replicated, may hold values from -1.75 to 1.75
- norm2_gain: float32 [1024], replicated, may hold values from 0.25 to 1.75
- norm2_bias: float32 [1024], replicated, may hold values from -1.75 to 1.75
- up_weight: bfloat16 [1024, 4096], P(None, 'tensor'), may hold values from -0.1875 to 0.1875
- up_bias: float32 [4096], P('tensor'), may hold values from -1.75 to 1.75
- down_weight: bfloat16 [4096, 1024], P('tensor'), may hold values from -0.1875 to 0.1875
- down_bias: float32 [1024], replicated, may hold values from -1.75 to 1.75
- cotangent: bfloat16 [8, 1024, 1024], P('dp', 'tensor'), may hold values from -6 to 6
Outputs:
- layer_out: bfloat16 [8, 1024, 1024], P('dp', 'tensor')
- grad_tokens: float32 [8, 1024, 1024], P('dp', 'tensor')
- grad_norm1_gain: float32 [1024], replicated
- grad_norm1_bias: float32 [1024], replicated
- grad_proj_weight: float32 [1024, 3, 1024], P(None, None, 'tensor')
- grad_proj_bias: float32 [3, 1024], P(None, 'tensor')
- grad_short_weight: float32 [3, 3, 1024], P(None, None, 'tensor')
- grad_short_bias: float32 [3, 1024], P(None, 'tensor')
- grad_embed_weight: float32 [33, 64], replicated
- grad_embed_bias: float32 [64], replicated
- grad_sine_freq: float32 [3, 64], replicated
- grad_inner_weight: float32 [2, 64, 64], replicated
- grad_inner_bias: float32 [2, 64], replicated
- grad_filter_weight: float32 [64, 1024], P(None, 'tensor')
- grad_skip_gain: float32 [1024], P('tensor')
- grad_out_weight: float32 [1024, 1024], P('tensor')
- grad_out_bias: float32 [1024], replicated
- grad_norm2_gain: float32 [1024], replicated
- grad_norm2_bias: float32 [1024], replicated
- grad_up_weight: float32 [1024, 4096], P(None, 'tensor')
- grad_up_bias: float32 [4096], P('tensor')
- grad_down_weight: float32 [4096, 1024], P('tensor')
- grad_down_bias: float32 [1024], replicated
Inputs may be any that keep to these rules, and one draw needn't show every extreme that they name: Within a row segment_ids never fall, start at 0 and rise by one at each of 7 document boundaries, so every document is non-empty. Every boundary lies within the first 256 or the last 256 positions of its row, so the document at position 255 covers all positions from 255 to 768, and every other document lies within the first or the last 256 positions.
All inputs are finite; a program needn't handle non-finite values.
Results may differ from a plain program's by a relative error of at most 0.015.
Values may be sent and summed in bfloat16 or wider, within the bound.
A program may use at most 384 MiB of HBM per device.

v0:
```python
import jax
import jax.numpy as jnp
from jax import lax
from jax.sharding import PartitionSpec as P

FEAT = 33
SEQ = 1024
NDOC = 8


EPS = 1e-05
HIGH = lax.Precision.HIGHEST
SHIFT = 0.1


def layer_norm(values, norm_gain, norm_bias):
    average = jnp.mean(values, axis=-1, keepdims=True)
    centered = values - average
    variance = jnp.mean(centered * centered, axis=-1, keepdims=True)
    return centered * lax.rsqrt(variance + EPS) * norm_gain + norm_bias


def gelu_tanh(values):
    return jax.nn.gelu(values, approximate=True)


def position_features():
    places = jnp.arange(SEQ, dtype=jnp.float32)
    band_index = jnp.arange(1, (FEAT - 1) // 2 + 1, dtype=jnp.float32)
    angles = 2.0 * jnp.pi * places[:, None] * band_index[None, :] / SEQ
    return jnp.concatenate(
        [(places / (SEQ - 1))[:, None], jnp.cos(angles), jnp.sin(angles)], axis=1
    )


def make_filter(
    embed_weight, embed_bias, sine_freq, inner_weight, inner_bias, filter_weight, decay_rate
):
    places = jnp.arange(SEQ, dtype=jnp.float32)
    hidden = jnp.sin(
        sine_freq[0] * (jnp.dot(position_features(), embed_weight, precision=HIGH) + embed_bias)
    )
    for layer_index in range(2):
        hidden = jnp.sin(
            sine_freq[layer_index + 1]
            * (jnp.dot(hidden, inner_weight[layer_index], precision=HIGH) + inner_bias[layer_index])
        )
    filter_taps = jnp.dot(hidden, filter_weight, precision=HIGH)
    return filter_taps * (jnp.exp(-decay_rate[None, :] * places[:, None] / SEQ) + SHIFT)


def short_conv(values, segment, short_weight, short_bias):
    length = values.shape[1]
    running = short_bias[None, None] + short_weight[0][None, None] * values
    for lag_index in range(1, 3):
        shifted = jnp.concatenate(
            [jnp.zeros_like(values[:, :lag_index]), values[:, : length - lag_index]], axis=1
        )
        same_doc = jnp.concatenate(
            [
                jnp.zeros(segment[:, :lag_index].shape, jnp.float32),
                (segment[:, lag_index:] == segment[:, : length - lag_index]).astype(jnp.float32),
            ],
            axis=1,
        )
        running = (
            running + short_weight[lag_index][None, None] * shifted * same_doc[:, :, None, None]
        )
    return running


def block_size(length):
    return min(128, length // 4)


def toeplitz_block(taps_cm, lag_index, block_len):
    span = taps_cm.shape[1]
    places = jnp.arange(block_len, dtype=jnp.int32)
    offsets = lag_index * block_len + places[:, None] - places[None, :]
    valid = (offsets >= 0).astype(taps_cm.dtype)
    picked = jnp.take(taps_cm, jnp.clip(offsets, 0, span - 1), axis=1)
    return (picked * valid[None], offsets, valid)


def shift_blocks(pieces, lag_index, later):
    if lag_index == 0:
        return pieces
    block_count = pieces.shape[2]
    padding = jnp.zeros(pieces.shape[:2] + (lag_index,) + pieces.shape[3:], pieces.dtype)
    if later:
        return jnp.concatenate([pieces[:, :, lag_index:], padding], axis=2)
    return jnp.concatenate([padding, pieces[:, :, : block_count - lag_index]], axis=2)


def blocked_conv(pieces, taps_cm):
    block_count = pieces.shape[2]
    block_len = pieces.shape[3]
    running = jnp.zeros(pieces.shape, jnp.float32)
    for lag_index in range(block_count):
        toeplitz, unused_offsets, unused_valid = toeplitz_block(taps_cm, lag_index, block_len)
        running = running + jnp.einsum(
            "cgns,cts->cgnt",
            shift_blocks(pieces, lag_index, False),
            toeplitz,
            preferred_element_type=jnp.float32,
        )
    return running


def blocked_conv_back(grad_pieces, value_pieces, taps_cm):
    chan_count = value_pieces.shape[0]
    block_count = value_pieces.shape[2]
    block_len = value_pieces.shape[3]
    span = taps_cm.shape[1]
    grad_values = jnp.zeros(value_pieces.shape, jnp.float32)
    grad_taps = jnp.zeros((chan_count, span), jnp.float32)
    for lag_index in range(block_count):
        toeplitz, offsets, valid = toeplitz_block(taps_cm, lag_index, block_len)
        grad_values = grad_values + jnp.einsum(
            "cgnt,cts->cgns",
            shift_blocks(grad_pieces, lag_index, True),
            toeplitz,
            preferred_element_type=jnp.float32,
        )
        tap_part = jnp.einsum(
            "cgnt,cgns->cts",
            grad_pieces,
            shift_blocks(value_pieces, lag_index, False),
            preferred_element_type=jnp.float32,
        )
        grad_taps = grad_taps.at[:, jnp.clip(offsets, 0, span - 1)].add(
            tap_part * valid.astype(jnp.float32)[None]
        )
    return (grad_values, grad_taps)


def document_masks(segment):
    return (segment[:, None, :] == jnp.arange(NDOC, dtype=jnp.int32)[None, :, None]).astype(
        jnp.bfloat16
    )


def split_parts(segment_ids, shard_len):
    length = segment_ids.shape[1]
    main_doc = segment_ids[:, shard_len - 1]
    main_mask = (segment_ids == main_doc[:, None]).astype(jnp.bfloat16)
    others = (jnp.arange(NDOC, dtype=jnp.int32)[None, :] != main_doc[:, None]).astype(jnp.bfloat16)
    head_masks = document_masks(segment_ids[:, :shard_len]) * others[:, :, None]
    tail_masks = document_masks(segment_ids[:, length - shard_len :]) * others[:, :, None]
    return (main_mask, head_masks, tail_masks)


def to_blocks(values_cm, block_len):
    chan_count, group_count, length = values_cm.shape
    return values_cm.reshape(chan_count, group_count, length // block_len, block_len)


def spread_docs(values_cm, masks_b):
    chan_count, row_count, length = values_cm.shape
    return (masks_b[None] * values_cm[:, :, None, :]).reshape(chan_count, row_count * NDOC, length)


def join_regions(head, tail, length):
    chan_count, row_count, region_len = head.shape
    middle = jnp.zeros((chan_count, row_count, length - 2 * region_len), head.dtype)
    return jnp.concatenate([head, middle, tail], axis=2)


def region_conv(values_cm, masks_b, taps_cm):
    chan_count, row_count, region_len = values_cm.shape
    block_len = block_size(region_len)
    result = blocked_conv(
        to_blocks(spread_docs(values_cm, masks_b), block_len), taps_cm[:, :region_len]
    )
    result = result.reshape(chan_count, row_count, NDOC, region_len)
    return jnp.sum(result * masks_b[None].astype(jnp.float32), axis=2)


def region_conv_back(grad_cm, values_cm, masks_b, taps_cm):
    chan_count, row_count, region_len = values_cm.shape
    block_len = block_size(region_len)
    grad_values, grad_taps = blocked_conv_back(
        to_blocks(spread_docs(grad_cm, masks_b), block_len),
        to_blocks(spread_docs(values_cm, masks_b), block_len),
        taps_cm[:, :region_len],
    )
    grad_values = grad_values.reshape(chan_count, row_count, NDOC, region_len)
    return (jnp.sum(grad_values * masks_b[None].astype(jnp.float32), axis=2), grad_taps)


def causal_conv(values_b, segment_ids, taps_b, shard_len):
    row_count, length, chan_count = values_b.shape
    values_cm = jnp.transpose(values_b, (2, 0, 1))
    taps_cm = jnp.transpose(taps_b)
    main_mask, head_masks, tail_masks = split_parts(segment_ids, shard_len)
    block_len = block_size(length)
    main_in = values_cm * main_mask[None]
    main_out = blocked_conv(to_blocks(main_in, block_len), taps_cm).reshape(
        chan_count, row_count, length
    )
    main_out = main_out * main_mask[None].astype(jnp.float32)
    head = region_conv(values_cm[:, :, :shard_len], head_masks, taps_cm)
    tail = region_conv(values_cm[:, :, length - shard_len :], tail_masks, taps_cm)
    return jnp.transpose(main_out + join_regions(head, tail, length), (1, 2, 0))


def causal_conv_back(grad_b, values_b, segment_ids, taps_b, shard_len):
    row_count, length, chan_count = values_b.shape
    grad_cm = jnp.transpose(grad_b, (2, 0, 1))
    values_cm = jnp.transpose(values_b, (2, 0, 1))
    taps_cm = jnp.transpose(taps_b)
    main_mask, head_masks, tail_masks = split_parts(segment_ids, shard_len)
    block_len = block_size(length)
    main_grad = grad_cm * main_mask[None]
    main_in = values_cm * main_mask[None]
    grad_main, grad_taps = blocked_conv_back(
        to_blocks(main_grad, block_len), to_blocks(main_in, block_len), taps_cm
    )
    grad_main = grad_main.reshape(chan_count, row_count, length) * main_mask[None].astype(
        jnp.float32
    )
    grad_head, taps_head = region_conv_back(
        grad_cm[:, :, :shard_len], values_cm[:, :, :shard_len], head_masks, taps_cm
    )
    grad_tail, taps_tail = region_conv_back(
        grad_cm[:, :, length - shard_len :],
        values_cm[:, :, length - shard_len :],
        tail_masks,
        taps_cm,
    )
    grad_values = grad_main + join_regions(grad_head, grad_tail, length)
    grad_taps = grad_taps.at[:, :shard_len].add(taps_head + taps_tail)
    return (jnp.transpose(grad_values, (1, 2, 0)), jnp.transpose(grad_taps))


def body(
    tokens,
    segment_ids,
    norm1_gain,
    norm1_bias,
    proj_weight,
    proj_bias,
    short_weight,
    short_bias,
    embed_weight,
    embed_bias,
    sine_freq,
    inner_weight,
    inner_bias,
    filter_weight,
    decay_rate,
    skip_gain,
    out_weight,
    out_bias,
    norm2_gain,
    norm2_bias,
    up_weight,
    up_bias,
    down_weight,
    down_bias,
    cotangent,
):
    row_count, shard_len, model_width = tokens.shape
    groups = lax.axis_size("tensor")
    length = shard_len * groups
    channels = proj_weight.shape[2]
    flat_rows = row_count * length
    tokens_f = tokens.astype(jnp.float32)
    normed1, norm1_back = jax.vjp(layer_norm, tokens_f, norm1_gain, norm1_bias)
    first_rows = lax.all_gather(normed1.astype(jnp.bfloat16), "tensor", axis=1, tiled=True)
    flat_first = first_rows.reshape(flat_rows, model_width)
    proj_flat = proj_weight.reshape(model_width, 3 * channels)
    projected = (
        jnp.dot(flat_first, proj_flat, preferred_element_type=jnp.float32).reshape(
            row_count, length, 3, channels
        )
        + proj_bias[None, None]
    )

    def local_short(values_in, weights_in, biases_in):
        return short_conv(values_in, segment_ids, weights_in, biases_in)

    mixed, short_back = jax.vjp(local_short, projected, short_weight, short_bias)
    gate_out = mixed[:, :, 0]
    gate_in = mixed[:, :, 1]
    values = mixed[:, :, 2]
    product = values * gate_in
    product_b = product.astype(jnp.bfloat16)

    def local_filter(embed_w, embed_b, freq_vals, inner_w, inner_b, filter_w):
        return make_filter(embed_w, embed_b, freq_vals, inner_w, inner_b, filter_w, decay_rate)

    filter_taps, filter_back = jax.vjp(
        local_filter, embed_weight, embed_bias, sine_freq, inner_weight, inner_bias, filter_weight
    )
    taps_b = filter_taps.astype(jnp.bfloat16)
    convolved = causal_conv(product_b, segment_ids, taps_b, shard_len)
    summed = convolved + skip_gain * product
    gated_b = (summed * gate_out).astype(jnp.bfloat16)
    flat_gated = gated_b.reshape(flat_rows, channels)
    partial_mix = jnp.dot(flat_gated, out_weight, preferred_element_type=jnp.float32).reshape(
        row_count, length, model_width
    )
    residual = (
        tokens_f
        + lax.psum_scatter(partial_mix, "tensor", scatter_dimension=1, tiled=True)
        + out_bias
    )
    normed2, norm2_back = jax.vjp(layer_norm, residual, norm2_gain, norm2_bias)
    second_rows = lax.all_gather(normed2.astype(jnp.bfloat16), "tensor", axis=1, tiled=True)
    flat_second = second_rows.reshape(flat_rows, model_width)
    hidden_pre = jnp.dot(flat_second, up_weight, preferred_element_type=jnp.float32) + up_bias
    active, gelu_back = jax.vjp(gelu_tanh, hidden_pre)
    active_b = active.astype(jnp.bfloat16)
    partial_mlp = jnp.dot(active_b, down_weight, preferred_element_type=jnp.float32).reshape(
        row_count, length, model_width
    )
    mlp_out = lax.psum_scatter(
        partial_mlp.astype(jnp.bfloat16), "tensor", scatter_dimension=1, tiled=True
    ).astype(jnp.float32)
    layer_out = (residual + mlp_out + down_bias).astype(jnp.bfloat16)
    grad_out = cotangent.astype(jnp.float32)
    grad_down_bias = jnp.sum(grad_out, axis=(0, 1))
    grad_rows = lax.all_gather(cotangent, "tensor", axis=1, tiled=True)
    flat_grad = grad_rows.reshape(flat_rows, model_width)
    grad_down_weight = jnp.einsum(
        "nf,nd->fd", active_b, flat_grad, preferred_element_type=jnp.float32
    )
    grad_active = jnp.einsum(
        "nd,fd->nf", flat_grad, down_weight, preferred_element_type=jnp.float32
    )
    grad_hidden = gelu_back(grad_active)[0]
    grad_up_bias = jnp.sum(grad_hidden, axis=0)
    hidden_b = grad_hidden.astype(jnp.bfloat16)
    grad_up_weight = jnp.einsum(
        "nd,nf->df", flat_second, hidden_b, preferred_element_type=jnp.float32
    )
    grad_second = jnp.einsum(
        "nf,df->nd", hidden_b, up_weight, preferred_element_type=jnp.float32
    ).reshape(row_count, length, model_width)
    grad_normed2 = lax.psum_scatter(grad_second, "tensor", scatter_dimension=1, tiled=True)
    grad_residual, grad_norm2_gain, grad_norm2_bias = norm2_back(grad_normed2)
    grad_residual = grad_residual + grad_out
    grad_resid_b = lax.all_gather(grad_residual.astype(jnp.bfloat16), "tensor", axis=1, tiled=True)
    grad_out_bias = jnp.sum(grad_residual, axis=(0, 1))
    flat_resid = grad_resid_b.reshape(flat_rows, model_width)
    grad_out_weight = jnp.einsum(
        "nc,nd->cd", flat_gated, flat_resid, preferred_element_type=jnp.float32
    )
    grad_gated = jnp.einsum(
        "nd,cd->nc", flat_resid, out_weight, preferred_element_type=jnp.float32
    ).reshape(row_count, length, channels)
    grad_summed = grad_gated * gate_out
    grad_gate_out = grad_gated * summed
    grad_skip_gain = jnp.sum(grad_summed * product, axis=(0, 1))
    grad_conv, grad_taps = causal_conv_back(
        grad_summed.astype(jnp.bfloat16), product_b, segment_ids, taps_b, shard_len
    )
    grad_product = grad_conv + grad_summed * skip_gain
    grad_mixed = jnp.stack([grad_gate_out, grad_product * values, grad_product * gate_in], axis=2)
    grad_projected, grad_short_weight, grad_short_bias = short_back(grad_mixed)
    (
        grad_embed_weight,
        grad_embed_bias,
        grad_sine_freq,
        grad_inner_weight,
        grad_inner_bias,
        grad_filter_weight,
    ) = filter_back(grad_taps)
    grad_proj_bias = jnp.sum(grad_projected, axis=(0, 1))
    projected_b = grad_projected.astype(jnp.bfloat16).reshape(flat_rows, 3 * channels)
    grad_proj_weight = jnp.einsum(
        "nd,nk->dk", flat_first, projected_b, preferred_element_type=jnp.float32
    ).reshape(model_width, 3, channels)
    grad_first = jnp.einsum(
        "nk,dk->nd", projected_b, proj_flat, preferred_element_type=jnp.float32
    ).reshape(row_count, length, model_width)
    grad_normed1 = lax.psum_scatter(
        grad_first.astype(jnp.bfloat16), "tensor", scatter_dimension=1, tiled=True
    ).astype(jnp.float32)
    grad_tokens, grad_norm1_gain, grad_norm1_bias = norm1_back(grad_normed1)
    grad_tokens = grad_tokens + grad_residual
    (
        grad_proj_weight,
        grad_proj_bias,
        grad_short_weight,
        grad_short_bias,
        grad_filter_weight,
        grad_skip_gain,
        grad_out_weight,
        grad_up_weight,
        grad_up_bias,
        grad_down_weight,
    ) = (
        lax.psum(grad_proj_weight.astype(jnp.bfloat16), "dp").astype(jnp.float32),
        lax.psum(grad_proj_bias.astype(jnp.bfloat16), "dp").astype(jnp.float32),
        lax.psum(grad_short_weight.astype(jnp.bfloat16), "dp").astype(jnp.float32),
        lax.psum(grad_short_bias.astype(jnp.bfloat16), "dp").astype(jnp.float32),
        lax.psum(grad_filter_weight.astype(jnp.bfloat16), "dp").astype(jnp.float32),
        lax.psum(grad_skip_gain.astype(jnp.bfloat16), "dp").astype(jnp.float32),
        lax.psum(grad_out_weight.astype(jnp.bfloat16), "dp").astype(jnp.float32),
        lax.psum(grad_up_weight.astype(jnp.bfloat16), "dp").astype(jnp.float32),
        lax.psum(grad_up_bias.astype(jnp.bfloat16), "dp").astype(jnp.float32),
        lax.psum(grad_down_weight.astype(jnp.bfloat16), "dp").astype(jnp.float32),
    )
    (
        grad_norm1_gain,
        grad_norm1_bias,
        grad_out_bias,
        grad_norm2_gain,
        grad_norm2_bias,
        grad_down_bias,
        grad_embed_weight,
        grad_embed_bias,
        grad_sine_freq,
        grad_inner_weight,
        grad_inner_bias,
    ) = lax.psum(
        (
            grad_norm1_gain,
            grad_norm1_bias,
            grad_out_bias,
            grad_norm2_gain,
            grad_norm2_bias,
            grad_down_bias,
            grad_embed_weight,
            grad_embed_bias,
            grad_sine_freq,
            grad_inner_weight,
            grad_inner_bias,
        ),
        ("dp", "tensor"),
    )
    return (
        layer_out,
        grad_tokens,
        grad_norm1_gain,
        grad_norm1_bias,
        grad_proj_weight,
        grad_proj_bias,
        grad_short_weight,
        grad_short_bias,
        grad_embed_weight,
        grad_embed_bias,
        grad_sine_freq,
        grad_inner_weight,
        grad_inner_bias,
        grad_filter_weight,
        grad_skip_gain,
        grad_out_weight,
        grad_out_bias,
        grad_norm2_gain,
        grad_norm2_bias,
        grad_up_weight,
        grad_up_bias,
        grad_down_weight,
        grad_down_bias,
    )


def solution(mesh):
    return jax.shard_map(
        body,
        mesh=mesh,
        in_specs=(
            P("dp", "tensor", None),
            P("dp", None),
            P(),
            P(),
            P(None, None, "tensor"),
            P(None, "tensor"),
            P(None, None, "tensor"),
            P(None, "tensor"),
            P(),
            P(),
            P(),
            P(),
            P(),
            P(None, "tensor"),
            P("tensor"),
            P("tensor"),
            P("tensor", None),
            P(),
            P(),
            P(),
            P(None, "tensor"),
            P("tensor"),
            P("tensor", None),
            P(),
            P("dp", "tensor", None),
        ),
        out_specs=(
            P("dp", "tensor", None),
            P("dp", "tensor", None),
            P(),
            P(),
            P(None, None, "tensor"),
            P(None, "tensor"),
            P(None, None, "tensor"),
            P(None, "tensor"),
            P(),
            P(),
            P(),
            P(),
            P(),
            P(None, "tensor"),
            P("tensor"),
            P("tensor", None),
            P(),
            P(),
            P(),
            P(None, "tensor"),
            P("tensor"),
            P("tensor", None),
            P(),
        ),
        check_vma=False,
    )
```

profile of v0, /device:TPU:0, one launch (start us, length us, event | category | flops | bytes accessed | tf_op | source)
XLA Modules:
  0.0 2853.8 jit_solution(10428988696006335675)
XLA Ops:
  37.0 17.0 gather_fusion.11
  54.0 17.0 gather_fusion.10
  71.1 17.0 gather_fusion.9
  88.1 17.0 gather_fusion.8
  135.0 65.2 %gather_fusion.7 = bf16[16384,256]{1,0:T(8,128)(2,1)} fusion(bf16[256,1024]{0,1:T(8,128)(2,1)S(1)} %fusion.198, s32[16384]{0:T(1024)S(1)} %bitcast_clamp_fusion), kind=kCustom, calls=%fused_computation.8.clone | custom fusion | bytes 16842752 | tf_op jit(solution)/shard_map/jit(_take)/gather | solution.py:81
  200.3 12.4 copy.186
  212.6 65.2 %gather_fusion.6 = bf16[16384,256]{1,0:T(8,128)(2,1)} fusion(bf16[256,1024]{0,1:T(8,128)(2,1)S(1)} %fusion.198, s32[16384]{0:T(1024)S(1)} %bitcast_clamp_fusion.1), kind=kCustom, calls=%fused_computation.7.clone | custom fusion | bytes 16842752 | tf_op jit(solution)/shard_map/jit(_take)/gather | solution.py:81
  277.8 12.4 copy.184
  290.3 65.2 %gather_fusion.5 = bf16[16384,256]{1,0:T(8,128)(2,1)} fusion(bf16[256,1024]{0,1:T(8,128)(2,1)S(1)} %fusion.198, s32[16384]{0:T(1024)S(1)} %bitcast_clamp_fusion.2), kind=kCustom, calls=%fused_computation.6.clone | custom fusion | bytes 16842752 | tf_op jit(solution)/shard_map/jit(_take)/gather | solution.py:81
  355.4 12.4 copy.182
  367.8 65.2 %gather_fusion.4 = bf16[16384,256]{1,0:T(8,128)(2,1)} fusion(bf16[256,1024]{0,1:T(8,128)(2,1)S(1)} %fusion.198, s32[16384]{0:T(1024)S(1)} %bitcast_clamp_fusion.3), kind=kCustom, calls=%fused_computation.5.clone | custom fusion | bytes 16842752 | tf_op jit(solution)/shard_map/jit(_take)/gather | solution.py:81
  433.1 12.4 copy.180
  445.5 65.2 %gather_fusion.3 = bf16[16384,256]{1,0:T(8,128)(2,1)} fusion(bf16[256,1024]{0,1:T(8,128)(2,1)S(1)} %fusion.198, s32[16384]{0:T(1024)S(1)} %copy-done.100), kind=kCustom, calls=%fused_computation.4.clone | custom fusion | bytes 16842752 | tf_op jit(solution)/shard_map/jit(_take)/gather | solution.py:81
  510.7 12.4 copy.178
  523.1 65.2 %gather_fusion.2 = bf16[16384,256]{1,0:T(8,128)(2,1)} fusion(bf16[256,1024]{0,1:T(8,128)(2,1)S(1)} %fusion.198, s32[16384]{0:T(1024)S(1)} %copy-done.99), kind=kCustom, calls=%fused_computation.3.clone | custom fusion | bytes 16842752 | tf_op jit(solution)/shard_map/jit(_take)/gather | solution.py:81
  588.3 12.4 copy.176
  600.8 65.3 %gather_fusion.1 = bf16[16384,256]{1,0:T(8,128)(2,1)} fusion(bf16[256,1024]{0,1:T(8,128)(2,1)S(1)} %fusion.198, s32[16384]{0:T(1024)S(1)} %copy-done.98), kind=kCustom, calls=%fused_computation.2.clone | custom fusion | bytes 16842752 | tf_op jit(solution)/shard_map/jit(_take)/gather | solution.py:81
  666.0 12.9 copy.174
  678.9 65.2 %gather_fusion = bf16[16384,256]{1,0:T(8,128)(2,1)} fusion(bf16[256,1024]{0,1:T(8,128)(2,1)S(1)} %fusion.198, s32[16384]{0:T(1024)S(1)} %copy-done.97), kind=kCustom, calls=%fused_computation.clone | custom fusion | bytes 16842752 | tf_op jit(solution)/shard_map/jit(_take)/gather | solution.py:81
  744.2 12.4 copy.171
  827.4 9.3 multiply_reduce_fusion.2
  837.7 9.2 multiply_reduce_fusion.3
  908.7 79.6 %reduce-scatter.5.cloned.1.call-done = f32[1,256,1024]{2,1,0:T(8,128)} async-done(((f32[1,1024,1024]{2,1,0:T(8,128)}), f32[1,256,1024]{2,1,0:T(8,128)}) %reduce-scatter.5.cloned.1.call-update) | async-done | bytes 1048592 | tf_op jit(solution)/shard_map/reduce_scatter | solution.py:306
  991.8 46.0 %all-gather.7.cloned.1.call-done = bf16[1,1024,1024]{2,1,0:T(8,128)(2,1)} async-done(((bf16[1,256,1024]{2,1,0:T(8,128)(2,1)}), bf16[1,1024,1024]{2,1,0:T(8,128)(2,1)}) %all-gather.7.cloned.1.call-update) | async-done | bytes 2097168 | tf_op jit(solution)/shard_map/all_gather | solution.py:310
  1044.3 39.6 %all-gather.9.cloned.1.call-done = bf16[1,1024,1024]{2,1,0:T(8,128)(2,1)} async-done(((bf16[1,256,1024]{2,1,0:T(8,128)(2,1)}), bf16[1,1024,1024]{2,1,0:T(8,128)(2,1)}) %all-gather.9.cloned.1.call-update) | async-done | bytes 2097168 | tf_op jit(solution)/shard_map/all_gather | solution.py:324
  1084.0 8.1 fusion.495
  1108.7 64.8 %reduce-scatter.9.cloned.1.call-done = f32[1,256,1024]{2,1,0:T(8,128)} async-done(((f32[1,1024,1024]{2,1,0:T(8,128)}), f32[1,256,1024]{2,1,0:T(8,128)}) %reduce-scatter.9.cloned.1.call-update) | async-done | bytes 1048592 | tf_op jit(solution)/shard_map/reduce_scatter | solution.py:341
  1175.7 44.4 %reduce-scatter.7.cloned.1.call-done = bf16[1,256,1024]{2,1,0:T(8,128)(2,1)} async-done(((bf16[1,1024,1024]{2,1,0:T(8,128)(2,1)}), bf16[1,256,1024]{2,1,0:T(8,128)(2,1)}) %reduce-scatter.7.cloned.1.call-update) | async-done | bytes 524304 | tf_op jit(solution)/shard_map/reduce_scatter | solution.py:318
  1248.4 21.6 all-gather.11.cloned.1.call-done
  1341.6 9.3 multiply_reduce_fusion.1
  1351.2 9.1 multiply_reduce_fusion
  1387.0 8.0 copy.229
  1401.3 7.9 copy.233
  1414.0 7.9 copy.230
  1426.8 7.8 copy.234
  1439.5 8.2 copy.231
  1468.1 7.8 copy.228
  1476.0 24.9 scatter_custom_fusion.12
  1500.9 25.5 scatter_custom_fusion.8
  1533.7 17.8 copy.253
  1558.7 17.8 copy.252
  1583.6 17.8 copy.251
  1608.5 17.8 copy.250
  1633.4 17.8 copy.255
  1658.4 17.8 copy.254
  1683.4 17.8 copy.257
  1708.4 17.8 copy.256
  1726.1 23.0 scatter_fusion.10
  1749.1 23.0 scatter_fusion.7
  1772.1 23.0 scatter_fusion.11
  1795.1 23.4 scatter_fusion.8
  1818.6 23.0 scatter_fusion.12
  1841.6 23.0 scatter_fusion.9
  1865.3 98.9 %scatter_custom_fusion = f32[256,1024]{0,1:T(8,128)S(1)} fusion(s32[16384]{0:T(1024)} %fusion.329, f32[16384,256]{1,0:T(8,128)} %bitcast.652, f32[]{:T(128)} %constant.50.clone.1), kind=kCustom, calls=%fused_computation.371 | custom fusion | flops 4194304 | bytes 1049088 | tf_op jit(solution)/shard_map/scatter-add | solution.py:131
  1964.2 88.5 %scatter_fusion = f32[256,1024]{0,1:T(8,128)S(1)} fusion(f32[256,1024]{0,1:T(8,128)S(1)} %scatter_custom_fusion, s32[16384]{0:T(1024)S(1)} %copy-done.91, f32[16384,256]{1,0:T(8,128)} %bitcast.631), kind=kCustom, calls=%fused_computation.13 | custom fusion | flops 4194304 | bytes 50397184 | tf_op jit(solution)/shard_map/scatter-add | solution.py:131
  2052.7 88.7 %scatter_fusion.1 = f32[256,1024]{0,1:T(8,128)S(1)} fusion(f32[256,1024]{0,1:T(8,128)S(1)} %scatter_fusion, s32[16384]{0:T(1024)S(1)} %copy-done.90, f32[16384,256]{1,0:T(8,128)} %bitcast.628), kind=kCustom, calls=%fused_computation.14 | custom fusion | flops 4194304 | bytes 50397184 | tf_op jit(solution)/shard_map/scatter-add | solution.py:131
  2141.4 88.5 %scatter_fusion.2 = f32[256,1024]{0,1:T(8,128)S(1)} fusion(f32[256,1024]{0,1:T(8,128)S(1)} %scatter_fusion.1, s32[16384]{0:T(1024)S(1)} %copy-done.89, f32[16384,256]{1,0:T(8,128)} %bitcast.627), kind=kCustom, calls=%fused_computation.15 | custom fusion | flops 4194304 | bytes 50397184 | tf_op jit(solution)/shard_map/scatter-add | solution.py:131
  2230.0 88.5 %scatter_fusion.3 = f32[256,1024]{0,1:T(8,128)S(1)} fusion(f32[256,1024]{0,1:T(8,128)S(1)} %scatter_fusion.2, s32[16384]{0:T(1024)S(1)} %copy-done.87, f32[16384,256]{1,0:T(8,128)} %bitcast.632), kind=kCustom, calls=%fused_computation.16 | custom fusion | flops 4194304 | bytes 50397184 | tf_op jit(solution)/shard_map/scatter-add | solution.py:131
  2318.5 88.5 %scatter_fusion.4 = f32[256,1024]{0,1:T(8,128)S(1)} fusion(f32[256,1024]{0,1:T(8,128)S(1)} %scatter_fusion.3, s32[16384]{0:T(1024)S(1)} %copy-done.86, f32[16384,256]{1,0:T(8,128)} %bitcast.629), kind=kCustom, calls=%fused_computation.17 | custom fusion | flops 4194304 | bytes 50397184 | tf_op jit(solution)/shard_map/scatter-add | solution.py:131
  2407.1 88.5 %scatter_fusion.5 = f32[256,1024]{0,1:T(8,128)S(1)} fusion(f32[256,1024]{0,1:T(8,128)S(1)} %scatter_fusion.4, s32[16384]{0:T(1024)S(1)} %copy-done.85, f32[16384,256]{1,0:T(8,128)} %bitcast.633), kind=kCustom, calls=%fused_computation.18 | custom fusion | flops 4194304 | bytes 50397184 | tf_op jit(solution)/shard_map/scatter-add | solution.py:131
  2495.6 88.6 %scatter_fusion.6 = f32[256,1024]{0,1:T(8,128)S(1)} fusion(f32[256,1024]{0,1:T(8,128)S(1)} %scatter_fusion.5, s32[16384]{0:T(1024)S(1)} %copy-done.84, f32[16384,256]{1,0:T(8,128)} %bitcast.630), kind=kCustom, calls=%fused_computation.19 | custom fusion | flops 4194304 | bytes 50397184 | tf_op jit(solution)/shard_map/scatter-add | solution.py:131
  2614.5 25.6 all-reduce.42
  2643.7 52.4 %all-reduce.49.cloned.1.call-done = (bf16[1024,3,256]{2,0,1:T(8,128)(2,1)}, bf16[256,1024]{1,0:T(8,128)(2,1)}, bf16[1024,1024]{1,0:T(8,128)(2,1)}, bf16[1024,1024]{1,0:T(8,128)(2,1)}) async-done(((bf16[1024,3,256]{2,0,1:T(8,128)(2,1)}, bf16[256,1024]{1,0:T(8,128)(2,1)}, bf16[1024,1024]{1,0:T(8,128)(2,1)}, bf16[1024,1024]{1,0:T(8,128)(2,1)}), (bf16[1024,3,256]{2,0,1:T(8,128)(2,1)}, ...) | async-done | bytes 6291472 | tf_op jit(solution)/shard_map/psum | solution.py:395
  2706.8 126.0 %all-reduce.47.cloned.1.call-done = (f32[1024]{0:T(1024)}, f32[1024]{0:T(1024)}, f32[33,64]{1,0:T(8,128)}, f32[64]{0:T(128)}, f32[3,64]{1,0:T(4,128)}, /*index=5...) async-done(((f32[1024]{0:T(1024)}, f32[1024]{0:T(1024)}, f32[33,64]{1,0:T(8,128)}, ...) | async-done | bytes 67344 | tf_op jit(solution)/shard_map/psum | solution.py:418
  (826 shorter events, 504.4 us)
Async XLA Ops:
  7.2 1076.8 %copy-start = (bf16[1024,1024]{1,0:T(8,128)(2,1)S(1)}, bf16[1024,1024]{1,0:T(8,128)(2,1)}, u32[]{:S(2)}) copy-start(bf16[1024,1024]{1,0:T(8,128)(2,1)} %param.53) | copy-start | bytes 6291460
  7.2 21.5 copy-start.92
  7.2 24.9 copy-start.233
  7.2 760.2 %all-gather.5.cloned.1.call-start = ((), (), s32[]{:S(2)}) async-start(), calls=%async_computation.4 | async-start | bytes 2621440 | tf_op jit(solution)/shard_map/all_gather | solution.py:270
  13.3 974.9 %reduce-scatter.5.cloned.1.call-start = ((), (), s32[]{:S(2)}) async-start(), calls=%async_computation.5 | async-start | bytes 5242880 | tf_op jit(solution)/shard_map/reduce_scatter | solution.py:306
  13.3 18.0 copy-start.187
  13.4 18.0 copy-start.190
  13.4 17.9 copy-start.193
  13.4 17.9 copy-start.196
  13.4 17.9 copy-start.199
  13.4 17.9 copy-start.202
  13.5 17.9 copy-start.205
  13.5 17.9 copy-start.208
  13.5 17.9 copy-start.211
  744.2 18.0 copy-start.188
  744.2 18.7 copy-start.191
  744.2 19.5 copy-start.194
  744.2 20.2 copy-start.197
  744.2 21.0 copy-start.200
  744.2 21.7 copy-start.203
  744.2 22.5 copy-start.206
  760.8 76.9 %copy-start.75 = (bf16[64,64]{1,0:T(8,128)(2,1)}, bf16[64,64]{1,0:T(8,128)(2,1)S(1)}, u32[]{:S(2)}) copy-start(bf16[64,64]{1,0:T(8,128)(2,1)S(1)} %get-tuple-element.132) | copy-start | bytes 24580
  760.8 76.9 %copy-start.101 = (pred[64,64]{1,0:T(8,128)(4,1)}, pred[64,64]{1,0:T(8,128)(4,1)S(1)}, u32[]{:S(2)}) copy-start(pred[64,64]{1,0:T(8,128)(4,1)S(1)} %get-tuple-element.131) | copy-start | bytes 12292
  827.4 20.4 copy-start.44
  905.9 82.4 %copy-start.220 = (f32[1024]{0:T(1024)S(1)}, f32[1024]{0:T(1024)}, u32[]{:S(2)}) copy-start(f32[1024]{0:T(1024)} %param.48) | copy-start | bytes 12292
  908.6 81.5 %copy-start.123 = (f32[1024]{0:T(1024)S(1)}, f32[1024]{0:T(1024)}, u32[]{:S(2)}) copy-start(f32[1024]{0:T(1024)} %param.49) | copy-start | bytes 12292
  908.6 81.5 %copy-start.221 = (f32[1024]{0:T(1024)S(1)}, f32[1024]{0:T(1024)}, u32[]{:S(2)}) copy-start(f32[1024]{0:T(1024)} %param.50) | copy-start | bytes 12292
  908.6 129.2 %all-gather.7.cloned.1.call-start = ((), (), s32[]{:S(2)}) async-start(), calls=%async_computation.6 | async-start | bytes 2621440 | tf_op jit(solution)/shard_map/all_gather | solution.py:310
  991.2 92.8 %all-gather.9.cloned.1.call-start = ((), (), s32[]{:S(2)}) async-start(), calls=%async_computation.8 | async-start | bytes 2621440 | tf_op jit(solution)/shard_map/all_gather | solution.py:324
  991.7 92.2 %copy-start.235 = (f32[1024]{0:T(1024)S(1)}, f32[1024]{0:T(1024)}, u32[]{:S(2)}) copy-start(f32[1024]{0:T(1024)} %param.52) | copy-start | bytes 12292
  991.8 181.7 %reduce-scatter.9.cloned.1.call-start = ((), (), s32[]{:S(2)}) async-start(), calls=%async_computation.9 | async-start | bytes 5242880 | tf_op jit(solution)/shard_map/reduce_scatter | solution.py:341
  1097.9 122.1 %reduce-scatter.7.cloned.1.call-start = ((), (), s32[]{:S(2)}) async-start(), calls=%async_computation.7 | async-start | bytes 2621440 | tf_op jit(solution)/shard_map/reduce_scatter | solution.py:318
  1104.3 115.8 %copy-start.222 = (f32[1024]{0:T(1024)S(1)}, f32[1024]{0:T(1024)}, u32[]{:S(2)}) copy-start(f32[1024]{0:T(1024)} %param.54) | copy-start | bytes 12292
  1104.3 165.8 %all-gather.11.cloned.1.call-start = ((), (), s32[]{:S(2)}) async-start(), calls=%async_computation.10 | async-start | bytes 2621440 | tf_op jit(solution)/shard_map/all_gather | solution.py:344
  1108.7 119.5 %copy-start.198 = (s32[128]{0:T(128)S(1)}, s32[128]{0:T(128)}, u32[]{:S(2)}) copy-start(s32[128]{0:T(128)} %copy-done.196) | copy-start | bytes 1540
  1108.7 120.2 %copy-start.195 = (s32[128]{0:T(128)S(1)}, s32[128]{0:T(128)}, u32[]{:S(2)}) copy-start(s32[128]{0:T(128)} %copy-done.193) | copy-start | bytes 1540
  1108.7 121.0 %copy-start.192 = (s32[128]{0:T(128)S(1)}, s32[128]{0:T(128)}, u32[]{:S(2)}) copy-start(s32[128]{0:T(128)} %copy-done.190) | copy-start | bytes 1540
  1108.7 121.7 %copy-start.189 = (s32[128]{0:T(128)S(1)}, s32[128]{0:T(128)}, u32[]{:S(2)}) copy-start(s32[128]{0:T(128)} %copy-done.187) | copy-start | bytes 1540
  1175.7 57.3 %copy-start.16 = (bf16[256,8,4,64]{3,1,2,0:T(8,128)(2,1)S(1)}, bf16[256,8,4,64]{3,1,2,0:T(8,128)(2,1)}, u32[]{:S(2)}) copy-start(bf16[256,8,4,64]{3,1,2,0:T(8,128)(2,1)} %copy-done.15) | copy-start | bytes 3145732
  1224.7 1382.2 %reduce-scatter.11.cloned.1.call-start = ((), (), s32[]{:S(2)}) async-start(), calls=%async_computation.11 | async-start | bytes 2621440 | tf_op jit(solution)/shard_map/reduce_scatter | solution.py:378
  1244.1 26.0 copy-start.71
  1248.4 26.4 copy-start.149
  1286.6 21.5 copy-start.56
  1380.6 1315.5 %all-reduce.49.cloned.1.call-start = ((), (), s32[]{:S(2)}) async-start(), calls=%async_computation.13 | async-start | bytes 12582912 | tf_op jit(solution)/shard_map/psum | solution.py:395
  1468.1 58.3 %copy-start.48 = (bf16[256,1,5,128]{3,2,0,1:T(8,128)(2,1)S(1)}, bf16[256,1,5,128]{3,2,0,1:T(8,128)(2,1)}, u32[]{:S(2)}) copy-start(bf16[256,1,5,128]{3,2,0,1:T(8,128)(2,1)} %copy.260) | copy-start | bytes 983044
  1468.1 58.3 %copy-start.83 = (f32[128,128]{1,0:T(8,128)S(1)}, f32[128,128]{1,0:T(8,128)}, u32[]{:S(2)}) copy-start(f32[128,128]{1,0:T(8,128)} %get-tuple-element.145) | copy-start | bytes 196612
  1533.7 17.8 copy-start.43
  1533.7 17.8 copy-start.82
  1726.1 23.0 copy-start.2
  1749.1 23.0 copy-start.73
  1795.1 23.5 copy-start.72
  1841.6 23.0 copy-start.5
  1841.6 122.6 %copy-start.91 = (s32[16384]{0:T(1024)S(1)}, s32[16384]{0:T(1024)}, u32[]{:S(2)}) copy-start(s32[16384]{0:T(1024)} %fusion.330) | copy-start | bytes 196612
  1964.2 88.5 %copy-start.90 = (s32[16384]{0:T(1024)S(1)}, s32[16384]{0:T(1024)}, u32[]{:S(2)}) copy-start(s32[16384]{0:T(1024)} %fusion.331) | copy-start | bytes 196612
  2052.7 88.7 %copy-start.89 = (s32[16384]{0:T(1024)S(1)}, s32[16384]{0:T(1024)}, u32[]{:S(2)}) copy-start(s32[16384]{0:T(1024)} %fusion.332) | copy-start | bytes 196612
  2141.4 88.5 %copy-start.87 = (s32[16384]{0:T(1024)S(1)}, s32[16384]{0:T(1024)}, u32[]{:S(2)}) copy-start(s32[16384]{0:T(1024)} %fusion.333) | copy-start | bytes 196612
  2230.0 88.5 %copy-start.86 = (s32[16384]{0:T(1024)S(1)}, s32[16384]{0:T(1024)}, u32[]{:S(2)}) copy-start(s32[16384]{0:T(1024)} %fusion.334) | copy-start | bytes 196612
  2318.5 88.5 %copy-start.85 = (s32[16384]{0:T(1024)S(1)}, s32[16384]{0:T(1024)}, u32[]{:S(2)}) copy-start(s32[16384]{0:T(1024)} %fusion.335) | copy-start | bytes 196612
  2407.0 88.5 %copy-start.84 = (s32[16384]{0:T(1024)S(1)}, s32[16384]{0:T(1024)}, u32[]{:S(2)}) copy-start(s32[16384]{0:T(1024)} %fusion.336) | copy-start | bytes 196612
  2495.6 88.6 %copy-start.4 = (f32[256,256]{0,1:T(8,128)S(1)}, f32[256,256]{0,1:T(8,128)}, u32[]{:S(2)}) copy-start(f32[256,256]{0,1:T(8,128)} %copy-done.3) | copy-start | bytes 786436
  2495.6 88.6 %copy-start.6 = (f32[256,256]{0,1:T(8,128)S(1)}, f32[256,256]{0,1:T(8,128)}, u32[]{:S(2)}) copy-start(f32[256,256]{0,1:T(8,128)} %copy-done.5) | copy-start | bytes 786436
  2495.6 89.5 %copy-start.27 = (bf16[1024,256]{1,0:T(8,128)(2,1)S(1)}, bf16[1024,256]{1,0:T(8,128)(2,1)}, u32[]{:S(2)}) copy-start(bf16[1024,256]{1,0:T(8,128)(2,1)} %copy-done.26) | copy-start | bytes 1572868
  2591.6 241.1 %all-reduce.47.cloned.1.call-start = ((), (), s32[]{:S(2)}) async-start(), calls=%async_computation.12 | async-start | bytes 228352 | tf_op jit(solution)/shard_map/psum | solution.py:418
  2701.7 144.9 %copy-start.1 = (bf16[1024,1024]{1,0:T(8,128)(2,1)S(1)}, bf16[1024,1024]{1,0:T(8,128)(2,1)}, u32[]{:S(2)}) copy-start(bf16[1024,1024]{1,0:T(8,128)(2,1)} %param.53) | copy-start | bytes 6291460
  (209 other events, 1477.2 us)
Sparse Core Ops, SparseCore 0:
  13.4 48.6 all-gather.4
  908.7 79.4 reduce-scatter.4
  991.3 46.4 all-gather.6
  1039.3 44.6 all-gather.8
  1098.0 75.4 reduce-scatter.8
  1175.6 44.3 reduce-scatter.6
  1224.8 45.2 all-gather.10
  1380.7 42.5 reduce-scatter.10
  2591.7 104.3 all-reduce.48
  2705.2 127.5 all-reduce.46
where the time goes:
time: 2870 us; the launch traced here: 2850 us
  local copies, waits for them, and re-layouts  1000 us (35%)
  other arithmetic  993 us (35%)
  waiting for transfers between devices  475 us (17%)
  matrix products  339 us (12%)
    scatter-add x16, other arithmetic, blocked_conv_back(): grad_taps.at[:, jnp.clip(offsets, 0, span - 1)]  907 us
    gather x24, local copies, waits for them, and re-layouts, toeplitz_block(): picked = jnp.take(taps_cm, jnp.clip(offsets, 0, span - 1), axis=1)  719 us
    mul x16, local copies, waits for them, and re-layouts, blocked_conv_back(): tap_part * valid.astype(jnp.float32)[None]  205 us
    psum x1, waiting for transfers between devices, body(): lax.psum((grad_norm1_gain, grad_norm1_bias, grad_out_bias, grad_norm2_gai...  126 us
    dot_general x16, matrix products, blocked_conv_back(): jnp.einsum('cgnt,cgns->cts', grad_pieces, shift_blocks(value_pieces, lag_...  99.7 us
    dot_general x16, matrix products, blocked_conv(): jnp.einsum('cgns,cts->cgnt', shift_blocks(pieces, lag_index, False), toep...  98.8 us
    reduce_scatter x1, waiting for transfers between devices, body(): lax.psum_scatter(partial_mix, 'tensor', scatter_dimension=1, tiled=True)  79.6 us
    dot_general x16, matrix products, blocked_conv_back(): jnp.einsum('cgnt,cts->cgns', shift_blocks(grad_pieces, lag_index, True),...  67.8 us
  transfers between devices with their start and end apart: 10, of which 8 were waited for; matrix products, arithmetic and copies ran while one was open for 72% of the time, Pallas kernels for 0%

commit v1 on v0

--- a/solution.py
+++ b/solution.py
@@ -1,5 +1,7 @@
 import jax
 import jax.numpy as jnp
+import ml_dtypes
+import numpy as np
 from jax import lax
 from jax.sharding import PartitionSpec as P
 
@@ -69,168 +71,144 @@
     return running
 
 
-def block_size(length):
-    return min(128, length // 4)
-
-
-def toeplitz_block(taps_cm, lag_index, block_len):
-    span = taps_cm.shape[1]
-    places = jnp.arange(block_len, dtype=jnp.int32)
-    offsets = lag_index * block_len + places[:, None] - places[None, :]
-    valid = (offsets >= 0).astype(taps_cm.dtype)
-    picked = jnp.take(taps_cm, jnp.clip(offsets, 0, span - 1), axis=1)
-    return (picked * valid[None], offsets, valid)
-
-
-def shift_blocks(pieces, lag_index, later):
-    if lag_index == 0:
-        return pieces
-    block_count = pieces.shape[2]
-    padding = jnp.zeros(pieces.shape[:2] + (lag_index,) + pieces.shape[3:], pieces.dtype)
-    if later:
-        return jnp.concatenate([pieces[:, :, lag_index:], padding], axis=2)
-    return jnp.concatenate([padding, pieces[:, :, : block_count - lag_index]], axis=2)
-
-
-def blocked_conv(pieces, taps_cm):
-    block_count = pieces.shape[2]
-    block_len = pieces.shape[3]
-    running = jnp.zeros(pieces.shape, jnp.float32)
-    for lag_index in range(block_count):
-        toeplitz, unused_offsets, unused_valid = toeplitz_block(taps_cm, lag_index, block_len)
-        running = running + jnp.einsum(
-            "cgns,cts->cgnt",
-            shift_blocks(pieces, lag_index, False),
-            toeplitz,
-            preferred_element_type=jnp.float32,
+def dft_rows(length):
+    span = 2 * length
+    places = np.arange(length)
+    turns = (np.arange(length)[:, None] * places[None, :]) % span
+    angles = turns * (2.0 * np.pi / span)
+    sines = -np.sin(angles)
+    sines[0] = 1.0 - 2.0 * (places % 2)
+    rows = np.concatenate([np.cos(angles), sines], axis=0).astype(np.float32)
+    high = rows.astype(ml_dtypes.bfloat16)
+    low = (rows - high.astype(np.float32)).astype(ml_dtypes.bfloat16)
+    return jnp.asarray(high), jnp.asarray(low)
+
+
+def to_spectrum(matrix, values_b):
+    high, low = matrix
+    return jnp.dot(high, values_b, preferred_element_type=jnp.float32) + jnp.dot(
+        low, values_b, preferred_element_type=jnp.float32
+    )
+
+
+def from_spectrum(matrix, spectrum):
+    high, low = matrix
+    top = spectrum.astype(jnp.bfloat16)
+    rest = (spectrum - top.astype(jnp.float32)).astype(jnp.bfloat16)
+
+    def back(rows, values):
+        return lax.dot_general(
+            rows, values, (((0,), (0,)), ((), ())), preferred_element_type=jnp.float32
         )
-    return running
-
-
-def blocked_conv_back(grad_pieces, value_pieces, taps_cm):
-    chan_count = value_pieces.shape[0]
-    block_count = value_pieces.shape[2]
-    block_len = value_pieces.shape[3]
-    span = taps_cm.shape[1]
-    grad_values = jnp.zeros(value_pieces.shape, jnp.float32)
-    grad_taps = jnp.zeros((chan_count, span), jnp.float32)
-    for lag_index in range(block_count):
-        toeplitz, offsets, valid = toeplitz_block(taps_cm, lag_index, block_len)
-        grad_values = grad_values + jnp.einsum(
-            "cgnt,cts->cgns",
-            shift_blocks(grad_pieces, lag_index, True),
-            toeplitz,
-            preferred_element_type=jnp.float32,
-        )
-        tap_part = jnp.einsum(
-            "cgnt,cgns->cts",
-            grad_pieces,
-            shift_blocks(value_pieces, lag_index, False),
-            preferred_element_type=jnp.float32,
-        )
-        grad_taps = grad_taps.at[:, jnp.clip(offsets, 0, span - 1)].add(
-            tap_part * valid.astype(jnp.float32)[None]
-        )
-    return (grad_values, grad_taps)
-
-
-def document_masks(segment):
-    return (segment[:, None, :] == jnp.arange(NDOC, dtype=jnp.int32)[None, :, None]).astype(
-        jnp.bfloat16
-    )
-
-
-def split_parts(segment_ids, shard_len):
-    length = segment_ids.shape[1]
-    main_doc = segment_ids[:, shard_len - 1]
-    main_mask = (segment_ids == main_doc[:, None]).astype(jnp.bfloat16)
-    others = (jnp.arange(NDOC, dtype=jnp.int32)[None, :] != main_doc[:, None]).astype(jnp.bfloat16)
-    head_masks = document_masks(segment_ids[:, :shard_len]) * others[:, :, None]
-    tail_masks = document_masks(segment_ids[:, length - shard_len :]) * others[:, :, None]
-    return (main_mask, head_masks, tail_masks)
-
-
-def to_blocks(values_cm, block_len):
-    chan_count, group_count, length = values_cm.shape
-    return values_cm.reshape(chan_count, group_count, length // block_len, block_len)
-
-
-def spread_docs(values_cm, masks_b):
-    chan_count, row_count, length = values_cm.shape
-    return (masks_b[None] * values_cm[:, :, None, :]).reshape(chan_count, row_count * NDOC, length)
-
-
-def join_regions(head, tail, length):
-    chan_count, row_count, region_len = head.shape
-    middle = jnp.zeros((chan_count, row_count, length - 2 * region_len), head.dtype)
-    return jnp.concatenate([head, middle, tail], axis=2)
-
-
-def region_conv(values_cm, masks_b, taps_cm):
-    chan_count, row_count, region_len = values_cm.shape
-    block_len = block_size(region_len)
-    result = blocked_conv(
-        to_blocks(spread_docs(values_cm, masks_b), block_len), taps_cm[:, :region_len]
-    )
-    result = result.reshape(chan_count, row_count, NDOC, region_len)
-    return jnp.sum(result * masks_b[None].astype(jnp.float32), axis=2)
-
-
-def region_conv_back(grad_cm, values_cm, masks_b, taps_cm):
-    chan_count, row_count, region_len = values_cm.shape
-    block_len = block_size(region_len)
-    grad_values, grad_taps = blocked_conv_back(
-        to_blocks(spread_docs(grad_cm, masks_b), block_len),
-        to_blocks(spread_docs(values_cm, masks_b), block_len),
-        taps_cm[:, :region_len],
-    )
-    grad_values = grad_values.reshape(chan_count, row_count, NDOC, region_len)
-    return (jnp.sum(grad_values * masks_b[None].astype(jnp.float32), axis=2), grad_taps)
-
-
-def causal_conv(values_b, segment_ids, taps_b, shard_len):
-    row_count, length, chan_count = values_b.shape
-    values_cm = jnp.transpose(values_b, (2, 0, 1))
-    taps_cm = jnp.transpose(taps_b)
-    main_mask, head_masks, tail_masks = split_parts(segment_ids, shard_len)
-    block_len = block_size(length)
-    main_in = values_cm * main_mask[None]
-    main_out = blocked_conv(to_blocks(main_in, block_len), taps_cm).reshape(
-        chan_count, row_count, length
-    )
-    main_out = main_out * main_mask[None].astype(jnp.float32)
-    head = region_conv(values_cm[:, :, :shard_len], head_masks, taps_cm)
-    tail = region_conv(values_cm[:, :, length - shard_len :], tail_masks, taps_cm)
-    return jnp.transpose(main_out + join_regions(head, tail, length), (1, 2, 0))
-
-
-def causal_conv_back(grad_b, values_b, segment_ids, taps_b, shard_len):
-    row_count, length, chan_count = values_b.shape
-    grad_cm = jnp.transpose(grad_b, (2, 0, 1))
-    values_cm = jnp.transpose(values_b, (2, 0, 1))
-    taps_cm = jnp.transpose(taps_b)
-    main_mask, head_masks, tail_masks = split_parts(segment_ids, shard_len)
-    block_len = block_size(length)
-    main_grad = grad_cm * main_mask[None]
-    main_in = values_cm * main_mask[None]
-    grad_main, grad_taps = blocked_conv_back(
-        to_blocks(main_grad, block_len), to_blocks(main_in, block_len), taps_cm
-    )
-    grad_main = grad_main.reshape(chan_count, row_count, length) * main_mask[None].astype(
-        jnp.float32
-    )
-    grad_head, taps_head = region_conv_back(
-        grad_cm[:, :, :shard_len], values_cm[:, :, :shard_len], head_masks, taps_cm
-    )
-    grad_tail, taps_tail = region_conv_back(
-        grad_cm[:, :, length - shard_len :],
-        values_cm[:, :, length - shard_len :],
-        tail_masks,
-        taps_cm,
-    )
-    grad_values = grad_main + join_regions(grad_head, grad_tail, length)
-    grad_taps = grad_taps.at[:, :shard_len].add(taps_head + taps_tail)
-    return (jnp.transpose(grad_values, (1, 2, 0)), jnp.transpose(grad_taps))
+
+    return back(high, top) + back(low, top) + back(high, rest)
+
+
+def spectral_scale(length):
+    weights = np.full((length, 1), 1.0 / length, np.float32)
+    weights[0] = 0.5 / length
+    return jnp.asarray(weights)
+
+
+def halves(spectrum):
+    length = spectrum.shape[0] // 2
+    return spectrum[:length], spectrum[length:]
+
+
+def spectral_product(left, right, conjugate):
+    left_re, left_im = halves(left)
+    right_re, right_im = halves(right)
+    first = lax.broadcasted_iota(jnp.int32, (left_re.shape[0],) + (1,) * (left.ndim - 1), 0) == 0
+    cross = left_im * right_im
+    if conjugate:
+        real = left_re * right_re + jnp.where(first, 0.0, cross)
+        imag = jnp.where(first, cross, left_re * right_im - left_im * right_re)
+    else:
+        real = left_re * right_re - jnp.where(first, 0.0, cross)
+        imag = jnp.where(first, cross, left_re * right_im + left_im * right_re)
+    return real, imag
+
+
+def scaled(parts, length):
+    scale = spectral_scale(length)
+    scale = scale.reshape((length,) + (1,) * (parts[0].ndim - 1))
+    return jnp.concatenate([parts[0] * scale, parts[1] * scale], axis=0)
+
+
+def document_masks(segment, main_doc):
+    docs = jnp.arange(NDOC, dtype=jnp.int32)
+    same = (segment[:, None] == docs[None, :]) & (docs[None, :] != main_doc)
+    return same.astype(jnp.bfloat16)
+
+
+def split_documents(values_b, masks):
+    main_mask, head_masks, tail_masks = masks
+    region = head_masks.shape[0]
+    length = values_b.shape[0]
+    main = values_b * main_mask[:, None]
+    small = (
+        head_masks[:, :, None] * values_b[:region, None, :]
+        + tail_masks[:, :, None] * values_b[length - region :, None, :]
+    )
+    return main, small.reshape(region, -1)
+
+
+def join_documents(main, small, masks):
+    main_mask, head_masks, tail_masks = masks
+    region = head_masks.shape[0]
+    length, channels = main.shape
+    small = small.reshape(region, NDOC, channels)
+    head = jnp.sum(small * head_masks[:, :, None].astype(jnp.float32), axis=1)
+    tail = jnp.sum(small * tail_masks[:, :, None].astype(jnp.float32), axis=1)
+    middle = jnp.zeros((length - 2 * region, channels), main.dtype)
+    return main * main_mask[:, None].astype(jnp.float32) + jnp.concatenate(
+        [head, middle, tail], axis=0
+    )
+
+
+def row_masks(segment, shard_len):
+    length = segment.shape[0]
+    main_doc = segment[shard_len - 1]
+    return (
+        (segment == main_doc).astype(jnp.bfloat16),
+        document_masks(segment[:shard_len], main_doc),
+        document_masks(segment[length - shard_len :], main_doc),
+    )
+
+
+def spectra_of(values_b, masks, matrices):
+    main, small = split_documents(values_b, masks)
+    region = masks[1].shape[0]
+    return (
+        to_spectrum(matrices[0], main),
+        to_spectrum(matrices[1], small).reshape(2 * region, NDOC, -1),
+    )
+
+
+def filter_row(spectra, taps_spectra, masks, matrices, conjugate):
+    length = spectra[0].shape[0] // 2
+    region = spectra[1].shape[0] // 2
+    main = from_spectrum(
+        matrices[0], scaled(spectral_product(taps_spectra[0], spectra[0], conjugate), length)
+    )
+    mixed = scaled(
+        spectral_product(taps_spectra[1][:, None, :], spectra[1], conjugate), region
+    )
+    small = from_spectrum(matrices[1], mixed.reshape(2 * region, -1))
+    return join_documents(main, small, masks)
+
+
+def taps_gradient(value_spectra, grad_spectra, matrices):
+    length = value_spectra[0].shape[0] // 2
+    region = value_spectra[1].shape[0] // 2
+    main = from_spectrum(
+        matrices[0], scaled(spectral_product(value_spectra[0], grad_spectra[0], True), length)
+    )
+    real, imag = spectral_product(value_spectra[1], grad_spectra[1], True)
+    small = from_spectrum(
+        matrices[1], scaled((jnp.sum(real, axis=1), jnp.sum(imag, axis=1)), region)
+    )
+    return main.at[:region].add(small)
 
 
 def body(
@@ -294,7 +272,14 @@
         local_filter, embed_weight, embed_bias, sine_freq, inner_weight, inner_bias, filter_weight
     )
     taps_b = filter_taps.astype(jnp.bfloat16)
-    convolved = causal_conv(product_b, segment_ids, taps_b, shard_len)
+    matrices = (dft_rows(length), dft_rows(shard_len))
+    masks = row_masks(segment_ids[0], shard_len)
+    taps_spectra = (
+        to_spectrum(matrices[0], taps_b),
+        to_spectrum(matrices[1], taps_b[:shard_len]),
+    )
+    value_spectra = spectra_of(product_b[0], masks, matrices)
+    convolved = filter_row(value_spectra, taps_spectra, masks, matrices, False)[None]
     summed = convolved + skip_gain * product
     gated_b = (summed * gate_out).astype(jnp.bfloat16)
     flat_gated = gated_b.reshape(flat_rows, channels)
@@ -353,9 +338,9 @@
     grad_summed = grad_gated * gate_out
     grad_gate_out = grad_gated * summed
     grad_skip_gain = jnp.sum(grad_summed * product, axis=(0, 1))
-    grad_conv, grad_taps = causal_conv_back(
-        grad_summed.astype(jnp.bfloat16), product_b, segment_ids, taps_b, shard_len
-    )
+    grad_spectra = spectra_of(grad_summed[0].astype(jnp.bfloat16), masks, matrices)
+    grad_conv = filter_row(grad_spectra, taps_spectra, masks, matrices, True)[None]
+    grad_taps = taps_gradient(value_spectra, grad_spectra, matrices)
     grad_product = grad_conv + grad_summed * skip_gain
     grad_mixed = jnp.stack([grad_gate_out, grad_product * values, grad_product * gate_in], axis=2)
     grad_projected, grad_short_weight, grad_short_bias = short_back(grad_mixed)

time: 2870 us -> 831 us (0.29)
  local copies, waits for them, and re-layouts: 1000 us -> 49.4 us
  other arithmetic: 993 us -> 62.4 us
  matrix products: 339 us -> 117 us
  waiting for transfers between devices: 475 us -> 537 us
    scatter-add x17 -> x0, other arithmetic: 908 us -> none  [the longest x16 907 us: blocked_conv_back(): grad_taps.at[:, jnp.clip(offsets, 0, span - 1)]]
    gather x24 -> x0, local copies, waits for them, and re-layouts: 719 us -> none  [toeplitz_block(): picked = jnp.take(taps_cm, jnp.clip(offsets, 0, span - 1), axis=1)]
    dot_general x48 -> x30, matrix products: 266 us -> 44.4 us  [the longest x18 25.6 us: back(): lax.dot_general(rows, values, (((0,), (0,)), ((), ())), preferred_element...]
    mul x20 -> x3, local copies, waits for them, and re-layouts: 209 us -> 4.04 us  [the longest x2 2.38 us: split_documents(): head_masks[:, :, None] * values_b[:region, None, :]]
    all_gather x1, waiting for transfers between devices: 0.01 us -> 28.9 us  [body(): lax.all_gather(normed1.astype(jnp.bfloat16), 'tensor', axis=1, tiled=True)]
  transfers between devices with their start and end apart: 10 -> 10, of which waited for: 8 -> 10; matrix products, arithmetic and copies ran while one was open for 72% -> 11% of each run, Pallas kernels for 0% -> 0%
where the time goes in v1:
time: 831 us; the launch traced here: 820 us
  waiting for transfers between devices  537 us (65%)
  matrix products  117 us (14%)
  other arithmetic  62.4 us (8%)
  local copies, waits for them, and re-layouts  49.4 us (6%)
  blocking collectives  26.3 us (3%)
  between operations  16.3 us (2%)
  starting transfers between devices  11.1 us (1%)
    psum x1, waiting for transfers between devices, body(): lax.psum((grad_norm1_gain, grad_norm1_bias, grad_out_bias, grad_norm2_gai...  127 us
    psum x1, waiting for transfers between devices, body(): lax.psum(grad_proj_weight.astype(jnp.bfloat16), 'dp').astype(jnp.float32)  72.7 us
    reduce_scatter x1, waiting for transfers between devices, body(): lax.psum_scatter(grad_second, 'tensor', scatter_dimension=1, tiled=True)  69 us
    reduce_scatter x1, waiting for transfers between devices, body(): lax.psum_scatter(partial_mix, 'tensor', scatter_dimension=1, tiled=True)  65 us
    all_gather x1, waiting for transfers between devices, body(): lax.all_gather(normed2.astype(jnp.bfloat16), 'tensor', axis=1, tiled=True)  46 us
    reduce_scatter x1, waiting for transfers between devices, body(): lax.psum_scatter(partial_mlp.astype(jnp.bfloat16), 'tensor', scatter_dime...  44.4 us
    unnamed x304, local copies, waits for them, and re-layouts  42.8 us
    all_gather x1, waiting for transfers between devices, body(): grad_rows = lax.all_gather(cotangent, 'tensor', axis=1, tiled=True)  39.6 us
  transfers between devices with their start and end apart: 10, of which 10 were waited for; matrix products, arithmetic and copies ran while one was open for 11% of the time, Pallas kernels for 0%

profile of v1, /device:TPU:0, one launch (start us, length us, event | category | flops | bytes accessed | tf_op | source)
XLA Modules:
  0.0 819.5 jit_solution(14950742324403853478)
XLA Ops:
  11.1 2.1 fusion.79
  17.6 2.7 copy.85
  24.7 2.0 fusion.68
  30.4 2.7 fusion.12
  33.1 28.9 %all-gather.5.cloned.1.call-done = bf16[1,1024,1024]{2,1,0:T(8,128)(2,1)} async-done(((bf16[1,256,1024]{2,1,0:T(8,128)(2,1)}), bf16[1,1024,1024]{2,1,0:T(8,128)(2,1)}) %all-gather.5.cloned.1.call-update) | async-done | bytes 2097168 | tf_op jit(solution)/shard_map/all_gather | solution.py:248
  62.0 3.9 fusion.39
  67.6 2.5 fusion.9
  70.4 1.4 copy-done.8
  72.5 1.7 copy.87
  74.2 1.7 copy.89
  75.8 1.8 multiply_add_fusion.2
  78.0 3.6 fusion.135
  84.7 1.5 copy-done.11
  95.5 3.7 multiply_convert_fusion.1
  99.9 2.8 convolution_bitcast_fusion.1
  102.7 10.6 %all-gather.7.cloned.1.call-start = ((), (), s32[]{:S(2)}) async-start(), calls=%async_computation.6 | async-start | bytes 2621440 | tf_op jit(solution)/shard_map/all_gather | solution.py:295
  113.3 65.0 %reduce-scatter.5.cloned.1.call-done = f32[1,256,1024]{2,1,0:T(8,128)} async-done(((f32[1,1024,1024]{2,1,0:T(8,128)}), f32[1,256,1024]{2,1,0:T(8,128)}) %reduce-scatter.5.cloned.1.call-update) | async-done | bytes 1048592 | tf_op jit(solution)/shard_map/reduce_scatter | solution.py:291
  178.3 1.6 fusion.202
  181.3 1.7 add_convert_fusion.1
  183.7 46.0 %all-gather.7.cloned.1.call-done = bf16[1,1024,1024]{2,1,0:T(8,128)(2,1)} async-done(((bf16[1,256,1024]{2,1,0:T(8,128)(2,1)}), bf16[1,1024,1024]{2,1,0:T(8,128)(2,1)}) %all-gather.7.cloned.1.call-update) | async-done | bytes 2097168 | tf_op jit(solution)/shard_map/all_gather | solution.py:295
  229.7 6.6 fusion.35
  236.3 39.6 %all-gather.9.cloned.1.call-done = bf16[1,1024,1024]{2,1,0:T(8,128)(2,1)} async-done(((bf16[1,256,1024]{2,1,0:T(8,128)(2,1)}), bf16[1,1024,1024]{2,1,0:T(8,128)(2,1)}) %all-gather.9.cloned.1.call-update) | async-done | bytes 2097168 | tf_op jit(solution)/shard_map/all_gather | solution.py:309
  275.9 8.1 fusion.207
  285.3 4.4 convolution_bitcast_fusion
  289.8 6.4 convert_bitcast_fusion.1
  296.3 69.0 %reduce-scatter.9.cloned.1.call-done = f32[1,256,1024]{2,1,0:T(8,128)} async-done(((f32[1,1024,1024]{2,1,0:T(8,128)}), f32[1,256,1024]{2,1,0:T(8,128)}) %reduce-scatter.9.cloned.1.call-update) | async-done | bytes 1048592 | tf_op jit(solution)/shard_map/reduce_scatter | solution.py:326
  365.3 2.2 multiply_reduce_fusion.6
  367.5 44.4 %reduce-scatter.7.cloned.1.call-done = bf16[1,256,1024]{2,1,0:T(8,128)(2,1)} async-done(((bf16[1,1024,1024]{2,1,0:T(8,128)(2,1)}), bf16[1,256,1024]{2,1,0:T(8,128)(2,1)}) %reduce-scatter.7.cloned.1.call-update) | async-done | bytes 524304 | tf_op jit(solution)/shard_map/reduce_scatter | solution.py:303
  411.9 2.6 fusion.201
  415.7 6.1 fusion.41
  421.8 39.2 %all-gather.11.cloned.1.call-done = bf16[1,1024,1024]{2,1,0:T(8,128)(2,1)} async-done(((bf16[1,256,1024]{2,1,0:T(8,128)(2,1)}), bf16[1,1024,1024]{2,1,0:T(8,128)(2,1)}) %all-gather.11.cloned.1.call-update) | async-done | bytes 2097168 | tf_op jit(solution)/shard_map/all_gather | solution.py:329
  461.0 2.5 fusion.25
  463.6 1.8 multiply_reduce_fusion.7
  465.4 1.5 copy-done.12
  466.9 2.6 fusion.107
  471.3 3.7 fusion.10
  475.0 2.2 add_multiply_fusion
  480.1 2.3 convolution_add_fusion.10
  484.3 1.4 copy-done.16
  485.6 4.5 multiply_subtract_fusion
  494.2 5.0 fusion.110
  499.2 3.1 multiply_reduce_fusion.1
  506.4 3.2 convert_bitcast_fusion
  510.2 7.4 fusion.44
  520.6 1.8 fusion.125
  522.8 1.8 convolution_add_fusion.8
  524.7 1.8 fusion.59
  526.9 1.5 fusion.69
  529.1 3.0 fusion.50
  533.7 2.3 multiply_reduce_fusion.15
  537.9 1.9 multiply_reduce_fusion.10
  544.7 3.0 convolution_convert_fusion
  548.3 4.0 reduce-scatter.11.cloned.1.call-done
  552.3 2.1 convert_reduce_fusion
  554.4 2.2 fusion.83
  556.7 2.2 convert_reduce_fusion.2
  558.9 26.3 %all-reduce.16 = (bf16[3,256]{1,0:T(4,128)(2,1)S(1)}, bf16[3,3,256]{2,1,0:T(4,128)(2,1)S(1)}, bf16[3,256]{1,0:T(4,128)(2,1)S(1)}, bf16[64,256]{1,0:T(8,128)(2,1)...) all-reduce(bf16[3,256]{1,0:T(4,128)(2,1)S(1)} %get-tuple-element.81, ...), channel_id=1, replica_groups=mesh['dp'=8,'tensor'=4] {'dp'}, use_global_device_ids=true, to_apply=%region_22.23 | all-reduce | flops 21504 | bytes 86016 | tf_op jit(solution)/shard_map/psum | solution.py:381
  588.8 72.7 %all-reduce.23.cloned.1.call-done = (bf16[1024,3,256]{2,0,1:T(8,128)(2,1)}, bf16[256,1024]{1,0:T(8,128)(2,1)}, bf16[1024,1024]{1,0:T(8,128)(2,1)}, bf16[1024,1024]{1,0:T(8,128)(2,1)}) async-done(((bf16[1024,3,256]{2,0,1:T(8,128)(2,1)}, bf16[256,1024]{1,0:T(8,128)(2,1)}, bf16[1024,1024]{1,0:T(8,128)(2,1)}, bf16[1024,1024]{1,0:T(8,128)(2,1)}), (bf16[1024,3,256]{2,0,1:T(8,128)(2,1)}, ...) | async-done | bytes 6291472 | tf_op jit(solution)/shard_map/psum | solution.py:380
  661.5 2.2 convert_element_type.307
  663.8 1.9 convert_element_type.289
  666.2 2.5 convert_element_type.309
  668.7 2.5 convert_element_type.313
  671.2 127.0 %all-reduce.21.cloned.1.call-done = (f32[1024]{0:T(1024)}, f32[1024]{0:T(1024)}, f32[33,64]{1,0:T(8,128)}, f32[64]{0:T(128)}, f32[3,64]{1,0:T(4,128)}, /*index=5...) async-done(((f32[1024]{0:T(1024)}, f32[1024]{0:T(1024)}, f32[33,64]{1,0:T(8,128)}, ...) | async-done | bytes 67344 | tf_op jit(solution)/shard_map/psum | solution.py:403
  804.5 1.5 copy.130
  (408 shorter events, 81.6 us)
Async XLA Ops:
  7.2 268.7 %copy-start = (bf16[1024,1024]{1,0:T(8,128)(2,1)S(1)}, bf16[1024,1024]{1,0:T(8,128)(2,1)}, u32[]{:S(2)}) copy-start(bf16[1024,1024]{1,0:T(8,128)(2,1)} %param.59) | copy-start | bytes 6291460
  7.2 7.2 copy-start.77
  7.2 9.3 %copy-start.135 = (f32[256]{0:T(256)S(1)}, f32[256]{0:T(256)}, u32[]{:S(2)}) copy-start(f32[256]{0:T(256)} %param.51) | copy-start | bytes 3076
  7.2 54.8 %all-gather.5.cloned.1.call-start = ((), (), s32[]{:S(2)}) async-start(), calls=%async_computation.4 | async-start | bytes 2621440 | tf_op jit(solution)/shard_map/all_gather | solution.py:248
  13.2 7.7 copy-start.133
  13.2 7.7 copy-start.134
  13.2 7.8 copy-start.117
  13.2 8.2 %copy-start.106 = (f32[33,64]{1,0:T(8,128)S(1)}, f32[33,64]{1,0:T(8,128)}, u32[]{:S(2)}) copy-start(f32[33,64]{1,0:T(8,128)} %param.45) | copy-start | bytes 25348
  13.2 8.2 %copy-start.138 = (f32[64]{0:T(128)S(1)}, f32[64]{0:T(128)}, u32[]{:S(2)}) copy-start(f32[64]{0:T(128)} %param.46) | copy-start | bytes 772
  13.2 8.8 %copy-start.73 = (f32[2,64,64]{2,1,0:T(8,128)S(1)}, f32[2,64,64]{2,1,0:T(8,128)}, u32[]{:S(2)}) copy-start(f32[2,64,64]{2,1,0:T(8,128)} %param.48) | copy-start | bytes 98308
  13.3 165.1 %reduce-scatter.5.cloned.1.call-start = ((), (), s32[]{:S(2)}) async-start(), calls=%async_computation.5 | async-start | bytes 5242880 | tf_op jit(solution)/shard_map/reduce_scatter | solution.py:291
  16.3 7.0 copy-start.98
  16.5 8.1 copy-start.136
  16.6 49.6 %copy-start.85 = (f32[1,1024]{1,0:T(1,128)}, f32[1,1024]{1,0:T(1,128)S(1)}, u32[]{:S(2)}) copy-start(f32[1,1024]{1,0:T(1,128)S(1)} %pad_convert_fusion) | copy-start | bytes 12292
  17.6 7.1 copy-start.141
  20.3 6.5 copy-start.20
  20.9 6.2 copy-start.107
  20.9 6.2 copy-start.126
  21.0 45.3 %copy-start.87 = (f32[1,1024]{1,0:T(1,128)}, f32[1,1024]{1,0:T(1,128)S(1)}, u32[]{:S(2)}) copy-start(f32[1,1024]{1,0:T(1,128)S(1)} %add_convert_fusion.2) | copy-start | bytes 12292
  21.0 45.2 %copy-start.89 = (f32[3,256]{1,0:T(4,128)}, f32[3,256]{1,0:T(4,128)S(1)}, u32[]{:S(2)}) copy-start(f32[3,256]{1,0:T(4,128)S(1)} %get-tuple-element.126) | copy-start | bytes 9220
  21.0 45.2 %copy-start.93 = (f32[3,256]{1,0:T(4,128)}, f32[3,256]{1,0:T(4,128)S(1)}, u32[]{:S(2)}) copy-start(f32[3,256]{1,0:T(4,128)S(1)} %get-tuple-element.128) | copy-start | bytes 9220
  21.0 45.2 %copy-start.95 = (f32[3,256]{1,0:T(4,128)}, f32[3,256]{1,0:T(4,128)S(1)}, u32[]{:S(2)}) copy-start(f32[3,256]{1,0:T(4,128)S(1)} %get-tuple-element.127) | copy-start | bytes 9220
  21.1 6.0 copy-start.27
  33.1 32.8 %copy-start.91 = (f32[3,256]{1,0:T(4,128)S(1)}, f32[3,256]{1,0:T(4,128)}, u32[]{:S(2)}) copy-start(f32[3,256]{1,0:T(4,128)} %param.42) | copy-start | bytes 9220
  102.7 127.0 %all-gather.7.cloned.1.call-start = ((), (), s32[]{:S(2)}) async-start(), calls=%async_computation.6 | async-start | bytes 2621440 | tf_op jit(solution)/shard_map/all_gather | solution.py:295
  183.1 92.8 %all-gather.9.cloned.1.call-start = ((), (), s32[]{:S(2)}) async-start(), calls=%async_computation.8 | async-start | bytes 2621440 | tf_op jit(solution)/shard_map/all_gather | solution.py:309
  183.7 181.7 %reduce-scatter.9.cloned.1.call-start = ((), (), s32[]{:S(2)}) async-start(), calls=%async_computation.9 | async-start | bytes 5242880 | tf_op jit(solution)/shard_map/reduce_scatter | solution.py:326
  275.9 9.4 %copy-start.139 = (bf16[1024,1024]{1,0:T(8,128)(2,1)S(1)}, bf16[1024,1024]{1,0:T(8,128)(2,1)}, u32[]{:S(2)}) copy-start(bf16[1024,1024]{1,0:T(8,128)(2,1)} %param.57) | copy-start | bytes 6291460
  289.7 122.2 %reduce-scatter.7.cloned.1.call-start = ((), (), s32[]{:S(2)}) async-start(), calls=%async_computation.7 | async-start | bytes 2621440 | tf_op jit(solution)/shard_map/reduce_scatter | solution.py:303
  296.2 69.1 %copy-start.97 = (f32[1024]{0:T(1024)S(1)}, f32[1024]{0:T(1024)}, u32[]{:S(2)}) copy-start(f32[1024]{0:T(1024)} %param.55) | copy-start | bytes 12292
  296.2 69.1 %copy-start.105 = (f32[256]{0:T(256)S(1)}, f32[256]{0:T(256)}, u32[]{:S(2)}) copy-start(f32[256]{0:T(256)} %copy-done.104) | copy-start | bytes 3076
  296.2 69.1 %copy-start.112 = (f32[256]{0:T(256)S(1)}, f32[256]{0:T(256)}, u32[]{:S(2)}) copy-start(f32[256]{0:T(256)} %copy-done.111) | copy-start | bytes 3076
  296.2 71.3 %copy-start.123 = (f32[256]{0:T(256)S(1)}, f32[256]{0:T(256)}, u32[]{:S(2)}) copy-start(f32[256]{0:T(256)} %copy-done.122) | copy-start | bytes 3076
  296.2 115.7 %copy-start.129 = (f32[1024]{0:T(1024)S(1)}, f32[1024]{0:T(1024)}, u32[]{:S(2)}) copy-start(f32[1024]{0:T(1024)} %param.60) | copy-start | bytes 12292
  296.3 164.8 %all-gather.11.cloned.1.call-start = ((), (), s32[]{:S(2)}) async-start(), calls=%async_computation.10 | async-start | bytes 2621440 | tf_op jit(solution)/shard_map/all_gather | solution.py:329
  367.5 46.9 %copy-start.42 = (bf16[1,256,1024]{2,1,0:T(8,128)(2,1)S(1)}, bf16[1,256,1024]{2,1,0:T(8,128)(2,1)}, u32[]{:S(2)}) copy-start(bf16[1,256,1024]{2,1,0:T(8,128)(2,1)} %param.61) | copy-start | bytes 1572868
  414.5 7.3 copy-start.30
  415.6 45.4 %copy-start.64 = (bf16[256,1024]{1,0:T(8,128)(2,1)S(1)}, bf16[256,1024]{1,0:T(8,128)(2,1)}, u32[]{:S(2)}) copy-start(bf16[256,1024]{1,0:T(8,128)(2,1)} %param.53) | copy-start | bytes 1572868
  415.6 136.7 %reduce-scatter.11.cloned.1.call-start = ((), (), s32[]{:S(2)}) async-start(), calls=%async_computation.11 | async-start | bytes 2621440 | tf_op jit(solution)/shard_map/reduce_scatter | solution.py:363
  421.8 41.7 %copy-start.51 = (f32[1024,256]{0,1:T(8,128)S(1)}, f32[1024,256]{0,1:T(8,128)}, u32[]{:S(2)}) copy-start(f32[1024,256]{0,1:T(8,128)} %get-tuple-element.147) | copy-start | bytes 3145732
  494.1 5.0 copy-start.7
  494.1 5.0 copy-start.32
  494.1 5.0 copy-start.86
  494.1 5.0 copy-start.88
  509.6 8.1 copy-start.37
  509.6 152.0 %all-reduce.23.cloned.1.call-start = ((), (), s32[]{:S(2)}) async-start(), calls=%async_computation.13 | async-start | bytes 12582912 | tf_op jit(solution)/shard_map/psum | solution.py:380
  510.2 7.4 copy-start.38
  510.2 7.4 copy-start.39
  532.2 11.5 %copy-start.72 = (f32[1024,16]{0,1:T(8,128)S(1)}, f32[1024,16]{0,1:T(8,128)}, u32[]{:S(2)}) copy-start(f32[1024,16]{0,1:T(8,128)} %copy-done.71) | copy-start | bytes 196612
  532.3 5.7 copy-start.45
  532.3 5.7 copy-start.116
  532.3 11.4 %copy-start.70 = (f32[1024,16]{0,1:T(8,128)S(1)}, f32[1024,16]{0,1:T(8,128)}, u32[]{:S(2)}) copy-start(f32[1024,16]{0,1:T(8,128)} %copy-done.69) | copy-start | bytes 196612
  532.3 11.4 %copy-start.99 = (f32[1024,1]{0,1:T(1,128)S(1)}, f32[1024,1]{0,1:T(1,128)}, u32[]{:S(2)}) copy-start(f32[1024,1]{0,1:T(1,128)} %copy-done.98) | copy-start | bytes 12292
  532.3 265.9 %all-reduce.21.cloned.1.call-start = ((), (), s32[]{:S(2)}) async-start(), calls=%async_computation.12 | async-start | bytes 228352 | tf_op jit(solution)/shard_map/psum | solution.py:403
  533.7 14.1 %copy-start.49 = (f32[1024,1,256]{0,2,1:T(8,128)S(1)}, f32[1024,1,256]{0,2,1:T(8,128)}, u32[]{:S(2)}) copy-start(f32[1024,1,256]{0,2,1:T(8,128)} %get-tuple-element.102) | copy-start | bytes 3145732
  533.7 14.1 %copy-start.50 = (f32[1024,1,256]{0,2,1:T(8,128)S(1)}, f32[1024,1,256]{0,2,1:T(8,128)}, u32[]{:S(2)}) copy-start(f32[1024,1,256]{0,2,1:T(8,128)} %get-tuple-element.103) | copy-start | bytes 3145732
  536.0 11.8 %copy-start.48 = (f32[1024,1,256]{0,2,1:T(8,128)S(1)}, f32[1024,1,256]{0,2,1:T(8,128)}, u32[]{:S(2)}) copy-start(f32[1024,1,256]{0,2,1:T(8,128)} %get-tuple-element.118) | copy-start | bytes 3145732
  537.3 10.4 %copy-start.18 = (f32[1024,3,256]{0,2,1:T(8,128)S(1)}, f32[1024,3,256]{0,2,1:T(8,128)}, u32[]{:S(2)}) copy-start(f32[1024,3,256]{0,2,1:T(8,128)} %copy-done.17) | copy-start | bytes 9437188
  537.4 10.4 %copy-start.92 = (f32[3,256]{1,0:T(4,128)S(1)}, f32[3,256]{1,0:T(4,128)}, u32[]{:S(2)}) copy-start(f32[3,256]{1,0:T(4,128)} %param.42) | copy-start | bytes 9220
  547.8 6.6 copy-start.121
  547.8 6.6 copy-start.114
  548.3 8.3 %copy-start.31 = (f32[1,256,1024]{2,1,0:T(8,128)S(1)}, f32[1,256,1024]{2,1,0:T(8,128)}, u32[]{:S(2)}) copy-start(f32[1,256,1024]{2,1,0:T(8,128)} %copy-done.30) | copy-start | bytes 3145732
  548.3 8.3 %copy-start.43 = (bf16[1,256,1024]{2,1,0:T(8,128)(2,1)S(1)}, bf16[1,256,1024]{2,1,0:T(8,128)(2,1)}, u32[]{:S(2)}) copy-start(bf16[1,256,1024]{2,1,0:T(8,128)(2,1)} %param.61) | copy-start | bytes 1572868
  668.7 143.6 %copy-start.1 = (bf16[1024,1024]{1,0:T(8,128)(2,1)S(1)}, bf16[1024,1024]{1,0:T(8,128)(2,1)}, u32[]{:S(2)}) copy-start(bf16[1024,1024]{1,0:T(8,128)(2,1)} %param.59) | copy-start | bytes 6291460
  (91 other events, 186.4 us)
Sparse Core Ops, SparseCore 0:
  13.4 48.6 all-gather.4
  102.8 75.4 reduce-scatter.4
  183.2 46.4 all-gather.6
  231.2 44.6 all-gather.8
  289.8 75.4 reduce-scatter.8
  367.5 44.3 reduce-scatter.6
  415.7 45.2 all-gather.10
  509.7 42.5 reduce-scatter.10
  556.5 104.9 all-reduce.22
  670.7 127.4 all-reduce.20

commit v2 on v1

v2 whole, which is shorter than its diff:
```python
import functools
import math

import jax
import jax.numpy as jnp
import ml_dtypes
import numpy as np
from jax import lax
from jax.experimental import pallas as pl
from jax.experimental.pallas import tpu as pltpu
from jax.sharding import PartitionSpec as P

FEAT = 33
SEQ = 1024
NDOC = 8


EPS = 1e-05
HIGH = lax.Precision.HIGHEST
SHIFT = 0.1
GELU_RATE = math.sqrt(2.0 / math.pi)
GELU_CUBE = 0.044715


def dot_nn(left, right):
    return jnp.dot(left, right, preferred_element_type=jnp.float32)


def dot_nt(left, right):
    return lax.dot_general(
        left, right, (((1,), (1,)), ((), ())), preferred_element_type=jnp.float32
    )


def dot_tn(left, right):
    return lax.dot_general(
        left, right, (((0,), (0,)), ((), ())), preferred_element_type=jnp.float32
    )


def transform(length):
    places = np.arange(length)
    angles = ((places[:, None] * places[None, :]) % (2 * length)) * (np.pi / length)
    return (
        jnp.asarray(np.cos(angles).astype(ml_dtypes.bfloat16)),
        jnp.asarray((-np.sin(angles)).astype(ml_dtypes.bfloat16)),
    )


def features_by_row():
    places = np.arange(SEQ, dtype=np.float32)
    bands = np.arange(1, (FEAT - 1) // 2 + 1, dtype=np.float32)
    angles = 2.0 * np.pi * np.arange(SEQ)[None, :] * bands[:, None].astype(np.float64) / SEQ
    rows = np.concatenate([(places / (SEQ - 1))[None, :], np.cos(angles), np.sin(angles)], axis=0)
    return jnp.asarray(rows.astype(np.float32))


def exact(left, right, contract):
    return lax.dot_general(
        left, right, (contract, ((), ())), precision=HIGH, preferred_element_type=jnp.float32
    )


def bin_scale(length):
    bins = lax.broadcasted_iota(jnp.int32, (length, 1), 0)
    return jnp.where(bins == 0, 0.5 / length, 1.0 / length)


def signs(length):
    places = lax.broadcasted_iota(jnp.int32, (length, 1), 0)
    return (1 - 2 * lax.rem(places, 2)).astype(jnp.float32)


def modulation(length, decay):
    places = lax.broadcasted_iota(jnp.int32, (length, 1), 0).astype(jnp.float32)
    return jnp.exp(-decay * (places / SEQ)) + SHIFT


def make_taps(
    features, embed, inner, columns, filter_weight, decay, transforms, pre, taps_bins
):
    cos_main, sin_main, cos_small, sin_small = transforms
    main_re, main_im, main_top, small_re, small_im, small_top = taps_bins
    length = features.shape[1]
    region = cos_small.shape[0]
    hidden = None
    for i in range(3):
        if i == 0:
            value = exact(embed[...], features[...], ((0,), (0,)))
        else:
            value = exact(inner[i - 1], hidden, ((0,), (0,)))
        value = value + columns[:, 3 + i : 4 + i]
        pre[i] = value
        hidden = jnp.sin(columns[:, i : i + 1] * value)
    taps = exact(hidden, filter_weight[...], ((0,), (0,)))
    taps = (taps * modulation(length, decay[...])).astype(jnp.bfloat16)
    scale = bin_scale(length)
    main_re[...] = dot_nn(cos_main[...], taps) * scale
    main_im[...] = dot_nn(sin_main[...], taps) * scale
    top = jnp.sum(taps.astype(jnp.float32) * signs(length), axis=0, keepdims=True)
    main_top[...] = top * (0.5 / length)
    short = taps[:region]
    scale = bin_scale(region)
    small_re[...] = dot_nn(cos_small[...], short) * scale
    small_im[...] = dot_nn(sin_small[...], short) * scale
    top = jnp.sum(short.astype(jnp.float32) * signs(region), axis=0, keepdims=True)
    small_top[...] = top * (0.5 / region)


def spectra(values, marks, cos_main, sin_main, cos_small, sin_small):
    length = values.shape[0]
    region = cos_small.shape[0]
    main = jnp.where(marks[:, 0:1] > 0, values, 0.0)
    top = jnp.sum(main * signs(length), axis=0, keepdims=True)
    main = main.astype(jnp.bfloat16)
    main_bins = (dot_nn(cos_main[...], main), dot_nn(sin_main[...], main), top)
    head, tail = values[:region], values[length - region :]
    head_slot, tail_slot = marks[:region, 3:4], marks[length - region :, 4:5]
    pieces = [
        jnp.where(head_slot == d, head, 0.0) + jnp.where(tail_slot == d, tail, 0.0)
        for d in range(NDOC)
    ]
    small = jnp.concatenate(pieces, axis=1)
    top = jnp.sum(small * signs(region), axis=0, keepdims=True)
    small = small.astype(jnp.bfloat16)
    small_bins = (dot_nn(cos_small[...], small), dot_nn(sin_small[...], small), top)
    return main_bins, small_bins


def times(left, right, conjugate):
    left_re, left_im, left_top = left
    right_re, right_im, right_top = right
    if conjugate:
        return (
            left_re * right_re + left_im * right_im,
            left_re * right_im - left_im * right_re,
            left_top * right_top,
        )
    return (
        left_re * right_re - left_im * right_im,
        left_re * right_im + left_im * right_re,
        left_top * right_top,
    )


def from_bins(bins, cos_rows, sin_rows):
    real, imag, top = bins
    return (
        dot_nn(cos_rows[...], real.astype(jnp.bfloat16))
        + dot_nn(sin_rows[...], imag.astype(jnp.bfloat16))
        + signs(real.shape[0]) * top
    )


def beside(part):
    return jnp.concatenate([part] * NDOC, axis=1)


def filtered(main_bins, small_bins, taps_main, taps_small, marks, transforms, conjugate):
    cos_main, sin_main, cos_small, sin_small = transforms
    main = from_bins(times(taps_main, main_bins, conjugate), cos_main, sin_main)
    taps_wide = tuple(beside(part) for part in taps_small)
    small = from_bins(times(taps_wide, small_bins, conjugate), cos_small, sin_small)
    length, channels = main.shape
    region = small.shape[0]
    main = jnp.where(marks[:, 0:1] > 0, main, 0.0)
    head, tail = main[:region], main[length - region :]
    head_slot, tail_slot = marks[:region, 3:4], marks[length - region :, 4:5]
    for d in range(NDOC):
        piece = small[:, d * channels : (d + 1) * channels]
        head = head + jnp.where(head_slot == d, piece, 0.0)
        tail = tail + jnp.where(tail_slot == d, piece, 0.0)
    return jnp.concatenate([head, main[region : length - region], tail], axis=0)


def filter_back_kernel(
    grad_taps,
    features,
    embed,
    inner,
    columns,
    filter_weight,
    decay,
    pre,
    embed_grad,
    inner_grad,
    filter_grad,
    column_grad,
):
    length = features.shape[1]
    raw = grad_taps[...] * modulation(length, decay[...])
    back = exact(filter_weight[...], raw, ((1,), (1,)))
    column_grad[...] = jnp.zeros_like(column_grad)
    for i in (2, 1, 0):
        rate = columns[:, i : i + 1]
        angle = rate * pre[i]
        if i == 2:
            filter_grad[...] = exact(jnp.sin(angle), raw, ((1,), (0,)))
        act = back * jnp.cos(angle)
        column_grad[:, i : i + 1] = jnp.sum(act * pre[i], axis=1, keepdims=True)
        step = act * rate
        column_grad[:, 3 + i : 4 + i] = jnp.sum(step, axis=1, keepdims=True)
        if i == 0:
            embed_grad[...] = exact(features[...], step, ((1,), (1,)))
        else:
            below = jnp.sin(columns[:, i - 1 : i] * pre[i - 1])
            inner_grad[i - 1] = exact(below, step, ((1,), (1,)))
            back = exact(inner[i - 1], step, ((1,), (0,)))


def shaped(shape, dtype=jnp.float32):
    return jax.ShapeDtypeStruct(shape, dtype)


def row_marks(segment, marks, region):
    ids = segment[...]
    length = ids.shape[0]
    places = lax.broadcasted_iota(jnp.int32, ids.shape, 0)
    inside = ids == ids[region - 1 : region]
    marks[:, 0:1] = inside.astype(jnp.int32)
    for lag in (1, 2):
        same = (ids == pltpu.roll(ids, lag, 0)) & (places >= lag)
        marks[:, lag : lag + 1] = same.astype(jnp.int32)
    marks[:, 3:4] = jnp.where(inside | (places >= region), -1, ids)
    marks[:, 4:5] = jnp.where(inside | (places < length - region), -1, ids)


BY_INDEX = pl.DeviceIdType.MESH


def greet(devices):
    barrier = pltpu.get_barrier_semaphore()
    for device in devices:
        pl.semaphore_signal(barrier, inc=1, device_id=device, device_id_type=BY_INDEX)
    pl.semaphore_wait(barrier, len(devices))


def remote(source, target, send_sem, recv_sem, device):
    return pltpu.make_async_remote_copy(
        src_ref=source,
        dst_ref=target,
        send_sem=send_sem,
        recv_sem=recv_sem,
        device_id=device,
        device_id_type=BY_INDEX,
    )


def tensor_peers():
    count = lax.axis_size("tensor")
    me = lax.axis_index("tensor")
    return [lax.rem(me + k, count) for k in range(1, count)]


def tensor_devices():
    return [{"tensor": peer} for peer in tensor_peers()]


def sibling():
    me = lax.axis_index("dp")
    return {"dp": me + 1 - 2 * lax.rem(me, 2)}


def chip_peers():
    chips = lax.axis_size("dp") // 2
    me = lax.axis_index("dp")
    core = lax.rem(me, 2)
    result = []
    for k in range(1, chips):
        chip = lax.rem(me // 2 + k, chips)
        result.append((chip, 2 * chip + core))
    return result


def chip_devices():
    return [{"dp": mate} for unused_chip, mate in chip_peers()]


def spread(source, target, sems, devices):
    copies = []
    for k, device in enumerate(devices):
        copies.append(
            remote(
                source(k) if callable(source) else source,
                target(k) if callable(target) else target,
                sems.at[0, k],
                sems.at[1, k],
                device,
            )
        )
        copies[-1].start()
    return copies


def wait_all(copies):
    for copy in copies:
        copy.wait()


def span(index, size):
    return pl.ds(pl.multiple_of(index * size, 16), size)


class Chain:
    def __init__(self, slots, send_sems, recv_sems):
        self.slots, self.send_sems, self.recv_sems = slots, send_sems, recv_sems
        self.count = lax.axis_size("tensor")
        self.me = lax.axis_index("tensor")

    def copy(self, block, side):
        step = 1 - 2 * side
        return remote(
            self.slots.at[block],
            self.slots.at[block],
            self.send_sems.at[side, block],
            self.recv_sems.at[block],
            {"tensor": lax.rem(self.me + step + self.count, self.count)},
        )

    def advance(self, step):
        lower, upper = self.me - step, self.me + step

        @pl.when(lower >= 0)
        def _():
            @pl.when(step > 0)
            def _():
                self.copy(lower, 0).wait_recv()

            @pl.when(self.me < self.count - 1)
            def _():
                self.copy(lower, 0).start()

        @pl.when(upper < self.count)
        def _():
            @pl.when(step > 0)
            def _():
                self.copy(upper, 1).wait_recv()

            @pl.when(self.me > 0)
            def _():
                self.copy(upper, 1).start()

    def finish(self):
        for block in range(self.count):

            @pl.when((self.me < self.count - 1) & (block <= self.me))
            def _():
                self.copy(block, 0).wait_send()

            @pl.when((self.me > 0) & (block >= self.me))
            def _():
                self.copy(block, 1).wait_send()


def normalised(values):
    average = jnp.mean(values, axis=-1, keepdims=True)
    centered = values - average
    variance = jnp.mean(centered * centered, axis=-1, keepdims=True)
    rate = lax.rsqrt(variance + EPS)
    return centered * rate, rate


def norm_back(grad, gain, hat, rate):
    e = grad * gain
    return rate * (
        e
        - jnp.mean(e, axis=-1, keepdims=True)
        - hat * jnp.mean(e * hat, axis=-1, keepdims=True)
    )


def column_sum(values):
    return jnp.sum(values, axis=0, keepdims=True)


def front_kernel(
    tokens,
    gain,
    shift,
    part,
    segment,
    features,
    embed,
    inner,
    columns,
    filter_weight,
    decay,
    proj,
    proj_bias,
    short,
    short_bias,
    skip,
    cos_main,
    sin_main,
    cos_small,
    sin_small,
    first_all,
    part_all,
    pre,
    main_re,
    main_im,
    main_top,
    small_re,
    small_im,
    small_top,
    gated_own,
    projected,
    mixed,
    summed,
    gated,
    marks,
    local_sems,
    first_send,
    first_recv,
    part_sems,
    chip_sems,
    core_sems,
    gated_sems,
):
    me = lax.axis_index("tensor")
    count = lax.axis_size("tensor")
    place = lax.axis_index("dp")
    core = lax.rem(place, 2)
    chip = place // 2
    peers = tensor_peers()
    shard = tokens.shape[0]
    channels = skip.shape[1]
    taps_bins = (main_re, main_im, main_top, small_re, small_im, small_top)
    transforms = (cos_main, sin_main, cos_small, sin_small)
    greet(tensor_devices() + [sibling()] + chip_devices())

    hat, unused_rate = normalised(tokens[...].astype(jnp.float32))
    first_all[me] = (hat * gain[...] + shift[...]).astype(jnp.bfloat16)
    chain = Chain(first_all, first_send, first_recv)
    chain.advance(0)
    own = pltpu.make_async_copy(part, part_all.at[me, chip, core], local_sems.at[0])
    own.start()
    parts = spread(part, part_all.at[me, chip, core], part_sems, tensor_devices())

    def project(block):
        rows = pl.ds(pl.multiple_of(block * shard, shard), shard)
        for k in range(3):
            lanes = slice(k * channels, (k + 1) * channels)
            projected[rows, lanes] = dot_nn(first_all[block], proj[k]) + proj_bias[:, lanes]

    project(me)
    make_taps(
        features, embed, inner, columns, filter_weight, decay, transforms, pre, taps_bins
    )
    row_marks(segment, marks, cos_small.shape[0])

    def turn(step, carry):
        chain.advance(step)

        def side(index, carry):
            block = me + step * (2 * index - 1)

            @pl.when((block >= 0) & (block < count))
            def _():
                project(block)

            return carry

        return lax.fori_loop(0, 2, side, carry)

    lax.fori_loop(1, 2, turn, 0)
    own.wait()
    wait_all(parts)
    held = part_all.at[:, chip, core]
    parts = spread(held, held, chip_sems, chip_devices())
    lax.fori_loop(2, count, turn, 0)
    wait_all(parts)
    held = part_all.at[:, :, core]
    parts = spread(held, held, core_sems, [sibling()])

    for k in range(3):
        lanes = slice(k * channels, (k + 1) * channels)
        value = projected[:, lanes]
        running = short_bias[:, lanes] + short[0:1, lanes] * value
        for lag in (1, 2):
            moved = jnp.where(marks[:, lag : lag + 1] > 0, pltpu.roll(value, lag, 0), 0.0)
            running = running + short[lag : lag + 1, lanes] * moved
        mixed[:, lanes] = running
    product = mixed[:, 2 * channels :] * mixed[:, channels : 2 * channels]
    low = product.astype(jnp.bfloat16).astype(jnp.float32)
    main_bins, small_bins = spectra(low, marks, *transforms)
    result = filtered(
        main_bins,
        small_bins,
        (main_re[...], main_im[...], main_top[...]),
        (small_re[...], small_im[...], small_top[...]),
        marks,
        transforms,
        False,
    )
    total = result + skip[...] * product
    summed[...] = total
    gated[...] = (total * mixed[:, :channels]).astype(jnp.bfloat16).reshape(gated.shape)
    swapped = spread(
        lambda k: gated.at[peers[k]], gated_own.at[me], gated_sems, tensor_devices()
    )
    gated_own[me] = gated[me]
    chain.finish()
    wait_all(parts + swapped)


def middle_kernel(
    gated,
    out,
    tokens,
    vectors,
    cotangent,
    up,
    bias,
    down,
    residual,
    grad_residual,
    mlp,
    up_grad,
    down_grad,
    bias_grad,
    grad_gated,
    out_grad,
    sums,
    second,
    active,
    low,
    parting,
    arriving,
    own_part,
    second_send,
    second_recv,
    part_send,
    part_recv,
):
    me = lax.axis_index("tensor")
    count = lax.axis_size("tensor")
    shard, width = tokens.shape
    units = up.shape[1]
    greet(tensor_devices())
    base = tokens[...].astype(jnp.float32) + vectors[0:1]
    for block in range(count):
        base = base + dot_nn(gated[block], out[block])
    residual[...] = base
    hat, unused_rate = normalised(base)
    second[me] = (hat * vectors[1:2] + vectors[2:3]).astype(jnp.bfloat16)
    chain = Chain(second, second_send, second_recv)
    bias_grad[...] = jnp.zeros_like(bias_grad)

    def sent(block):
        return remote(
            parting.at[block],
            arriving.at[me],
            part_send.at[block],
            part_recv.at[me],
            {"tensor": block},
        )

    def work(block):
        cut = units // 2
        mlp_part = None
        for lanes in (slice(0, cut), slice(cut, units)):
            hidden = dot_nn(second[block], up[:, lanes]) + bias[:, lanes]
            cube = GELU_CUBE * hidden * hidden
            slope = jnp.tanh(GELU_RATE * hidden * (1.0 + cube))
            gate = 0.5 * (1.0 + slope)
            active[block, :, lanes] = (hidden * gate).astype(jnp.bfloat16)
            rate = gate + (0.5 * GELU_RATE) * hidden * (1.0 - slope * slope) * (1.0 + 3.0 * cube)
            grad_hidden = dot_nt(cotangent[block], down[lanes]) * rate
            bias_grad[:, lanes] += column_sum(grad_hidden)
            low[block, :, lanes] = grad_hidden.astype(jnp.bfloat16)
        part = dot_nt(low[block], up[...])

        @pl.when(block == me)
        def _():
            own_part[...] = part

        @pl.when(block != me)
        def _():
            parting[block] = part.astype(jnp.bfloat16)
            sent(block).start()

        mlp[block] = dot_nn(active[block], down[...]).astype(jnp.bfloat16)

    def turn(step, carry):
        chain.advance(step)

        def side(index, carry):
            block = me + step * (2 * index - 1)

            @pl.when((block >= 0) & (block < count) & ((step > 0) | (index == 0)))
            def _():
                work(block)

            return carry

        return lax.fori_loop(0, 2, side, carry)

    lax.fori_loop(0, count, turn, 0)
    tokens_all = count * shard
    up_grad[...] = dot_tn(
        second[...].reshape(tokens_all, width), low[...].reshape(tokens_all, units)
    ).astype(jnp.bfloat16)
    down_grad[...] = dot_tn(
        active[...].reshape(tokens_all, units), cotangent[...].reshape(tokens_all, width)
    ).astype(jnp.bfloat16)
    for peer in tensor_peers():
        remote(
            parting.at[peer], arriving.at[peer], part_send.at[peer], part_recv.at[peer], {"tensor": peer}
        ).wait_recv()
        own_part[...] += arriving[peer].astype(jnp.float32)
    grad_normed = own_part[...]
    hat, rate = normalised(residual[...])
    grad_out = cotangent[me].astype(jnp.float32)
    grad = grad_out + norm_back(grad_normed, vectors[1:2], hat, rate)
    grad_residual[...] = grad
    sums[...] = jnp.zeros_like(sums)
    sums[0:1] = column_sum(grad_normed * hat)
    sums[1:2] = column_sum(grad_normed)
    sums[2:3] = column_sum(grad)
    sums[3:4] = column_sum(grad_out)
    grad_low = grad.astype(jnp.bfloat16)
    for block in range(count):
        grad_gated[block] = dot_nt(grad_low, out[block]).astype(jnp.bfloat16)
        out_grad[block] = dot_tn(gated[block], grad_low).astype(jnp.bfloat16)
    chain.finish()
    for peer in tensor_peers():
        sent(peer).wait_send()


class RowReduce:
    def __init__(self, source, part, refs):
        half, core_recv, chip_recv, load_sem, core_sems, chip_sems = refs[:6]
        self.source, self.part, self.half = source, part, half
        self.core_recv, self.chip_recv = core_recv, chip_recv
        self.load_sem, self.core_sems, self.chip_sems = load_sem, core_sems, chip_sems
        self.across = tuple(refs[6:])
        place = lax.axis_index("dp")
        self.core, self.chip = lax.rem(place, 2), place // 2
        self.chips = lax.axis_size("dp") // 2
        self.rows = half.shape[-2]
        self.size = self.rows // self.chips

    def pair(self):
        self.load = pltpu.make_async_copy(
            self.source.at[..., span(self.core, self.rows), :], self.half, self.load_sem.at[0]
        )
        self.load.start()
        self.copies = spread(
            self.source.at[..., span(1 - self.core, self.rows), :],
            self.core_recv,
            self.core_sems,
            [sibling()],
        )

    def plane(self):
        self.load.wait()
        wait_all(self.copies)
        self.half[...] = (
            self.half[...].astype(jnp.float32) + self.core_recv[...].astype(jnp.float32)
        ).astype(self.half.dtype)
        mates = chip_peers()
        self.copies = spread(
            lambda k: self.half.at[..., span(mates[k][0], self.size), :],
            lambda k: self.chip_recv.at[k],
            self.chip_sems,
            chip_devices(),
        )

    def gathered(self):
        value = self.half[..., span(self.chip, self.size), :].astype(jnp.float32)
        for k, copy in enumerate(self.copies):
            copy.wait()
            value = value + self.chip_recv[k].astype(jnp.float32)
        return value

    def cross(self):
        held, held_recv, sems = self.across
        held[...] = self.gathered().astype(held.dtype)
        peers = tensor_peers()
        self.copies = spread(
            lambda k: held.at[peers[k]], lambda k: held_recv.at[k], sems, tensor_devices()
        )

    def crossed(self):
        held, held_recv, sems = self.across
        value = held[lax.axis_index("tensor")].astype(jnp.float32)
        for k, copy in enumerate(self.copies):
            copy.wait()
            value = value + held_recv[k].astype(jnp.float32)
        return value

    def finish(self):
        value = self.crossed() if self.across else self.gathered()
        self.part[...] = value.astype(self.part.dtype)


def row_reduce_scratch(shape, chips):
    rows, columns = shape[-2:]
    lead = tuple(shape[:-2])
    size = rows // 2 // chips
    low = jnp.bfloat16
    scratch = [
        pltpu.VMEM(lead + (rows // 2, columns), low),
        pltpu.VMEM(lead + (rows // 2, columns), low),
        pltpu.VMEM((chips - 1,) + lead + (size, columns), low),
        pltpu.SemaphoreType.DMA((1,)),
        pltpu.SemaphoreType.DMA((2, 1)),
        pltpu.SemaphoreType.DMA((2, chips - 1)),
    ]
    if lead:
        scratch += [
            pltpu.VMEM(lead + (size, columns), low),
            pltpu.VMEM((lead[0] - 1, size, columns), low),
            pltpu.SemaphoreType.DMA((2, lead[0] - 1)),
        ]
    return scratch


class RowGather:
    def __init__(self, part, total, refs):
        self.part, self.total = part, total
        self.chip_sems, self.core_sems = refs
        place = lax.axis_index("dp")
        core, chip = lax.rem(place, 2), place // 2
        chips = lax.axis_size("dp") // 2
        self.mine = span(core * chips + chip, part.shape[0])
        self.half = span(core, part.shape[0] * chips)

    def plane(self):
        own = self.total.at[self.mine]
        own[...] = self.part[...]
        self.copies = spread(own, own, self.chip_sems, chip_devices())

    def pair(self):
        wait_all(self.copies)
        own = self.total.at[self.half]
        self.copies = spread(own, own, self.core_sems, [sibling()])

    def finish(self):
        wait_all(self.copies)


def row_gather_scratch(chips):
    return [pltpu.SemaphoreType.DMA((2, chips - 1)), pltpu.SemaphoreType.DMA((2, 1))]


def back_kernel(
    grad_blocks,
    mlp,
    up_grad,
    down_grad,
    out_grad,
    proj,
    short,
    skip,
    segment,
    features,
    embed,
    inner,
    columns,
    filter_weight,
    decay,
    pre,
    cos_main,
    sin_main,
    cos_small,
    sin_small,
    main_re,
    main_im,
    main_top,
    small_re,
    small_im,
    small_top,
    projected,
    mixed,
    summed,
    grad_first,
    grad_low,
    sums,
    skip_sum,
    mlp_sum,
    up_part,
    down_part,
    out_part,
    embed_grad,
    inner_grad,
    filter_grad,
    column_grad,
    grad_gated,
    grad_taps,
    marks,
    mlp_own,
    mlp_recv,
    local_sems,
    gated_sems,
    mlp_sems,
    *scratch,
):
    me = lax.axis_index("tensor")
    count = lax.axis_size("tensor")
    peers = tensor_peers()
    channels = skip.shape[1]
    length = projected.shape[0]
    region = cos_small.shape[0]
    shard = length // count
    transforms = (cos_main, sin_main, cos_small, sin_small)
    greet(tensor_devices() + [sibling()] + chip_devices())
    up_row = RowReduce(up_grad, up_part, scratch[:6])
    down_row = RowReduce(down_grad, down_part, scratch[6:12])
    out_row = RowReduce(out_grad, out_part, scratch[12:])
    weights = (out_row, up_row, down_row)

    own = pltpu.make_async_copy(grad_blocks.at[me], grad_gated.at[me], local_sems.at[0])
    own.start()
    arriving = spread(
        lambda k: grad_blocks.at[peers[k]], grad_gated.at[me], gated_sems, tensor_devices()
    )
    for weight in weights:
        weight.pair()
    own_mlp = pltpu.make_async_copy(mlp.at[me], mlp_own, local_sems.at[1])
    own_mlp.start()
    row_marks(segment, marks, region)
    gate_out = mixed[:, :channels]
    gate_in = mixed[:, channels : 2 * channels]
    values = mixed[:, 2 * channels :]
    product = values * gate_in
    low = product.astype(jnp.bfloat16).astype(jnp.float32)
    value_main, value_small = spectra(low, marks, *transforms)
    for weight in weights:
        weight.plane()
    own.wait()
    wait_all(arriving)
    mlps = spread(
        lambda k: mlp.at[peers[k]], lambda k: mlp_recv.at[k], mlp_sems, tensor_devices()
    )
    grad = grad_gated[...].reshape(length, channels).astype(jnp.float32)
    grad_summed = grad * gate_out
    skip_sum[...] = column_sum(grad_summed * product)
    low = grad_summed.astype(jnp.bfloat16).astype(jnp.float32)
    grad_main, grad_small = spectra(low, marks, *transforms)
    real, imag, top = times(value_main, grad_main, True)
    scale = bin_scale(length)
    taps = from_bins((real * scale, imag * scale, top * (0.5 / length)), cos_main, sin_main)
    scale = bin_scale(region)
    real, imag, top = (
        sum(part[:, d * channels : (d + 1) * channels] for d in range(NDOC))
        for part in times(value_small, grad_small, True)
    )
    taps_small = from_bins((real * scale, imag * scale, top * (0.5 / region)), cos_small, sin_small)
    grad_taps[:region] = taps[:region] + taps_small
    grad_taps[region:] = taps[region:]
    out_row.cross()
    result = filtered(
        grad_main,
        grad_small,
        (main_re[...], main_im[...], main_top[...]),
        (small_re[...], small_im[...], small_top[...]),
        marks,
        transforms,
        True,
    )
    grad_product = result + grad_summed * skip[...]
    parts = (grad * summed[...], grad_product * values, grad_product * gate_in)
    for k, part in enumerate(parts):
        lanes = slice(k * channels, (k + 1) * channels)
        source = projected[:, lanes]
        sums[3:4, lanes] = column_sum(part)
        sums[0:1, lanes] = column_sum(part * source)
        running = short[0:1, lanes] * part
        for lag in (1, 2):
            kept = jnp.where(marks[:, lag : lag + 1] > 0, part, 0.0)
            sums[lag : lag + 1, lanes] = column_sum(kept * pltpu.roll(source, lag, 0))
            running = running + short[lag : lag + 1, lanes] * pltpu.roll(kept, length - lag, 0)
        sums[4:5, lanes] = column_sum(running)
        grad_low[:, lanes] = running.astype(jnp.bfloat16)
    sums[5:8] = jnp.zeros_like(sums[5:8])
    for block in range(count):
        rows = slice(block * shard, (block + 1) * shard)
        total = dot_nt(grad_low[rows, :channels], proj[0])
        for k in (1, 2):
            total = total + dot_nt(grad_low[rows, k * channels : (k + 1) * channels], proj[k])
        grad_first[block] = total.astype(jnp.bfloat16)
    filter_back_kernel(
        grad_taps,
        features,
        embed,
        inner,
        columns,
        filter_weight,
        decay,
        pre,
        embed_grad,
        inner_grad,
        filter_grad,
        column_grad,
    )
    for weight in weights:
        weight.finish()
    own_mlp.wait()
    total = mlp_own[...].astype(jnp.float32)
    for k, copy in enumerate(mlps):
        copy.wait()
        total = total + mlp_recv[k].astype(jnp.float32)
    mlp_sum[...] = total


class SmallSum:
    def __init__(self, packed, result, refs):
        self.packed, self.result = packed, result
        (
            self.core_recv,
            self.chip_slots,
            self.group_slots,
            self.core_sems,
            self.chip_sems,
            self.group_sems,
        ) = refs
        self.me = lax.axis_index("tensor")
        self.chip = lax.axis_index("dp") // 2
        self.wide = self.group_slots.shape[1]

    def pair(self):
        self.copies = spread(self.packed, self.core_recv, self.core_sems, [sibling()])

    def plane(self):
        wait_all(self.copies)
        self.chip_slots[self.chip] = self.packed[...] + self.core_recv[...]
        own = self.chip_slots.at[self.chip]
        self.copies = spread(own, own, self.chip_sems, chip_devices())

    def tensor(self):
        wait_all(self.copies)
        total = self.chip_slots[0]
        for i in range(1, self.chip_slots.shape[0]):
            total = total + self.chip_slots[i]
        self.result[...] = total
        self.group_slots[self.me] = total[: self.wide]
        own = self.group_slots.at[self.me]
        self.copies = spread(own, own, self.group_sems, tensor_devices())

    def finish(self):
        wait_all(self.copies)
        total = self.group_slots[0]
        for i in range(1, self.group_slots.shape[0]):
            total = total + self.group_slots[i]
        self.result[: self.wide] = total


def small_sum_scratch(shape, wide, chips, groups):
    rows, columns = shape
    return [
        pltpu.VMEM((rows, columns), jnp.float32),
        pltpu.VMEM((chips, rows, columns), jnp.float32),
        pltpu.VMEM((groups, wide, columns), jnp.float32),
        pltpu.SemaphoreType.DMA((2, 1)),
        pltpu.SemaphoreType.DMA((2, chips - 1)),
        pltpu.SemaphoreType.DMA((2, groups - 1)),
    ]


def final_kernel(
    grad_first,
    first,
    grad_low,
    tokens,
    gain,
    grad_residual,
    packed,
    up_part,
    down_part,
    out_part,
    grad_tokens,
    proj_sum,
    norm_sums,
    packed_sum,
    up_sum,
    down_sum,
    out_sum,
    proj_grad,
    proj_part,
    norm_own,
    block_recv,
    block_sems,
    *scratch,
):
    me = lax.axis_index("tensor")
    peers = tensor_peers()
    greet(tensor_devices() + [sibling()] + chip_devices())
    blocks = spread(
        lambda k: grad_first.at[peers[k]], lambda k: block_recv.at[k], block_sems, tensor_devices()
    )
    row = RowReduce(proj_grad, proj_part, scratch[:6])
    proj_all = RowGather(proj_part, proj_sum, scratch[6:8])
    gathers = [
        RowGather(up_part, up_sum, scratch[8:10]),
        RowGather(down_part, down_sum, scratch[10:12]),
        RowGather(out_part, out_sum, scratch[12:14]),
    ]
    small = SmallSum(packed, packed_sum, scratch[14:20])
    norms = SmallSum(norm_own, norm_sums, scratch[20:26])
    small.pair()
    length = grad_low.shape[0]
    proj_grad[...] = dot_tn(first[...].reshape(length, first.shape[2]), grad_low[...]).astype(
        jnp.bfloat16
    )
    row.pair()
    small.plane()
    row.plane()
    for gather in gathers:
        gather.plane()
    hat, rate = normalised(tokens[...].astype(jnp.float32))
    small.tensor()
    row.finish()
    proj_all.plane()
    small.finish()
    for gather in gathers:
        gather.pair()
    proj_all.pair()
    grad = grad_first[me].astype(jnp.float32)
    for k, copy in enumerate(blocks):
        copy.wait()
        grad = grad + block_recv[k].astype(jnp.float32)
    norm_own[...] = jnp.zeros_like(norm_own)
    norm_own[0:1] = column_sum(grad * hat)
    norm_own[1:2] = column_sum(grad)
    norms.pair()
    grad_tokens[...] = grad_residual[...] + norm_back(grad, gain[...], hat, rate)
    norms.plane()
    norms.tensor()
    norms.finish()
    for gather in gathers + [proj_all]:
        gather.finish()


def communicate(kernel, shapes, operands, anywhere, scratch, channel, name):
    vmem = pl.BlockSpec(memory_space=pltpu.VMEM)
    free = pl.BlockSpec(memory_space=pl.ANY)
    return pl.pallas_call(
        kernel,
        out_shape=shapes,
        in_specs=[free if i in anywhere[0] else vmem for i in range(len(operands))],
        out_specs=[free if i in anywhere[1] else vmem for i in range(len(shapes))],
        scratch_shapes=scratch,
        compiler_params=pltpu.CompilerParams(
            collective_id=channel, has_side_effects=True, vmem_limit_bytes=60 * 1024 * 1024
        ),
        cost_estimate=pl.CostEstimate(flops=0, bytes_accessed=200_000_000, transcendentals=0),
        name=name,
    )(*operands)


def body(
    tokens,
    segment_ids,
    norm1_gain,
    norm1_bias,
    proj_weight,
    proj_bias,
    short_weight,
    short_bias,
    embed_weight,
    embed_bias,
    sine_freq,
    inner_weight,
    inner_bias,
    filter_weight,
    decay_rate,
    skip_gain,
    out_weight,
    out_bias,
    norm2_gain,
    norm2_bias,
    up_weight,
    up_bias,
    down_weight,
    down_bias,
    cotangent,
):
    row_count, shard_len, model_width = tokens.shape
    groups = lax.axis_size("tensor")
    rows = lax.axis_size("dp")
    place = lax.axis_index("tensor")
    row_place = lax.axis_index("dp")
    length = shard_len * groups
    channels = proj_weight.shape[2]
    units = up_weight.shape[1]
    channel_slice = channels // rows

    out_part = lax.dynamic_slice_in_dim(out_weight, row_place * channel_slice, channel_slice, 0)
    out_rows = -(-channel_slice // 16) * 16
    out_part = jnp.pad(out_part, ((0, out_rows - channel_slice), (0, 0)))

    low = jnp.bfloat16
    region = shard_len
    chips = rows // 2
    proj_columns = 3 * channels
    transforms = transform(length) + transform(region)
    features = features_by_row()
    columns = jnp.stack(
        [*sine_freq, embed_bias, *inner_bias] + [jnp.zeros_like(embed_bias)] * 2, axis=1
    )
    decay = decay_rate[None]
    width = embed_weight.shape[1]
    segment = segment_ids.reshape(length, 1)
    proj = proj_weight.transpose(1, 0, 2)
    cotangent = cotangent[0]
    all_cotangent = lax.all_gather(cotangent, "tensor")
    short_flat = short_weight.reshape(3, proj_columns)
    skip = skip_gain[None]
    filter_parts = [features, embed_weight, inner_weight, columns, filter_weight, decay]
    semaphores = pltpu.SemaphoreType.DMA
    blocked = (groups, shard_len, model_width)
    (
        first_all,
        out_all,
        pre,
        main_re,
        main_im,
        main_top,
        small_re,
        small_im,
        small_top,
        gated_own,
        projected,
        mixed,
        summed,
    ) = communicate(
        front_kernel,
        [
            shaped(blocked, low),
            shaped((groups, chips, 2) + out_part.shape, low),
            shaped((3, width, length)),
            shaped((length, channels)),
            shaped((length, channels)),
            shaped((1, channels)),
            shaped((region, channels)),
            shaped((region, channels)),
            shaped((1, channels)),
            shaped((groups, shard_len, channels), low),
            shaped((length, proj_columns)),
            shaped((length, proj_columns)),
            shaped((length, channels)),
        ],
        [
            tokens[0],
            norm1_gain[None],
            norm1_bias[None],
            out_part,
            segment,
            *filter_parts,
            proj,
            proj_bias.reshape(1, proj_columns),
            short_flat,
            short_bias.reshape(1, proj_columns),
            skip,
            *transforms,
        ],
        ((3,), (1,)),
        [
            pltpu.VMEM((groups, shard_len, channels), low),
            pltpu.VMEM((length, 8), jnp.int32),
            semaphores((1,)),
            semaphores((2, groups)),
            semaphores((groups,)),
            semaphores((2, groups - 1)),
            semaphores((2, chips - 1)),
            semaphores((2, 1)),
            semaphores((2, groups - 1)),
        ],
        0,
        "front",
    )
    taps_bins = (main_re, main_im, main_top, small_re, small_im, small_top)
    out_all = out_all[..., :channel_slice, :].reshape(groups, channels, model_width)
    vectors = jnp.stack([out_bias, norm2_gain, norm2_bias])
    (
        residual,
        grad_residual,
        mlp_partial,
        up_grad,
        down_grad,
        grad_up_bias,
        grad_gated,
        out_grad,
        middle_sums,
    ) = communicate(
        middle_kernel,
        [
            shaped((shard_len, model_width)),
            shaped((shard_len, model_width)),
            shaped(blocked, low),
            shaped((model_width, units), low),
            shaped((units, model_width), low),
            shaped((1, units)),
            shaped((groups, shard_len, channels), low),
            shaped((groups, channels, model_width), low),
            shaped((8, model_width)),
        ],
        [
            gated_own,
            out_all,
            tokens[0],
            vectors,
            all_cotangent,
            up_weight,
            up_bias[None],
            down_weight,
        ],
        ((), ()),
        [
            pltpu.VMEM(blocked, low),
            pltpu.VMEM((groups, shard_len, units), low),
            pltpu.VMEM((groups, shard_len, units), low),
            pltpu.VMEM(blocked, low),
            pltpu.VMEM(blocked, low),
            pltpu.VMEM((shard_len, model_width), jnp.float32),
            semaphores((2, groups)),
            semaphores((groups,)),
            semaphores((groups,)),
            semaphores((groups,)),
        ],
        1,
        "middle",
    )
    fold = max(1, 32 * chips // channels)
    out_grad = out_grad.reshape(groups, channels * fold, model_width // fold)
    (
        grad_first,
        grad_low,
        back_sums,
        skip_sum,
        mlp_out,
        up_part,
        down_part,
        out_part,
        embed_grad,
        grad_inner_weight,
        grad_filter_weight,
        column_grad,
    ) = communicate(
        back_kernel,
        [
            shaped(blocked, low),
            shaped((length, proj_columns), low),
            shaped((8, proj_columns)),
            shaped((1, channels)),
            shaped((shard_len, model_width)),
            shaped((model_width // rows, units), low),
            shaped((units // rows, model_width), low),
            shaped((channels * fold // rows, model_width // fold), low),
            shaped(embed_weight.shape),
            shaped(inner_weight.shape),
            shaped(filter_weight.shape),
            shaped(columns.shape),
        ],
        [
            grad_gated,
            mlp_partial,
            up_grad,
            down_grad,
            out_grad,
            proj,
            short_flat,
            skip,
            segment,
            *filter_parts,
            pre,
            *transforms,
            *taps_bins,
            projected,
            mixed,
            summed,
        ],
        ((0, 1, 2, 3, 4), ()),
        [
            pltpu.VMEM((groups, shard_len, channels), low),
            pltpu.VMEM((length, channels), jnp.float32),
            pltpu.VMEM((length, 8), jnp.int32),
            pltpu.VMEM((shard_len, model_width), low),
            pltpu.VMEM((groups - 1, shard_len, model_width), low),
            semaphores((2,)),
            semaphores((2, groups - 1)),
            semaphores((2, groups - 1)),
        ]
        + row_reduce_scratch(up_grad.shape, chips)
        + row_reduce_scratch(down_grad.shape, chips)
        + row_reduce_scratch(out_grad.shape, chips),
        2,
        "back",
    )
    grad_norm2_gain, grad_norm2_bias, grad_out_bias, grad_down_bias = middle_sums[:4]
    grad_skip_gain = skip_sum[0]
    grad_up_bias = grad_up_bias[0]
    grad_short_weight = back_sums[:3].reshape(short_weight.shape)
    grad_short_bias = back_sums[3].reshape(short_bias.shape)
    grad_proj_bias = back_sums[4].reshape(proj_bias.shape)
    grad_embed_weight = embed_grad
    grad_sine_freq = column_grad[:, :3].T
    grad_embed_bias = column_grad[:, 3]
    grad_inner_bias = column_grad[:, 4:6].T

    everywhere = (
        grad_out_bias,
        grad_norm2_gain,
        grad_norm2_bias,
        grad_down_bias,
        grad_embed_weight,
        grad_embed_bias,
        grad_sine_freq,
        grad_inner_weight,
        grad_inner_bias,
    )
    rows_only = (
        grad_proj_bias,
        grad_short_weight,
        grad_short_bias,
        grad_filter_weight,
        grad_skip_gain,
        grad_up_bias,
    )

    def pack(parts):
        flat = jnp.concatenate([part.reshape(-1) for part in parts])
        return jnp.pad(flat, (0, -flat.size % 1024)).reshape(-1, 128)

    def unpack(packed, parts):
        flat = packed.reshape(-1)
        results = []
        start = 0
        for part in parts:
            results.append(flat[start : start + part.size].reshape(part.shape))
            start += part.size
        return results

    wide = pack(everywhere)
    packed = jnp.concatenate([wide, pack(rows_only)], axis=0)
    part_rows = proj.shape[1] // rows
    grad_tokens, proj_grad, final_sums, packed, up_grad, down_grad, out_grad = communicate(
        final_kernel,
        [
            shaped((shard_len, model_width)),
            shaped((model_width, proj_columns), low),
            shaped((8, model_width)),
            shaped(packed.shape),
            shaped(up_grad.shape, low),
            shaped(down_grad.shape, low),
            shaped(out_grad.shape[1:], low),
        ],
        [
            grad_first,
            first_all,
            grad_low,
            tokens[0],
            norm1_gain[None],
            grad_residual,
            packed,
            up_part,
            down_part,
            out_part,
        ],
        ((), ()),
        [
            pltpu.VMEM((model_width, proj_columns), low),
            pltpu.VMEM((part_rows, proj_columns), low),
            pltpu.VMEM((8, model_width), jnp.float32),
            pltpu.VMEM((groups - 1, shard_len, model_width), low),
            semaphores((2, groups - 1)),
        ]
        + row_reduce_scratch((model_width, proj_columns), chips)
        + row_gather_scratch(chips) * 4
        + small_sum_scratch(packed.shape, wide.shape[0], chips, groups)
        + small_sum_scratch((8, model_width), 8, chips, groups),
        3,
        "final",
    )
    grad_tokens = grad_tokens[None]
    grad_proj_weight = proj_grad.astype(jnp.float32).reshape(model_width, 3, channels)
    grad_out_weight = out_grad.reshape(out_weight.shape).astype(jnp.float32)
    grad_up_weight = up_grad.astype(jnp.float32)
    grad_down_weight = down_grad.astype(jnp.float32)
    layer_out = (residual + mlp_out + down_bias).astype(low)[None]
    grad_norm1_gain, grad_norm1_bias = final_sums[:2]
    wide, narrow = packed[: wide.shape[0]], packed[wide.shape[0] :]
    (
        grad_out_bias,
        grad_norm2_gain,
        grad_norm2_bias,
        grad_down_bias,
        grad_embed_weight,
        grad_embed_bias,
        grad_sine_freq,
        grad_inner_weight,
        grad_inner_bias,
    ) = unpack(wide, everywhere)
    (
        grad_proj_bias,
        grad_short_weight,
        grad_short_bias,
        grad_filter_weight,
        grad_skip_gain,
        grad_up_bias,
    ) = unpack(narrow, rows_only)
    return (
        layer_out,
        grad_tokens,
        grad_norm1_gain,
        grad_norm1_bias,
        grad_proj_weight,
        grad_proj_bias,
        grad_short_weight,
        grad_short_bias,
        grad_embed_weight,
        grad_embed_bias,
        grad_sine_freq,
        grad_inner_weight,
        grad_inner_bias,
        grad_filter_weight,
        grad_skip_gain,
        grad_out_weight,
        grad_out_bias,
        grad_norm2_gain,
        grad_norm2_bias,
        grad_up_weight,
        grad_up_bias,
        grad_down_weight,
        grad_down_bias,
    )


def solution(mesh):
    return jax.shard_map(
        body,
        mesh=mesh,
        in_specs=(
            P("dp", "tensor", None),
            P("dp", None),
            P(),
            P(),
            P(None, None, "tensor"),
            P(None, "tensor"),
            P(None, None, "tensor"),
            P(None, "tensor"),
            P(),
            P(),
            P(),
            P(),
            P(),
            P(None, "tensor"),
            P("tensor"),
            P("tensor"),
            P("tensor", None),
            P(),
            P(),
            P(),
            P(None, "tensor"),
            P("tensor"),
            P("tensor", None),
            P(),
            P("dp", "tensor", None),
        ),
        out_specs=(
            P("dp", "tensor", None),
            P("dp", "tensor", None),
            P(),
            P(),
            P(None, None, "tensor"),
            P(None, "tensor"),
            P(None, None, "tensor"),
            P(None, "tensor"),
            P(),
            P(),
            P(),
            P(),
            P(),
            P(None, "tensor"),
            P("tensor"),
            P("tensor", None),
            P(),
            P(),
            P(),
            P(None, "tensor"),
            P("tensor"),
            P("tensor", None),
            P(),
        ),
        check_vma=False,
    )
```

time: 831 us -> 412 us (0.50)
  waiting for transfers between devices: 537 us -> 0.68 us
  Pallas kernels: 0 us -> 345 us
  matrix products: 117 us -> 0 us
  other arithmetic: 62.4 us -> 10.1 us
  blocking collectives: 26.3 us -> 0 us
  local copies, waits for them, and re-layouts: 49.4 us -> 35.4 us
  starting transfers between devices: 11.1 us -> 0.04 us
    pallas_call x0 -> x4, Pallas kernels: none -> 345 us  [communicate(): pl.pallas_call(kernel, out_shape=shapes, in_specs=[free if i in anywhere[...]
    psum x2 -> x0, waiting for transfers between devices: 200 us -> none  [the longest x1 127 us: body(): lax.psum((grad_norm1_gain, grad_norm1_bias, grad_out_bias, grad_norm2_gai...]
    reduce_scatter x4 -> x0, waiting for transfers between devices: 182 us -> none  [the longest x1 69 us: body(): lax.psum_scatter(grad_second, 'tensor', scatter_dimension=1, tiled=True)]
    all_gather x4 -> x1, waiting for transfers between devices: 154 us -> 0.01 us  [body(): all_cotangent = lax.all_gather(cotangent, 'tensor')]
    dot_general x53 -> x0, matrix products: 117 us -> none  [the longest x18 25.6 us: back(): lax.dot_general(rows, values, (((0,), (0,)), ((), ())), preferred_element...]
    unnamed x304 -> x35, local copies, waits for them, and re-layouts: 42.8 us -> 10.1 us
    psum x1 -> x0, blocking collectives: 26.3 us -> none  [body(): lax.psum(grad_proj_bias.astype(jnp.bfloat16), 'dp').astype(jnp.float32)]
    reduce_sum x16 -> x0, other arithmetic: 23 us -> none  [the longest x3 6.49 us: layer_norm(): return centered * lax.rsqrt(variance + EPS) * norm_gain + norm_bias]
  transfers between devices with their start and end apart: 10 -> 1, of which waited for: 10 -> 0; matrix products, arithmetic and copies ran while one was open for 11% -> 2% of each run, Pallas kernels for 0% -> 26%
where the time goes in v2:
time: 412 us; the launch traced here: 405 us
  Pallas kernels  345 us (84%)
  local copies, waits for them, and re-layouts  35.4 us (9%)
  between operations  14.7 us (4%)
  other arithmetic  10.1 us (2%)
    pallas_call x4, Pallas kernels, communicate(): pl.pallas_call(kernel, out_shape=shapes, in_specs=[free if i in anywhere[...  345 us
    unnamed x35, local copies, waits for them, and re-layouts  10.1 us
  transfers between devices with their start and end apart: 1, of which 0 were waited for; matrix products, arithmetic and copies ran while one was open for 2% of the time, Pallas kernels for 26%

profile of v2, /device:TPU:0, one launch (start us, length us, event | category | flops | bytes accessed | tf_op | source)
XLA Modules:
  0.0 405.4 jit_solution(8865303445958180179)
XLA Ops:
  7.2 0.0 copy-start
  7.2 0.0 all-gather.2.cloned.1.call-start
  7.3 0.7 all-gather.2.cloned.1.call-update
  8.0 0.8 slice_bitcast_fusion.8
  8.8 0.7 stack.23
  9.4 0.7 copy.74.columns
  10.1 1.7 copy.73.segment
  11.8 1.3 copy.82
  13.1 1.3 copy.81
  14.4 1.3 copy.83
  15.7 0.0 copy-done
  15.7 0.6 constant_dynamic-slice_fusion.part
  16.3 105.1 %front.1 = (bf16[4,256,1024]{2,1,0:T(8,128)(2,1)}, bf16[4,4,2,32,1024]{4,3,2,1,0:T(8,128)(2,1)}, f32[3,64,1024]{2,1,0:T(8,128)}, f32[1024,256]{1,0:T(8,128)}, f3...) custom-call(bf16[256,1024]{1,0:T(8,128)(2,1)} %bitcast.69, ...), custom_call_target="tpu_custom_call" | custom-call | bytes 200000000 | tf_op jit(solution)/shard_map/front/pallas_call | solution.py:1039
  121.4 0.0 copy-done.8
  121.4 0.0 copy-done.9
  121.5 0.0 copy-done.10
  121.5 0.6 pad_maximum_fusion.1.vectors
  122.1 89.8 %middle.1 = (f32[256,1024]{1,0:T(8,128)}, f32[256,1024]{1,0:T(8,128)}, bf16[4,256,1024]{2,1,0:T(8,128)(2,1)}, bf16[1024,1024]{1,0:T(8,128)(2,1)}, bf16[1024,1024...) custom-call(bf16[4,256,256]{2,1,0:T(8,128)(2,1)} %get-tuple-element., ...), custom_call_target="tpu_custom_call" | custom-call | bytes 200000000 | tf_op jit(solution)/shard_map/middle/pallas_call | solution.py:1039
  211.9 0.0 copy-start.6
  211.9 75.6 %back.1 = (bf16[4,256,1024]{2,1,0:T(8,128)(2,1)}, bf16[1024,768]{1,0:T(8,128)(2,1)}, f32[8,768]{1,0:T(8,128)}, f32[1,256]{1,0:T(1,128)}, f32[256,1024]{1,0:T(8,1...) custom-call(bf16[4,256,256]{2,1,0:T(8,128)(2,1)} %get-tuple-element., ...), custom_call_target="tpu_custom_call" | custom-call | bytes 200000000 | tf_op jit(solution)/shard_map/back/pallas_call | solution.py:1039
  287.5 0.8 slice_bitcast_fusion.1
  288.3 0.8 slice_bitcast_fusion
  289.1 0.9 slice_reduce_fusion
  290.1 0.8 slice_reduce_fusion.1
  290.9 0.7 slice.116
  291.6 0.1 copy.77
  291.7 0.1 reshape.137
  291.8 0.1 copy.78
  291.9 0.1 reshape.139
  292.0 0.9 reshape.138
  292.9 0.8 reshape.136
  293.7 0.0 copy-done.6
  293.7 0.1 concatenate.9
  293.8 0.9 copy.84
  294.8 0.7 constant_dynamic-update-slice_fusion.1
  295.5 0.7 pad_maximum_fusion.packed
  296.1 74.0 %final.1 = (f32[256,1024]{1,0:T(8,128)}, bf16[1024,768]{1,0:T(8,128)(2,1)}, f32[8,1024]{1,0:T(8,128)}, f32[288,128]{1,0:T(8,128)}, bf16[1024,1024]{1,0:T(8,128)(...) custom-call(bf16[4,256,1024]{2,1,0:T(8,128)(2,1)} %get-tuple-element.83.grad_first, ...), custom_call_target="tpu_custom_call" | custom-call | bytes 200000000 | tf_op jit(solution)/shard_map/final/pallas_call | solution.py:1039
  370.2 0.8 slice_bitcast_fusion.13
  371.0 0.1 slice.122
  371.1 0.6 slice.141
  371.7 0.6 slice.143
  372.3 0.6 slice.145
  372.8 0.9 slice.128
  373.7 0.1 slice.144
  373.8 0.6 slice.142
  374.4 0.7 slice.119
  375.1 1.3 slice_bitcast_fusion.2
  376.4 0.7 fusion.1
  377.1 1.2 slice_bitcast_fusion.7
  378.3 1.7 copy.79
  380.1 2.4 copy.80
  382.4 4.2 %convert_element_type.17 = f32[1024,1024]{1,0:T(8,128)} convert(bf16[1024,1024]{1,0:T(8,128)(2,1)} %get-tuple-element.103) | non-fusion elementwise | flops 1048576 | bytes 6291456 | tf_op jit(solution)/shard_map/convert_element_type | solution.py:1380
  386.6 0.0 copy-done.2
  386.7 2.5 convert_element_type.18
  389.1 1.1 convert_element_type.16
  390.2 0.7 reshape.149
  390.9 0.6 reshape.150
  391.6 0.6 reshape.146
  392.2 0.6 reshape.145
  392.8 0.6 reshape.147
  393.4 1.4 fusion.2
  394.8 0.0 copy-done.3
  394.8 1.0 fusion
  395.8 2.3 copy.92
  (26 shorter events, 0.1 us)
Async XLA Ops:
  7.2 8.5 %copy-start = (bf16[256,1024]{1,0:T(8,128)(2,1)S(1)}, bf16[256,1024]{1,0:T(8,128)(2,1)}, u32[]{:S(2)}) copy-start(bf16[256,1024]{1,0:T(8,128)(2,1)} %param.46) | copy-start | bytes 1572868
  7.2 114.9 %all-gather.2.cloned.1.call-start = ((), (), s32[]{:S(2)}) async-start(), calls=%async_computation | async-start | bytes 2621440 | tf_op jit(solution)/shard_map/all_gather | solution.py:1108
  16.3 105.1 %copy-start.8 = (f32[1024]{0:T(1024)S(1)}, f32[1024]{0:T(1024)}, u32[]{:S(2)}) copy-start(f32[1024]{0:T(1024)} %param.49) | copy-start | bytes 12292
  16.3 105.1 %copy-start.9 = (f32[1024]{0:T(1024)S(1)}, f32[1024]{0:T(1024)}, u32[]{:S(2)}) copy-start(f32[1024]{0:T(1024)} %param.48) | copy-start | bytes 12292
  16.3 105.1 %copy-start.10 = (f32[1024]{0:T(1024)S(1)}, f32[1024]{0:T(1024)}, u32[]{:S(2)}) copy-start(f32[1024]{0:T(1024)} %param.47) | copy-start | bytes 12292
  211.9 81.8 %copy-start.6 = (f32[8,1024]{1,0:T(8,128)S(1)}, f32[8,1024]{1,0:T(8,128)}, u32[]{:S(2)}) copy-start(f32[8,1024]{1,0:T(8,128)} %get-tuple-element.87) | copy-start | bytes 98308
  211.9 83.5 %copy-start.11 = (f32[1,1024]{1,0:T(1,128)S(1)}, f32[1,1024]{1,0:T(1,128)}, u32[]{:S(2)}) copy-start(f32[1,1024]{1,0:T(1,128)} %get-tuple-element.94) | copy-start | bytes 12292
  382.4 4.2 %copy-start.2 = (bf16[1024,1024]{1,0:T(8,128)(2,1)S(1)}, bf16[1024,1024]{1,0:T(8,128)(2,1)}, u32[]{:S(2)}) copy-start(bf16[1024,1024]{1,0:T(8,128)(2,1)} %get-tuple-element.104) | copy-start | bytes 6291460
  386.6 2.5 copy-start.5
  386.6 8.2 %copy-start.4 = (f32[256,1024]{1,0:T(8,128)S(1)}, f32[256,1024]{1,0:T(8,128)}, u32[]{:S(2)}) copy-start(f32[256,1024]{1,0:T(8,128)} %get-tuple-element.82) | copy-start | bytes 3145732
  386.6 8.2 %copy-start.7 = (f32[1024]{0:T(1024)S(1)}, f32[1024]{0:T(1024)}, u32[]{:S(2)}) copy-start(f32[1024]{0:T(1024)} %param.53) | copy-start | bytes 12292
  389.1 5.7 %copy-start.3 = (f32[256,1024]{1,0:T(8,128)S(1)}, f32[256,1024]{1,0:T(8,128)}, u32[]{:S(2)}) copy-start(f32[256,1024]{1,0:T(8,128)} %get-tuple-element.66) | copy-start | bytes 3145732
  394.8 3.3 copy-start.1
Sparse Core Ops, SparseCore 0:
  9.6 66.4 all-gather.1

commit v3 on v2

--- a/solution.py
+++ b/solution.py
@@ -77,7 +77,7 @@
 
 
 def make_taps(
-    features, embed, inner, columns, filter_weight, decay, transforms, pre, taps_bins
+    features, embed, inner, columns, biases, filter_weight, decay, transforms, pre, taps_bins
 ):
     cos_main, sin_main, cos_small, sin_small = transforms
     main_re, main_im, main_top, small_re, small_im, small_top = taps_bins
@@ -89,9 +89,9 @@
             value = exact(embed[...], features[...], ((0,), (0,)))
         else:
             value = exact(inner[i - 1], hidden, ((0,), (0,)))
-        value = value + columns[:, 3 + i : 4 + i]
+        value = value + biases[i]
         pre[i] = value
-        hidden = jnp.sin(columns[:, i : i + 1] * value)
+        hidden = jnp.sin(columns[i] * value)
     taps = exact(hidden, filter_weight[...], ((0,), (0,)))
     taps = (taps * modulation(length, decay[...])).astype(jnp.bfloat16)
     scale = bin_scale(length)
@@ -173,38 +173,39 @@
     return jnp.concatenate([head, main[region : length - region], tail], axis=0)
 
 
-def filter_back_kernel(
+def filter_back(
     grad_taps,
     features,
     embed,
+    rates,
     inner,
-    columns,
     filter_weight,
     decay,
     pre,
-    embed_grad,
-    inner_grad,
-    filter_grad,
-    column_grad,
+    filter_sums,
+    channel_sums,
 ):
     length = features.shape[1]
+    width = filter_weight.shape[0]
+    rows = filter_rows(width)
+    ones = jnp.ones((8, length), jnp.float32)
     raw = grad_taps[...] * modulation(length, decay[...])
     back = exact(filter_weight[...], raw, ((1,), (1,)))
-    column_grad[...] = jnp.zeros_like(column_grad)
     for i in (2, 1, 0):
-        rate = columns[:, i : i + 1]
-        angle = rate * pre[i]
+        angle = rates[i] * pre[i]
         if i == 2:
-            filter_grad[...] = exact(jnp.sin(angle), raw, ((1,), (0,)))
+            channel_sums[:width] = exact(jnp.sin(angle), raw, ((1,), (0,)))
         act = back * jnp.cos(angle)
-        column_grad[:, i : i + 1] = jnp.sum(act * pre[i], axis=1, keepdims=True)
-        step = act * rate
-        column_grad[:, 3 + i : 4 + i] = jnp.sum(step, axis=1, keepdims=True)
+        filter_sums[rows.freq + i : rows.freq + i + 1] = exact(ones, act * pre[i], ((1,), (1,)))[0:1]
+        step = act * rates[i]
+        bias = exact(ones, step, ((1,), (1,)))[0:1]
         if i == 0:
-            embed_grad[...] = exact(features[...], step, ((1,), (1,)))
+            filter_sums[rows.embed_bias : rows.embed_bias + 1] = bias
+            filter_sums[rows.embed : rows.embed + FEAT] = exact(features[...], step, ((1,), (1,)))
         else:
-            below = jnp.sin(columns[:, i - 1 : i] * pre[i - 1])
-            inner_grad[i - 1] = exact(below, step, ((1,), (1,)))
+            filter_sums[rows.inner_bias + i - 1 : rows.inner_bias + i] = bias
+            below = jnp.sin(rates[i - 1] * pre[i - 1])
+            filter_sums[(i - 1) * width : i * width] = exact(below, step, ((1,), (1,)))
             back = exact(inner[i - 1], step, ((1,), (0,)))
 
 
@@ -213,7 +214,7 @@
 
 
 def row_marks(segment, marks, region):
-    ids = segment[...]
+    ids = to_column(segment[...].astype(jnp.float32)).astype(jnp.int32)
     length = ids.shape[0]
     places = lax.broadcasted_iota(jnp.int32, ids.shape, 0)
     inside = ids == ids[region - 1 : region]
@@ -301,6 +302,26 @@
     return pl.ds(pl.multiple_of(index * size, 16), size)
 
 
+def staged(pairs, sems):
+    copies = []
+    for i, (source, target) in enumerate(pairs):
+        copies.append(pltpu.make_async_copy(source, target, sems.at[i]))
+        copies[-1].start()
+    return copies
+
+
+def to_column(row):
+    size = row.shape[1]
+    piece = min(size, 128)
+    shape = (piece, piece)
+    same = lax.broadcasted_iota(jnp.int32, shape, 0) == lax.broadcasted_iota(jnp.int32, shape, 1)
+    pieces = [
+        jnp.sum(jnp.where(same, row[:, i : i + piece], 0.0), axis=1, keepdims=True)
+        for i in range(0, size, piece)
+    ]
+    return jnp.concatenate(pieces, axis=0)
+
+
 class Chain:
     def __init__(self, slots, send_sems, recv_sems):
         self.slots, self.send_sems, self.recv_sems = slots, send_sems, recv_sems
@@ -378,40 +399,60 @@
     gain,
     shift,
     part,
+    cotangent,
     segment,
-    features,
     embed,
+    embed_bias,
+    freq,
     inner,
-    columns,
+    inner_bias,
     filter_weight,
     decay,
-    proj,
     proj_bias,
     short,
     short_bias,
     skip,
-    cos_main,
-    sin_main,
+    features_hbm,
+    proj_hbm,
+    cos_main_hbm,
+    sin_main_hbm,
     cos_small,
     sin_small,
-    first_all,
+    first_out,
     part_all,
-    pre,
-    main_re,
-    main_im,
+    cotangent_out,
+    pre_out,
+    main_re_out,
+    main_im_out,
     main_top,
     small_re,
     small_im,
     small_top,
     gated_own,
+    projected_out,
+    mixed_out,
+    summed_out,
+    features,
+    proj,
+    cos_main,
+    sin_main,
+    first_all,
+    cotangent_all,
+    pre,
+    main_re,
+    main_im,
     projected,
     mixed,
     summed,
     gated,
     marks,
+    load_sems,
+    store_sems,
     local_sems,
     first_send,
     first_recv,
+    cotangent_send,
+    cotangent_recv,
     part_sems,
     chip_sems,
     core_sems,
@@ -427,12 +468,23 @@
     channels = skip.shape[1]
     taps_bins = (main_re, main_im, main_top, small_re, small_im, small_top)
     transforms = (cos_main, sin_main, cos_small, sin_small)
+    loads = staged(
+        [
+            (proj_hbm, proj),
+            (features_hbm, features),
+            (cos_main_hbm, cos_main),
+            (sin_main_hbm, sin_main),
+        ],
+        load_sems,
+    )
     greet(tensor_devices() + [sibling()] + chip_devices())
 
     hat, unused_rate = normalised(tokens[...].astype(jnp.float32))
     first_all[me] = (hat * gain[...] + shift[...]).astype(jnp.bfloat16)
     chain = Chain(first_all, first_send, first_recv)
     chain.advance(0)
+    cotangent_all[me] = cotangent[...]
+    later = Chain(cotangent_all, cotangent_send, cotangent_recv)
     own = pltpu.make_async_copy(part, part_all.at[me, chip, core], local_sems.at[0])
     own.start()
     parts = spread(part, part_all.at[me, chip, core], part_sems, tensor_devices())
@@ -441,13 +493,18 @@
         rows = pl.ds(pl.multiple_of(block * shard, shard), shard)
         for k in range(3):
             lanes = slice(k * channels, (k + 1) * channels)
-            projected[rows, lanes] = dot_nn(first_all[block], proj[k]) + proj_bias[:, lanes]
-
+            projected[rows, lanes] = dot_nn(first_all[block], proj[k]) + proj_bias[k : k + 1]
+
+    wait_all(loads)
     project(me)
+    columns = [to_column(freq[i : i + 1]) for i in range(3)]
+    biases = [to_column(embed_bias[...])] + [to_column(inner_bias[i : i + 1]) for i in range(2)]
     make_taps(
-        features, embed, inner, columns, filter_weight, decay, transforms, pre, taps_bins
+        features, embed, inner, columns, biases, filter_weight, decay, transforms, pre, taps_bins
     )
     row_marks(segment, marks, cos_small.shape[0])
+    stores = [(pre, pre_out), (main_re, main_re_out), (main_im, main_im_out)]
+    stored = staged(stores, store_sems)
 
     def turn(step, carry):
         chain.advance(step)
@@ -469,6 +526,9 @@
     held = part_all.at[:, chip, core]
     parts = spread(held, held, chip_sems, chip_devices())
     lax.fori_loop(2, count, turn, 0)
+    later.advance(0)
+    more = store_sems.at[pl.ds(len(stores), 5)]
+    stored += staged([(first_all, first_out), (projected, projected_out)], more)
     wait_all(parts)
     held = part_all.at[:, :, core]
     parts = spread(held, held, core_sems, [sibling()])
@@ -476,12 +536,14 @@
     for k in range(3):
         lanes = slice(k * channels, (k + 1) * channels)
         value = projected[:, lanes]
-        running = short_bias[:, lanes] + short[0:1, lanes] * value
+        running = short_bias[k : k + 1] + short[0, k : k + 1] * value
         for lag in (1, 2):
             moved = jnp.where(marks[:, lag : lag + 1] > 0, pltpu.roll(value, lag, 0), 0.0)
-            running = running + short[lag : lag + 1, lanes] * moved
+            running = running + short[lag, k : k + 1] * moved
         mixed[:, lanes] = running
     product = mixed[:, 2 * channels :] * mixed[:, channels : 2 * channels]
+    more = store_sems.at[pl.ds(len(stores) + 2, 3)]
+    stored += staged([(mixed, mixed_out)], more)
     low = product.astype(jnp.bfloat16).astype(jnp.float32)
     main_bins, small_bins = spectra(low, marks, *transforms)
     result = filtered(
@@ -499,35 +561,56 @@
     swapped = spread(
         lambda k: gated.at[peers[k]], gated_own.at[me], gated_sems, tensor_devices()
     )
+    more = store_sems.at[pl.ds(len(stores) + 3, 2)]
+    stored += staged([(summed, summed_out)], more)
     gated_own[me] = gated[me]
+    for step in range(1, count):
+        later.advance(step)
+    more = store_sems.at[pl.ds(len(stores) + 4, 1)]
+    stored += staged([(cotangent_all, cotangent_out)], more)
     chain.finish()
-    wait_all(parts + swapped)
+    later.finish()
+    wait_all(parts + swapped + stored)
 
 
 def middle_kernel(
     gated,
     out,
     tokens,
-    vectors,
+    out_bias,
+    gain,
+    shift,
+    cotangent_hbm,
+    up_hbm,
+    bias,
+    down_hbm,
+    residual_out,
+    grad_residual,
+    mlp_out,
+    up_out,
+    down_out,
+    bias_grad,
+    grad_gated,
+    out_grad,
+    gain_sum,
+    shift_sum,
+    out_sum,
+    down_sum,
     cotangent,
     up,
-    bias,
     down,
     residual,
-    grad_residual,
     mlp,
     up_grad,
     down_grad,
-    bias_grad,
-    grad_gated,
-    out_grad,
-    sums,
     second,
     active,
     low,
     parting,
     arriving,
     own_part,
+    load_sems,
+    store_sems,
     second_send,
     second_recv,
     part_send,
@@ -537,13 +620,14 @@
     count = lax.axis_size("tensor")
     shard, width = tokens.shape
     units = up.shape[1]
+    loads = staged([(up_hbm, up), (down_hbm, down), (cotangent_hbm, cotangent)], load_sems)
     greet(tensor_devices())
-    base = tokens[...].astype(jnp.float32) + vectors[0:1]
+    base = tokens[...].astype(jnp.float32) + out_bias[...]
     for block in range(count):
         base = base + dot_nn(gated[block], out[block])
     residual[...] = base
     hat, unused_rate = normalised(base)
-    second[me] = (hat * vectors[1:2] + vectors[2:3]).astype(jnp.bfloat16)
+    second[me] = (hat * gain[...] + shift[...]).astype(jnp.bfloat16)
     chain = Chain(second, second_send, second_recv)
     bias_grad[...] = jnp.zeros_like(bias_grad)
 
@@ -558,7 +642,6 @@
 
     def work(block):
         cut = units // 2
-        mlp_part = None
         for lanes in (slice(0, cut), slice(cut, units)):
             hidden = dot_nn(second[block], up[:, lanes]) + bias[:, lanes]
             cube = GELU_CUBE * hidden * hidden
@@ -585,6 +668,10 @@
     def turn(step, carry):
         chain.advance(step)
 
+        @pl.when(step == 0)
+        def _():
+            wait_all(loads)
+
         def side(index, carry):
             block = me + step * (2 * index - 1)
 
@@ -597,6 +684,7 @@
         return lax.fori_loop(0, 2, side, carry)
 
     lax.fori_loop(0, count, turn, 0)
+    stored = staged([(residual, residual_out), (mlp, mlp_out)], store_sems)
     tokens_all = count * shard
     up_grad[...] = dot_tn(
         second[...].reshape(tokens_all, width), low[...].reshape(tokens_all, units)
@@ -604,21 +692,25 @@
     down_grad[...] = dot_tn(
         active[...].reshape(tokens_all, units), cotangent[...].reshape(tokens_all, width)
     ).astype(jnp.bfloat16)
+    stored += staged([(up_grad, up_out), (down_grad, down_out)], store_sems.at[pl.ds(2, 2)])
     for peer in tensor_peers():
         remote(
-            parting.at[peer], arriving.at[peer], part_send.at[peer], part_recv.at[peer], {"tensor": peer}
+            parting.at[peer],
+            arriving.at[peer],
+            part_send.at[peer],
+            part_recv.at[peer],
+            {"tensor": peer},
         ).wait_recv()
         own_part[...] += arriving[peer].astype(jnp.float32)
     grad_normed = own_part[...]
     hat, rate = normalised(residual[...])
     grad_out = cotangent[me].astype(jnp.float32)
-    grad = grad_out + norm_back(grad_normed, vectors[1:2], hat, rate)
+    grad = grad_out + norm_back(grad_normed, gain[...], hat, rate)
     grad_residual[...] = grad
-    sums[...] = jnp.zeros_like(sums)
-    sums[0:1] = column_sum(grad_normed * hat)
-    sums[1:2] = column_sum(grad_normed)
-    sums[2:3] = column_sum(grad)
-    sums[3:4] = column_sum(grad_out)
+    gain_sum[...] = column_sum(grad_normed * hat)
+    shift_sum[...] = column_sum(grad_normed)
+    out_sum[...] = column_sum(grad)
+    down_sum[...] = column_sum(grad_out)
     grad_low = grad.astype(jnp.bfloat16)
     for block in range(count):
         grad_gated[block] = dot_nt(grad_low, out[block]).astype(jnp.bfloat16)
@@ -626,6 +718,7 @@
     chain.finish()
     for peer in tensor_peers():
         sent(peer).wait_send()
+    wait_all(stored)
 
 
 class RowReduce:
@@ -720,7 +813,7 @@
 class RowGather:
     def __init__(self, part, total, refs):
         self.part, self.total = part, total
-        self.chip_sems, self.core_sems = refs
+        self.own_sem, self.chip_sems, self.core_sems = refs
         place = lax.axis_index("dp")
         core, chip = lax.rem(place, 2), place // 2
         chips = lax.axis_size("dp") // 2
@@ -729,8 +822,8 @@
 
     def plane(self):
         own = self.total.at[self.mine]
-        own[...] = self.part[...]
-        self.copies = spread(own, own, self.chip_sems, chip_devices())
+        self.copies = staged([(self.part, own)], self.own_sem)
+        self.copies += spread(self.part, own, self.chip_sems, chip_devices())
 
     def pair(self):
         wait_all(self.copies)
@@ -742,7 +835,91 @@
 
 
 def row_gather_scratch(chips):
-    return [pltpu.SemaphoreType.DMA((2, chips - 1)), pltpu.SemaphoreType.DMA((2, 1))]
+    return [
+        pltpu.SemaphoreType.DMA((1,)),
+        pltpu.SemaphoreType.DMA((2, chips - 1)),
+        pltpu.SemaphoreType.DMA((2, 1)),
+    ]
+
+
+class SmallSums:
+    def __init__(self, sources, results, wide, refs):
+        self.sources, self.results, self.wide = sources, results, wide
+        count = len(sources)
+        self.core_recv = refs[:count]
+        self.chip_slots = refs[count : 2 * count]
+        self.group_slots = refs[2 * count : 2 * count + wide]
+        self.core_sems, self.chip_sems, self.group_sems = refs[2 * count + wide :]
+        self.me = lax.axis_index("tensor")
+        self.chip = lax.axis_index("dp") // 2
+
+    def pair(self):
+        self.copies = []
+        for i, source in enumerate(self.sources):
+            self.copies += spread(source, self.core_recv[i], self.core_sems.at[i], [sibling()])
+
+    def plane(self):
+        wait_all(self.copies)
+        self.copies = []
+        for i, source in enumerate(self.sources):
+            self.chip_slots[i][self.chip] = source[...] + self.core_recv[i][...]
+            own = self.chip_slots[i].at[self.chip]
+            self.copies += spread(own, own, self.chip_sems.at[i], chip_devices())
+
+    def total(self, slots):
+        value = slots[0]
+        for i in range(1, slots.shape[0]):
+            value = value + slots[i]
+        return value
+
+    def tensor(self):
+        wait_all(self.copies)
+        self.copies = []
+        for i in range(len(self.sources)):
+            if i >= self.wide:
+                self.results[i][...] = self.total(self.chip_slots[i])
+                continue
+            self.group_slots[i][self.me] = self.total(self.chip_slots[i])
+            own = self.group_slots[i].at[self.me]
+            self.copies += spread(own, own, self.group_sems.at[i], tensor_devices())
+
+    def finish(self):
+        wait_all(self.copies)
+        for i in range(self.wide):
+            self.results[i][...] = self.total(self.group_slots[i])
+
+
+def small_sums_scratch(shapes, wide, chips, groups):
+    return (
+        [pltpu.VMEM(shape, jnp.float32) for shape in shapes]
+        + [pltpu.VMEM((chips,) + tuple(shape), jnp.float32) for shape in shapes]
+        + [pltpu.VMEM((groups,) + tuple(shape), jnp.float32) for shape in shapes[:wide]]
+        + [
+            pltpu.SemaphoreType.DMA((len(shapes), 2, 1)),
+            pltpu.SemaphoreType.DMA((len(shapes), 2, chips - 1)),
+            pltpu.SemaphoreType.DMA((max(wide, 1), 2, groups - 1)),
+        ]
+    )
+
+
+class channel_rows:
+    def __init__(self, width):
+        self.filter = 0
+        self.short = width
+        self.short_bias = width + 9
+        self.proj_bias = width + 12
+        self.skip = width + 15
+        self.size = width + 16
+
+
+class filter_rows:
+    def __init__(self, width):
+        self.inner = 0
+        self.embed = 2 * width
+        self.embed_bias = self.embed + FEAT + -FEAT % 8
+        self.freq = self.embed_bias + 1
+        self.inner_bias = self.embed_bias + 4
+        self.size = self.embed_bias + 8
 
 
 def back_kernel(
@@ -751,47 +928,54 @@
     up_grad,
     down_grad,
     out_grad,
-    proj,
     short,
     skip,
     segment,
-    features,
     embed,
+    freq,
     inner,
-    columns,
     filter_weight,
     decay,
-    pre,
-    cos_main,
-    sin_main,
-    cos_small,
-    sin_small,
-    main_re,
-    main_im,
     main_top,
     small_re,
     small_im,
     small_top,
-    projected,
-    mixed,
-    summed,
+    cos_small,
+    sin_small,
+    mixed_hbm,
+    cos_main_hbm,
+    sin_main_hbm,
+    main_re_hbm,
+    main_im_hbm,
+    summed_hbm,
+    projected_hbm,
+    proj_hbm,
+    features_hbm,
+    pre_hbm,
     grad_first,
     grad_low,
-    sums,
-    skip_sum,
     mlp_sum,
     up_part,
     down_part,
     out_part,
-    embed_grad,
-    inner_grad,
-    filter_grad,
-    column_grad,
+    filter_sums,
+    channel_sums,
+    mixed,
+    cos_main,
+    sin_main,
+    main_re,
+    main_im,
+    summed,
+    projected,
+    proj,
+    features,
+    pre,
     grad_gated,
     grad_taps,
     marks,
     mlp_own,
     mlp_recv,
+    load_sems,
     local_sems,
     gated_sems,
     mlp_sems,
@@ -805,12 +989,28 @@
     region = cos_small.shape[0]
     shard = length // count
     transforms = (cos_main, sin_main, cos_small, sin_small)
+    loads = staged(
+        [
+            (mixed_hbm, mixed),
+            (cos_main_hbm, cos_main),
+            (sin_main_hbm, sin_main),
+            (main_re_hbm, main_re),
+            (main_im_hbm, main_im),
+            (summed_hbm, summed),
+            (projected_hbm, projected),
+            (proj_hbm, proj),
+            (features_hbm, features),
+            (pre_hbm, pre),
+        ],
+        load_sems,
+    )
     greet(tensor_devices() + [sibling()] + chip_devices())
     up_row = RowReduce(up_grad, up_part, scratch[:6])
     down_row = RowReduce(down_grad, down_part, scratch[6:12])
-    out_row = RowReduce(out_grad, out_part, scratch[12:])
+    out_row = RowReduce(out_grad, out_part, scratch[12:21])
     weights = (out_row, up_row, down_row)
-
+    places = channel_rows(filter_weight.shape[0])
+    filter_sums[...] = jnp.zeros_like(filter_sums)
     own = pltpu.make_async_copy(grad_blocks.at[me], grad_gated.at[me], local_sems.at[0])
     own.start()
     arriving = spread(
@@ -821,6 +1021,7 @@
     own_mlp = pltpu.make_async_copy(mlp.at[me], mlp_own, local_sems.at[1])
     own_mlp.start()
     row_marks(segment, marks, region)
+    wait_all(loads[:3])
     gate_out = mixed[:, :channels]
     gate_in = mixed[:, channels : 2 * channels]
     values = mixed[:, 2 * channels :]
@@ -836,7 +1037,7 @@
     )
     grad = grad_gated[...].reshape(length, channels).astype(jnp.float32)
     grad_summed = grad * gate_out
-    skip_sum[...] = column_sum(grad_summed * product)
+    channel_sums[places.skip : places.skip + 1] = column_sum(grad_summed * product)
     low = grad_summed.astype(jnp.bfloat16).astype(jnp.float32)
     grad_main, grad_small = spectra(low, marks, *transforms)
     real, imag, top = times(value_main, grad_main, True)
@@ -850,7 +1051,7 @@
     taps_small = from_bins((real * scale, imag * scale, top * (0.5 / region)), cos_small, sin_small)
     grad_taps[:region] = taps[:region] + taps_small
     grad_taps[region:] = taps[region:]
-    out_row.cross()
+    wait_all(loads[3:])
     result = filtered(
         grad_main,
         grad_small,
@@ -865,35 +1066,37 @@
     for k, part in enumerate(parts):
         lanes = slice(k * channels, (k + 1) * channels)
         source = projected[:, lanes]
-        sums[3:4, lanes] = column_sum(part)
-        sums[0:1, lanes] = column_sum(part * source)
-        running = short[0:1, lanes] * part
+        row = places.short_bias + k
+        channel_sums[row : row + 1] = column_sum(part)
+        row = places.short + k
+        channel_sums[row : row + 1] = column_sum(part * source)
+        running = short[0, k : k + 1] * part
         for lag in (1, 2):
             kept = jnp.where(marks[:, lag : lag + 1] > 0, part, 0.0)
-            sums[lag : lag + 1, lanes] = column_sum(kept * pltpu.roll(source, lag, 0))
-            running = running + short[lag : lag + 1, lanes] * pltpu.roll(kept, length - lag, 0)
-        sums[4:5, lanes] = column_sum(running)
+            row = places.short + 3 * lag + k
+            channel_sums[row : row + 1] = column_sum(kept * pltpu.roll(source, lag, 0))
+            running = running + short[lag, k : k + 1] * pltpu.roll(kept, length - lag, 0)
+        row = places.proj_bias + k
+        channel_sums[row : row + 1] = column_sum(running)
         grad_low[:, lanes] = running.astype(jnp.bfloat16)
-    sums[5:8] = jnp.zeros_like(sums[5:8])
+    out_row.cross()
     for block in range(count):
         rows = slice(block * shard, (block + 1) * shard)
         total = dot_nt(grad_low[rows, :channels], proj[0])
         for k in (1, 2):
             total = total + dot_nt(grad_low[rows, k * channels : (k + 1) * channels], proj[k])
         grad_first[block] = total.astype(jnp.bfloat16)
-    filter_back_kernel(
+    filter_back(
         grad_taps,
         features,
         embed,
+        [to_column(freq[i : i + 1]) for i in range(3)],
         inner,
-        columns,
         filter_weight,
         decay,
         pre,
-        embed_grad,
-        inner_grad,
-        filter_grad,
-        column_grad,
+        filter_sums,
+        channel_sums,
     )
     for weight in weights:
         weight.finish()
@@ -905,132 +1108,203 @@
     mlp_sum[...] = total
 
 
-class SmallSum:
-    def __init__(self, packed, result, refs):
-        self.packed, self.result = packed, result
-        (
-            self.core_recv,
-            self.chip_slots,
-            self.group_slots,
-            self.core_sems,
-            self.chip_sems,
-            self.group_sems,
-        ) = refs
-        self.me = lax.axis_index("tensor")
-        self.chip = lax.axis_index("dp") // 2
-        self.wide = self.group_slots.shape[1]
-
-    def pair(self):
-        self.copies = spread(self.packed, self.core_recv, self.core_sems, [sibling()])
-
-    def plane(self):
-        wait_all(self.copies)
-        self.chip_slots[self.chip] = self.packed[...] + self.core_recv[...]
-        own = self.chip_slots.at[self.chip]
-        self.copies = spread(own, own, self.chip_sems, chip_devices())
-
-    def tensor(self):
-        wait_all(self.copies)
-        total = self.chip_slots[0]
-        for i in range(1, self.chip_slots.shape[0]):
-            total = total + self.chip_slots[i]
-        self.result[...] = total
-        self.group_slots[self.me] = total[: self.wide]
-        own = self.group_slots.at[self.me]
-        self.copies = spread(own, own, self.group_sems, tensor_devices())
-
-    def finish(self):
-        wait_all(self.copies)
-        total = self.group_slots[0]
-        for i in range(1, self.group_slots.shape[0]):
-            total = total + self.group_slots[i]
-        self.result[: self.wide] = total
-
-
-def small_sum_scratch(shape, wide, chips, groups):
-    rows, columns = shape
-    return [
-        pltpu.VMEM((rows, columns), jnp.float32),
-        pltpu.VMEM((chips, rows, columns), jnp.float32),
-        pltpu.VMEM((groups, wide, columns), jnp.float32),
-        pltpu.SemaphoreType.DMA((2, 1)),
-        pltpu.SemaphoreType.DMA((2, chips - 1)),
-        pltpu.SemaphoreType.DMA((2, groups - 1)),
-    ]
-
-
 def final_kernel(
     grad_first,
-    first,
-    grad_low,
     tokens,
     gain,
-    grad_residual,
-    packed,
+    shift,
+    out_bias_sum,
+    gain_sum,
+    shift_sum,
+    down_bias_sum,
+    filter_sums,
+    channel_sums,
+    up_bias_sum,
     up_part,
     down_part,
     out_part,
+    first_hbm,
+    grad_low_hbm,
     grad_tokens,
     proj_sum,
-    norm_sums,
-    packed_sum,
     up_sum,
     down_sum,
     out_sum,
+    line_all,
+    filter_all,
+    channel_all,
+    up_bias_all,
+    first,
+    grad_low,
     proj_grad,
     proj_part,
-    norm_own,
+    lines,
+    load_sems,
     block_recv,
     block_sems,
     *scratch,
 ):
     me = lax.axis_index("tensor")
+    count = lax.axis_size("tensor")
     peers = tensor_peers()
+    loads = staged([(first_hbm, first), (grad_low_hbm, grad_low)], load_sems)
     greet(tensor_devices() + [sibling()] + chip_devices())
     blocks = spread(
         lambda k: grad_first.at[peers[k]], lambda k: block_recv.at[k], block_sems, tensor_devices()
     )
     row = RowReduce(proj_grad, proj_part, scratch[:6])
-    proj_all = RowGather(proj_part, proj_sum, scratch[6:8])
-    gathers = [
-        RowGather(up_part, up_sum, scratch[8:10]),
-        RowGather(down_part, down_sum, scratch[10:12]),
-        RowGather(out_part, out_sum, scratch[12:14]),
-    ]
-    small = SmallSum(packed, packed_sum, scratch[14:20])
-    norms = SmallSum(norm_own, norm_sums, scratch[20:26])
+    proj_all = RowGather(proj_part, proj_sum, scratch[6:9])
+    gathers = (
+        RowGather(up_part, up_sum, scratch[9:12]),
+        RowGather(down_part, down_sum, scratch[12:15]),
+        RowGather(out_part, out_sum, scratch[15:18]),
+    )
+    small = SmallSums(
+        (lines, filter_sums, channel_sums, up_bias_sum),
+        (line_all, filter_all, channel_all, up_bias_all),
+        2,
+        scratch[18:],
+    )
+    length, columns = grad_low.shape
+    channels = columns // 3
+    width = tokens.shape[1]
+    wait_all(loads)
+    for k in range(3):
+        proj_grad[k * width : (k + 1) * width] = dot_tn(
+            first[...].reshape(length, width), grad_low[:, k * channels : (k + 1) * channels]
+        ).astype(jnp.bfloat16)
+    row.pair()
+    plain = jnp.zeros_like(gain[...])
+    scaled = jnp.zeros_like(gain[...])
+    for block in range(count):
+        grad = grad_first[block].astype(jnp.float32)
+        plain = plain + column_sum(grad)
+        scaled = scaled + column_sum(grad * first[block].astype(jnp.float32))
+    lines[0:1] = out_bias_sum[...]
+    lines[1:2] = gain_sum[...]
+    lines[2:3] = shift_sum[...]
+    lines[3:4] = down_bias_sum[...]
+    lines[4:5] = (scaled - shift[...] * plain) / gain[...]
+    lines[5:6] = plain
+    lines[6:8] = jnp.zeros_like(lines[6:8])
     small.pair()
-    length = grad_low.shape[0]
-    proj_grad[...] = dot_tn(first[...].reshape(length, first.shape[2]), grad_low[...]).astype(
-        jnp.bfloat16
-    )
-    row.pair()
-    small.plane()
     row.plane()
     for gather in gathers:
         gather.plane()
+    small.plane()
     hat, rate = normalised(tokens[...].astype(jnp.float32))
-    small.tensor()
     row.finish()
     proj_all.plane()
-    small.finish()
+    small.tensor()
     for gather in gathers:
         gather.pair()
     proj_all.pair()
+    small.finish()
     grad = grad_first[me].astype(jnp.float32)
     for k, copy in enumerate(blocks):
         copy.wait()
         grad = grad + block_recv[k].astype(jnp.float32)
-    norm_own[...] = jnp.zeros_like(norm_own)
-    norm_own[0:1] = column_sum(grad * hat)
-    norm_own[1:2] = column_sum(grad)
-    norms.pair()
-    grad_tokens[...] = grad_residual[...] + norm_back(grad, gain[...], hat, rate)
-    norms.plane()
-    norms.tensor()
-    norms.finish()
-    for gather in gathers + [proj_all]:
+    grad_tokens[...] = norm_back(grad, gain[...], hat, rate)
+    for gather in gathers + (proj_all,):
         gather.finish()
+
+
+def finish_kernel(
+    residual,
+    mlp_sum,
+    down_bias,
+    grad_tokens,
+    grad_residual,
+    proj_sum,
+    up_sum,
+    down_sum,
+    out_sum,
+    line_all,
+    filter_all,
+    channel_all,
+    up_bias_all,
+    layer_out,
+    tokens_out,
+    proj_out,
+    up_out,
+    down_out,
+    out_out,
+    out_bias_out,
+    gain2_out,
+    shift2_out,
+    down_bias_out,
+    gain1_out,
+    shift1_out,
+    embed_out,
+    embed_bias_out,
+    freq_out,
+    inner_out,
+    inner_bias_out,
+    filter_out,
+    short_out,
+    short_bias_out,
+    proj_bias_out,
+    skip_out,
+    up_bias_out,
+):
+    layer_out[...] = (residual[...] + mlp_sum[...] + down_bias[...]).astype(layer_out.dtype)
+    tokens_out[...] = grad_tokens[...] + grad_residual[...]
+    for source, target in (
+        (proj_sum, proj_out),
+        (up_sum, up_out),
+        (down_sum, down_out),
+        (out_sum, out_out),
+    ):
+        target[...] = source[...].astype(jnp.float32)
+
+    @pl.when(pl.program_id(0) == 0)
+    def _():
+        lines = (out_bias_out, gain2_out, shift2_out, down_bias_out, gain1_out, shift1_out)
+        for i, line in enumerate(lines):
+            line[...] = line_all[i : i + 1]
+        width = filter_out.shape[0]
+        rows = filter_rows(width)
+        for i in range(2):
+            inner_out[i] = filter_all[i * width : (i + 1) * width]
+        embed_out[...] = filter_all[rows.embed : rows.embed + FEAT]
+        embed_bias_out[...] = filter_all[rows.embed_bias : rows.embed_bias + 1]
+        freq_out[...] = filter_all[rows.freq : rows.freq + 3]
+        inner_bias_out[...] = filter_all[rows.inner_bias : rows.inner_bias + 2]
+        rows = channel_rows(width)
+        filter_out[...] = channel_all[:width]
+        for lag in range(3):
+            row = rows.short + 3 * lag
+            short_out[lag] = channel_all[row : row + 3]
+        short_bias_out[...] = channel_all[rows.short_bias : rows.short_bias + 3]
+        proj_bias_out[...] = channel_all[rows.proj_bias : rows.proj_bias + 3]
+        skip_out[...] = channel_all[rows.skip : rows.skip + 1]
+        up_bias_out[...] = up_bias_all[...]
+
+
+def finish(big, shapes):
+    steps = 8
+
+    def rows(shape):
+        return pl.BlockSpec((shape[0] // steps, shape[1]), lambda i: (i, 0))
+
+    def whole(shape):
+        return pl.BlockSpec(tuple(shape), lambda i: (0,) * len(shape))
+
+    in_specs = [
+        whole(array.shape) if i == 2 or i > 8 else rows(array.shape) for i, array in enumerate(big)
+    ]
+    out_specs = [rows(shape.shape) if i < 6 else whole(shape.shape) for i, shape in enumerate(shapes)]
+    return pl.pallas_call(
+        finish_kernel,
+        grid=(steps,),
+        in_specs=in_specs,
+        out_specs=out_specs,
+        out_shape=shapes,
+        compiler_params=pltpu.CompilerParams(
+            dimension_semantics=("arbitrary",), vmem_limit_bytes=48 * 1024 * 1024
+        ),
+        name="finish",
+    )(*big)
 
 
 def communicate(kernel, shapes, operands, anywhere, scratch, channel, name):
@@ -1095,25 +1369,24 @@
     region = shard_len
     chips = rows // 2
     proj_columns = 3 * channels
-    transforms = transform(length) + transform(region)
+    cos_main, sin_main = transform(length)
+    cos_small, sin_small = transform(region)
     features = features_by_row()
-    columns = jnp.stack(
-        [*sine_freq, embed_bias, *inner_bias] + [jnp.zeros_like(embed_bias)] * 2, axis=1
-    )
     decay = decay_rate[None]
     width = embed_weight.shape[1]
-    segment = segment_ids.reshape(length, 1)
+    embed_bias = embed_bias[None]
     proj = proj_weight.transpose(1, 0, 2)
-    cotangent = cotangent[0]
-    all_cotangent = lax.all_gather(cotangent, "tensor")
-    short_flat = short_weight.reshape(3, proj_columns)
     skip = skip_gain[None]
-    filter_parts = [features, embed_weight, inner_weight, columns, filter_weight, decay]
     semaphores = pltpu.SemaphoreType.DMA
+    vmem = pltpu.VMEM
+    single = jnp.float32
     blocked = (groups, shard_len, model_width)
+    swapped = (groups, shard_len, channels)
+    line = (1, model_width)
     (
         first_all,
         out_all,
+        all_cotangent,
         pre,
         main_re,
         main_im,
@@ -1130,6 +1403,7 @@
         [
             shaped(blocked, low),
             shaped((groups, chips, 2) + out_part.shape, low),
+            shaped(blocked, low),
             shaped((3, width, length)),
             shaped((length, channels)),
             shaped((length, channels)),
@@ -1137,7 +1411,7 @@
             shaped((region, channels)),
             shaped((region, channels)),
             shaped((1, channels)),
-            shaped((groups, shard_len, channels), low),
+            shaped(swapped, low),
             shaped((length, proj_columns)),
             shaped((length, proj_columns)),
             shaped((length, channels)),
@@ -1147,20 +1421,47 @@
             norm1_gain[None],
             norm1_bias[None],
             out_part,
-            segment,
-            *filter_parts,
+            cotangent[0],
+            segment_ids,
+            embed_weight,
+            embed_bias,
+            sine_freq,
+            inner_weight,
+            inner_bias,
+            filter_weight,
+            decay,
+            proj_bias,
+            short_weight,
+            short_bias,
+            skip,
+            features,
             proj,
-            proj_bias.reshape(1, proj_columns),
-            short_flat,
-            short_bias.reshape(1, proj_columns),
-            skip,
-            *transforms,
+            cos_main,
+            sin_main,
+            cos_small,
+            sin_small,
         ],
-        ((3,), (1,)),
+        ((3, 17, 18, 19, 20), (0, 1, 2, 3, 4, 5, 11, 12, 13)),
         [
-            pltpu.VMEM((groups, shard_len, channels), low),
-            pltpu.VMEM((length, 8), jnp.int32),
+            vmem(features.shape, single),
+            vmem(proj.shape, low),
+            vmem(cos_main.shape, low),
+            vmem(sin_main.shape, low),
+            vmem(blocked, low),
+            vmem(blocked, low),
+            vmem((3, width, length), single),
+            vmem((length, channels), single),
+            vmem((length, channels), single),
+            vmem((length, proj_columns), single),
+            vmem((length, proj_columns), single),
+            vmem((length, channels), single),
+            vmem(swapped, low),
+            vmem((length, 8), jnp.int32),
+            semaphores((4,)),
+            semaphores((8,)),
             semaphores((1,)),
+            semaphores((2, groups)),
+            semaphores((groups,)),
             semaphores((2, groups)),
             semaphores((groups,)),
             semaphores((2, groups - 1)),
@@ -1171,9 +1472,7 @@
         0,
         "front",
     )
-    taps_bins = (main_re, main_im, main_top, small_re, small_im, small_top)
     out_all = out_all[..., :channel_slice, :].reshape(groups, channels, model_width)
-    vectors = jnp.stack([out_bias, norm2_gain, norm2_bias])
     (
         residual,
         grad_residual,
@@ -1183,7 +1482,10 @@
         grad_up_bias,
         grad_gated,
         out_grad,
-        middle_sums,
+        grad_norm2_gain,
+        grad_norm2_bias,
+        grad_out_bias,
+        grad_down_bias,
     ) = communicate(
         middle_kernel,
         [
@@ -1193,28 +1495,42 @@
             shaped((model_width, units), low),
             shaped((units, model_width), low),
             shaped((1, units)),
-            shaped((groups, shard_len, channels), low),
+            shaped(swapped, low),
             shaped((groups, channels, model_width), low),
-            shaped((8, model_width)),
+            shaped(line),
+            shaped(line),
+            shaped(line),
+            shaped(line),
         ],
         [
             gated_own,
             out_all,
             tokens[0],
-            vectors,
+            out_bias[None],
+            norm2_gain[None],
+            norm2_bias[None],
             all_cotangent,
             up_weight,
             up_bias[None],
             down_weight,
         ],
-        ((), ()),
+        ((6, 7, 9), (0, 2, 3, 4)),
         [
-            pltpu.VMEM(blocked, low),
-            pltpu.VMEM((groups, shard_len, units), low),
-            pltpu.VMEM((groups, shard_len, units), low),
-            pltpu.VMEM(blocked, low),
-            pltpu.VMEM(blocked, low),
-            pltpu.VMEM((shard_len, model_width), jnp.float32),
+            vmem(blocked, low),
+            vmem((model_width, units), low),
+            vmem((units, model_width), low),
+            vmem((shard_len, model_width), single),
+            vmem(blocked, low),
+            vmem((model_width, units), low),
+            vmem((units, model_width), low),
+            vmem(blocked, low),
+            vmem((groups, shard_len, units), low),
+            vmem((groups, shard_len, units), low),
+            vmem(blocked, low),
+            vmem(blocked, low),
+            vmem((shard_len, model_width), single),
+            semaphores((3,)),
+            semaphores((4,)),
             semaphores((2, groups)),
             semaphores((groups,)),
             semaphores((groups,)),
@@ -1225,34 +1541,29 @@
     )
     fold = max(1, 32 * chips // channels)
     out_grad = out_grad.reshape(groups, channels * fold, model_width // fold)
+    out_size = (channels * fold // rows, model_width // fold)
+    filter_shape = (filter_rows(width).size, width)
+    channel_shape = (channel_rows(width).size, channels)
     (
         grad_first,
         grad_low,
-        back_sums,
-        skip_sum,
         mlp_out,
         up_part,
         down_part,
         out_part,
-        embed_grad,
-        grad_inner_weight,
-        grad_filter_weight,
-        column_grad,
+        filter_sums,
+        channel_sums,
     ) = communicate(
         back_kernel,
         [
             shaped(blocked, low),
             shaped((length, proj_columns), low),
-            shaped((8, proj_columns)),
-            shaped((1, channels)),
             shaped((shard_len, model_width)),
             shaped((model_width // rows, units), low),
             shaped((units // rows, model_width), low),
-            shaped((channels * fold // rows, model_width // fold), low),
-            shaped(embed_weight.shape),
-            shaped(inner_weight.shape),
-            shaped(filter_weight.shape),
-            shaped(columns.shape),
+            shaped(out_size, low),
+            shaped(filter_shape),
+            shaped(channel_shape),
         ],
         [
             grad_gated,
@@ -1260,25 +1571,49 @@
             up_grad,
             down_grad,
             out_grad,
+            short_weight,
+            skip,
+            segment_ids,
+            embed_weight,
+            sine_freq,
+            inner_weight,
+            filter_weight,
+            decay,
+            main_top,
+            small_re,
+            small_im,
+            small_top,
+            cos_small,
+            sin_small,
+            mixed,
+            cos_main,
+            sin_main,
+            main_re,
+            main_im,
+            summed,
+            projected,
             proj,
-            short_flat,
-            skip,
-            segment,
-            *filter_parts,
+            features,
             pre,
-            *transforms,
-            *taps_bins,
-            projected,
-            mixed,
-            summed,
         ],
-        ((0, 1, 2, 3, 4), ()),
+        ((0, 1, 2, 3, 4, 19, 20, 21, 22, 23, 24, 25, 26, 27, 28), ()),
         [
-            pltpu.VMEM((groups, shard_len, channels), low),
-            pltpu.VMEM((length, channels), jnp.float32),
-            pltpu.VMEM((length, 8), jnp.int32),
-            pltpu.VMEM((shard_len, model_width), low),
-            pltpu.VMEM((groups - 1, shard_len, model_width), low),
+            vmem((length, proj_columns), single),
+            vmem(cos_main.shape, low),
+            vmem(sin_main.shape, low),
+            vmem((length, channels), single),
+            vmem((length, channels), single),
+            vmem((length, channels), single),
+            vmem((length, proj_columns), single),
+            vmem(proj.shape, low),
+            vmem(features.shape, single),
+            vmem(pre.shape, single),
+            vmem(swapped, low),
+            vmem((length, channels), single),
+            vmem((length, 8), jnp.int32),
+            vmem((shard_len, model_width), low),
+            vmem((groups - 1, shard_len, model_width), low),
+            semaphores((10,)),
             semaphores((2,)),
             semaphores((2, groups - 1)),
             semaphores((2, groups - 1)),
@@ -1289,142 +1624,157 @@
         2,
         "back",
     )
-    grad_norm2_gain, grad_norm2_bias, grad_out_bias, grad_down_bias = middle_sums[:4]
-    grad_skip_gain = skip_sum[0]
-    grad_up_bias = grad_up_bias[0]
-    grad_short_weight = back_sums[:3].reshape(short_weight.shape)
-    grad_short_bias = back_sums[3].reshape(short_bias.shape)
-    grad_proj_bias = back_sums[4].reshape(proj_bias.shape)
-    grad_embed_weight = embed_grad
-    grad_sine_freq = column_grad[:, :3].T
-    grad_embed_bias = column_grad[:, 3]
-    grad_inner_bias = column_grad[:, 4:6].T
-
-    everywhere = (
+    (
+        grad_tokens,
+        proj_sum,
+        up_sum,
+        down_sum,
+        out_sum,
+        line_all,
+        filter_all,
+        channel_all,
+        up_bias_all,
+    ) = communicate(
+        final_kernel,
+        [
+            shaped((shard_len, model_width)),
+            shaped((3 * model_width, channels), low),
+            shaped(up_grad.shape, low),
+            shaped(down_grad.shape, low),
+            shaped(out_grad.shape[1:], low),
+            shaped((8, model_width)),
+            shaped(filter_shape),
+            shaped(channel_shape),
+            shaped(grad_up_bias.shape),
+        ],
+        [
+            grad_first,
+            tokens[0],
+            norm1_gain[None],
+            norm1_bias[None],
+            grad_out_bias,
+            grad_norm2_gain,
+            grad_norm2_bias,
+            grad_down_bias,
+            filter_sums,
+            channel_sums,
+            grad_up_bias,
+            up_part,
+            down_part,
+            out_part,
+            first_all,
+            grad_low,
+        ],
+        ((14, 15), (1, 2, 3, 4)),
+        [
+            vmem(blocked, low),
+            vmem((length, proj_columns), low),
+            vmem((3 * model_width, channels), low),
+            vmem((3 * model_width // rows, channels), low),
+            vmem((8, model_width), single),
+            semaphores((2,)),
+            vmem((groups - 1, shard_len, model_width), low),
+            semaphores((2, groups - 1)),
+        ]
+        + row_reduce_scratch((3 * model_width, channels), chips)
+        + row_gather_scratch(chips) * 4
+        + small_sums_scratch(
+            [(8, model_width), filter_shape, channel_shape, grad_up_bias.shape], 2, chips, groups
+        ),
+        3,
+        "final",
+    )
+    (
+        layer_out,
+        grad_tokens,
+        grad_proj_weight,
+        grad_up_weight,
+        grad_down_weight,
+        grad_out_weight,
         grad_out_bias,
         grad_norm2_gain,
         grad_norm2_bias,
         grad_down_bias,
-        grad_embed_weight,
-        grad_embed_bias,
-        grad_sine_freq,
-        grad_inner_weight,
-        grad_inner_bias,
-    )
-    rows_only = (
-        grad_proj_bias,
-        grad_short_weight,
-        grad_short_bias,
-        grad_filter_weight,
-        grad_skip_gain,
-        grad_up_bias,
-    )
-
-    def pack(parts):
-        flat = jnp.concatenate([part.reshape(-1) for part in parts])
-        return jnp.pad(flat, (0, -flat.size % 1024)).reshape(-1, 128)
-
-    def unpack(packed, parts):
-        flat = packed.reshape(-1)
-        results = []
-        start = 0
-        for part in parts:
-            results.append(flat[start : start + part.size].reshape(part.shape))
-            start += part.size
-        return results
-
-    wide = pack(everywhere)
-    packed = jnp.concatenate([wide, pack(rows_only)], axis=0)
-    part_rows = proj.shape[1] // rows
-    grad_tokens, proj_grad, final_sums, packed, up_grad, down_grad, out_grad = communicate(
-        final_kernel,
-        [
-            shaped((shard_len, model_width)),
-            shaped((model_width, proj_columns), low),
-            shaped((8, model_width)),
-            shaped(packed.shape),
-            shaped(up_grad.shape, low),
-            shaped(down_grad.shape, low),
-            shaped(out_grad.shape[1:], low),
-        ],
-        [
-            grad_first,
-            first_all,
-            grad_low,
-            tokens[0],
-            norm1_gain[None],
-            grad_residual,
-            packed,
-            up_part,
-            down_part,
-            out_part,
-        ],
-        ((), ()),
-        [
-            pltpu.VMEM((model_width, proj_columns), low),
-            pltpu.VMEM((part_rows, proj_columns), low),
-            pltpu.VMEM((8, model_width), jnp.float32),
-            pltpu.VMEM((groups - 1, shard_len, model_width), low),
-            semaphores((2, groups - 1)),
-        ]
-        + row_reduce_scratch((model_width, proj_columns), chips)
-        + row_gather_scratch(chips) * 4
-        + small_sum_scratch(packed.shape, wide.shape[0], chips, groups)
-        + small_sum_scratch((8, model_width), 8, chips, groups),
-        3,
-        "final",
-    )
-    grad_tokens = grad_tokens[None]
-    grad_proj_weight = proj_grad.astype(jnp.float32).reshape(model_width, 3, channels)
-    grad_out_weight = out_grad.reshape(out_weight.shape).astype(jnp.float32)
-    grad_up_weight = up_grad.astype(jnp.float32)
-    grad_down_weight = down_grad.astype(jnp.float32)
-    layer_out = (residual + mlp_out + down_bias).astype(low)[None]
-    grad_norm1_gain, grad_norm1_bias = final_sums[:2]
-    wide, narrow = packed[: wide.shape[0]], packed[wide.shape[0] :]
-    (
-        grad_out_bias,
-        grad_norm2_gain,
-        grad_norm2_bias,
-        grad_down_bias,
-        grad_embed_weight,
-        grad_embed_bias,
-        grad_sine_freq,
-        grad_inner_weight,
-        grad_inner_bias,
-    ) = unpack(wide, everywhere)
-    (
-        grad_proj_bias,
-        grad_short_weight,
-        grad_short_bias,
-        grad_filter_weight,
-        grad_skip_gain,
-        grad_up_bias,
-    ) = unpack(narrow, rows_only)
-    return (
-        layer_out,
-        grad_tokens,
         grad_norm1_gain,
         grad_norm1_bias,
-        grad_proj_weight,
-        grad_proj_bias,
-        grad_short_weight,
-        grad_short_bias,
         grad_embed_weight,
         grad_embed_bias,
         grad_sine_freq,
         grad_inner_weight,
         grad_inner_bias,
         grad_filter_weight,
+        grad_short_weight,
+        grad_short_bias,
+        grad_proj_bias,
         grad_skip_gain,
+        grad_up_bias,
+    ) = finish(
+        [
+            residual,
+            mlp_out,
+            down_bias[None],
+            grad_tokens,
+            grad_residual,
+            proj_sum,
+            up_sum,
+            down_sum,
+            out_sum.reshape(out_weight.shape),
+            line_all,
+            filter_all,
+            channel_all,
+            up_bias_all,
+        ],
+        [
+            shaped((shard_len, model_width), low),
+            shaped((shard_len, model_width)),
+            shaped((3 * model_width, channels)),
+            shaped(up_weight.shape),
+            shaped(down_weight.shape),
+            shaped(out_weight.shape),
+            shaped(line),
+            shaped(line),
+            shaped(line),
+            shaped(line),
+            shaped(line),
+            shaped(line),
+            shaped(embed_weight.shape),
+            shaped(embed_bias.shape),
+            shaped(sine_freq.shape),
+            shaped(inner_weight.shape),
+            shaped(inner_bias.shape),
+            shaped(filter_weight.shape),
+            shaped(short_weight.shape),
+            shaped(short_bias.shape),
+            shaped(proj_bias.shape),
+            shaped(skip.shape),
+            shaped(up_bias_all.shape),
+        ],
+    )
+    grad_proj_weight = grad_proj_weight.reshape(3, model_width, channels).transpose(1, 0, 2)
+    return (
+        layer_out[None],
+        grad_tokens[None],
+        grad_norm1_gain[0],
+        grad_norm1_bias[0],
+        grad_proj_weight,
+        grad_proj_bias,
+        grad_short_weight,
+        grad_short_bias,
+        grad_embed_weight,
+        grad_embed_bias[0],
+        grad_sine_freq,
+        grad_inner_weight,
+        grad_inner_bias,
+        grad_filter_weight,
+        grad_skip_gain[0],
         grad_out_weight,
-        grad_out_bias,
-        grad_norm2_gain,
-        grad_norm2_bias,
+        grad_out_bias[0],
+        grad_norm2_gain[0],
+        grad_norm2_bias[0],
         grad_up_weight,
-        grad_up_bias,
+        grad_up_bias[0],
         grad_down_weight,
-        grad_down_bias,
+        grad_down_bias[0],
     )
 
 

time: 412 us -> 330 us (0.80)
  Pallas kernels: 345 us -> 315 us
  local copies, waits for them, and re-layouts: 35.4 us -> 8.39 us
  between operations: 14.7 us -> 1.24 us
  other arithmetic: 10.1 us -> 0 us
    pallas_call x4, Pallas kernels: 345 us -> 306 us  [communicate(): pl.pallas_call(kernel, out_shape=shapes, in_specs=[free if i in anywhere[...]
    slice x14 -> x0, local copies, waits for them, and re-layouts: 9.85 us -> none  [the longest x11 7.33 us: unpack(): results.append(flat[start:start + part.size].reshape(part.shape))]
    reshape x13 -> x0, local copies, waits for them, and re-layouts: 9.32 us -> none  [the longest x5 3.16 us: unpack(): results.append(flat[start:start + part.size].reshape(part.shape))]
    pallas_call x0 -> x1, Pallas kernels: none -> 9.15 us  [finish(): pl.pallas_call(finish_kernel, grid=(steps,), in_specs=in_specs, out_specs...]
    convert_element_type x3 -> x0, other arithmetic: 7.78 us -> none  [the longest x1 4.22 us: body(): grad_up_weight = up_grad.astype(jnp.float32)]
    unnamed x35 -> x24, local copies, waits for them, and re-layouts: 10.1 us -> 7.75 us
  transfers between devices with their start and end apart: 1 -> 0, of which waited for: 0 -> 0; matrix products, arithmetic and copies ran while one was open for 2% -> 0% of each run, Pallas kernels for 26% -> 0%
where the time goes in v3:
time: 330 us; the launch traced here: 325 us
  Pallas kernels  315 us (95%)
  local copies, waits for them, and re-layouts  8.39 us (3%)
    pallas_call x4, Pallas kernels, communicate(): pl.pallas_call(kernel, out_shape=shapes, in_specs=[free if i in anywhere[...  306 us
    pallas_call x1, Pallas kernels, finish(): pl.pallas_call(finish_kernel, grid=(steps,), in_specs=in_specs, out_specs...  9.15 us
    unnamed x24, local copies, waits for them, and re-layouts  7.75 us

profile of v3, /device:TPU:0, one launch (start us, length us, event | category | flops | bytes accessed | tf_op | source)
XLA Modules:
  0.0 324.6 jit_solution(17387437346855213656)
XLA Ops:
  0.7 0.0 copy-start
  0.7 1.0 copy-done
  1.7 0.6 constant_dynamic-slice_fusion.part
  2.3 93.5 %front.1 = (bf16[4,256,1024]{2,1,0:T(8,128)(2,1)}, bf16[4,4,2,32,1024]{4,3,2,1,0:T(8,128)(2,1)}, bf16[4,256,1024]{2,1,0:T(8,128)(2,1)}, f32[3,64,1024]{2,1,0:T(8...) custom-call(bf16[256,1024]{1,0:T(8,128)(2,1)} %bitcast.31, ...), custom_call_target="tpu_custom_call" | custom-call | bytes 200000000 | tf_op jit(solution)/shard_map/front/pallas_call | solution.py:1313
  95.8 76.5 %middle.1 = (f32[256,1024]{1,0:T(8,128)}, f32[256,1024]{1,0:T(8,128)}, bf16[4,256,1024]{2,1,0:T(8,128)(2,1)}, bf16[1024,1024]{1,0:T(8,128)(2,1)}, bf16[1024,1024...) custom-call(bf16[4,256,256]{2,1,0:T(8,128)(2,1)} %get-tuple-element., ...), custom_call_target="tpu_custom_call" | custom-call | bytes 200000000 | tf_op jit(solution)/shard_map/middle/pallas_call | solution.py:1313
  172.3 66.6 %back.1 = (bf16[4,256,1024]{2,1,0:T(8,128)(2,1)}, bf16[1024,768]{1,0:T(8,128)(2,1)}, f32[256,1024]{1,0:T(8,128)}, bf16[128,1024]{1,0:T(8,128)(2,1)}, bf16[128,10...) custom-call(bf16[4,256,256]{2,1,0:T(8,128)(2,1)} %get-tuple-element.93.grad_blocks, ...), custom_call_target="tpu_custom_call" | custom-call | bytes 200000000 | tf_op jit(solution)/shard_map/back/pallas_call | solution.py:1313
  238.9 0.0 copy-start.2
  238.9 0.0 copy-start.3
  238.9 0.0 copy-start.10
  238.9 69.3 %final.1 = (f32[256,1024]{1,0:T(8,128)}, bf16[3072,256]{1,0:T(8,128)(2,1)}, bf16[1024,1024]{1,0:T(8,128)(2,1)}, bf16[1024,1024]{1,0:T(8,128)(2,1)}, bf16[256,102...) custom-call(bf16[4,256,1024]{2,1,0:T(8,128)(2,1)} %get-tuple-element.109.gr, ...), custom_call_target="tpu_custom_call" | custom-call | bytes 200000000 | tf_op jit(solution)/shard_map/final/pallas_call | solution.py:1313
  308.2 0.0 copy-done.2
  308.2 0.0 copy-done.3
  308.2 0.0 copy-done.10
  308.2 0.0 copy-start.4
  308.2 1.2 copy-done.4
  309.5 0.0 copy-start.5
  309.5 1.2 copy-done.5
  310.7 0.0 copy-start.6
  310.7 1.0 copy-done.6
  311.7 0.0 copy-start.7
  311.7 0.9 copy-done.7
  312.6 0.0 copy-start.8
  312.6 0.9 copy-done.8
  313.5 0.0 copy-start.9
  313.5 0.8 copy-done.9
  314.3 0.0 copy-start.11
  314.3 0.7 copy-done.11
  314.9 0.0 copy-start.1
  314.9 9.2 %finish.1 = (bf16[256,1024]{1,0:T(8,128)(2,1)}, f32[256,1024]{1,0:T(8,128)}, f32[3072,256]{1,0:T(8,128)}, f32[1024,1024]{1,0:T(8,128)}, f32[1024,1024]{1,0:T(8,1...) custom-call(f32[256,1024]{1,0:T(8,128)S(1)} %copy-done.2, ...), custom_call_target="tpu_custom_call" | custom-call | tf_op jit(solution)/shard_map/finish/pallas_call | solution.py:1297
  324.1 0.0 copy-done.1
Async XLA Ops:
  0.7 1.1 copy-start
  238.9 69.3 %copy-start.2 = (f32[256,1024]{1,0:T(8,128)S(1)}, f32[256,1024]{1,0:T(8,128)}, u32[]{:S(2)}) copy-start(f32[256,1024]{1,0:T(8,128)} %get-tuple-element.92.residual) | copy-start | bytes 3145732
  238.9 69.3 %copy-start.3 = (f32[256,1024]{1,0:T(8,128)S(1)}, f32[256,1024]{1,0:T(8,128)}, u32[]{:S(2)}) copy-start(f32[256,1024]{1,0:T(8,128)} %get-tuple-element.123.grad_residual) | copy-start | bytes 3145732
  238.9 69.3 %copy-start.10 = (f32[1024]{0:T(1024)S(1)}, f32[1024]{0:T(1024)}, u32[]{:S(2)}) copy-start(f32[1024]{0:T(1024)} %param.53) | copy-start | bytes 12292
  308.2 1.2 copy-start.4
  309.5 1.2 copy-start.5
  310.7 1.0 copy-start.6
  311.7 0.9 copy-start.7
  312.6 0.9 copy-start.8
  313.5 0.8 copy-start.9
  314.3 0.7 copy-start.11
  314.9 9.2 %copy-start.1 = (bf16[256,1024]{1,0:T(8,128)(2,1)S(1)}, bf16[256,1024]{1,0:T(8,128)(2,1)}, u32[]{:S(2)}) copy-start(bf16[256,1024]{1,0:T(8,128)(2,1)} %param.46) | copy-start | bytes 1572868

commit v4 on v3

--- a/solution.py
+++ b/solution.py
@@ -196,16 +196,18 @@
         if i == 2:
             channel_sums[:width] = exact(jnp.sin(angle), raw, ((1,), (0,)))
         act = back * jnp.cos(angle)
-        filter_sums[rows.freq + i : rows.freq + i + 1] = exact(ones, act * pre[i], ((1,), (1,)))[0:1]
+        filter_sums[rows.freq + i : rows.freq + i + 1, :width] = exact(ones, act * pre[i], ((1,), (1,)))[0:1]
         step = act * rates[i]
         bias = exact(ones, step, ((1,), (1,)))[0:1]
         if i == 0:
-            filter_sums[rows.embed_bias : rows.embed_bias + 1] = bias
-            filter_sums[rows.embed : rows.embed + FEAT] = exact(features[...], step, ((1,), (1,)))
+            filter_sums[rows.embed_bias : rows.embed_bias + 1, :width] = bias
+            filter_sums[rows.embed : rows.embed + FEAT, :width] = exact(
+                features[...], step, ((1,), (1,))
+            )
         else:
-            filter_sums[rows.inner_bias + i - 1 : rows.inner_bias + i] = bias
+            filter_sums[rows.inner_bias + i - 1 : rows.inner_bias + i, :width] = bias
             below = jnp.sin(rates[i - 1] * pre[i - 1])
-            filter_sums[(i - 1) * width : i * width] = exact(below, step, ((1,), (1,)))
+            filter_sums[:width, (i - 1) * width : i * width] = exact(below, step, ((1,), (1,)))
             back = exact(inner[i - 1], step, ((1,), (0,)))
 
 
@@ -327,50 +329,52 @@
         self.slots, self.send_sems, self.recv_sems = slots, send_sems, recv_sems
         self.count = lax.axis_size("tensor")
         self.me = lax.axis_index("tensor")
-
-    def copy(self, block, side):
+        self.rows = slots.shape[1] // 2
+
+    def copy(self, block, half, side):
         step = 1 - 2 * side
+        piece = self.slots.at[block, pl.ds(half * self.rows, self.rows)]
         return remote(
-            self.slots.at[block],
-            self.slots.at[block],
-            self.send_sems.at[side, block],
-            self.recv_sems.at[block],
+            piece,
+            piece,
+            self.send_sems.at[side, half, block],
+            self.recv_sems.at[half, block],
             {"tensor": lax.rem(self.me + step + self.count, self.count)},
         )
 
-    def advance(self, step):
-        lower, upper = self.me - step, self.me + step
-
-        @pl.when(lower >= 0)
+    def pass_on(self, step, half, side):
+        block = self.me - step * (1 - 2 * side)
+
+        @pl.when((block >= 0) & (block < self.count))
         def _():
             @pl.when(step > 0)
             def _():
-                self.copy(lower, 0).wait_recv()
-
-            @pl.when(self.me < self.count - 1)
+                self.copy(block, half, side).wait_recv()
+
+            @pl.when((self.me < self.count - 1) if side == 0 else (self.me > 0))
             def _():
-                self.copy(lower, 0).start()
-
-        @pl.when(upper < self.count)
-        def _():
-            @pl.when(step > 0)
-            def _():
-                self.copy(upper, 1).wait_recv()
-
-            @pl.when(self.me > 0)
-            def _():
-                self.copy(upper, 1).start()
+                self.copy(block, half, side).start()
+
+    def advance(self, step):
+        for half in range(2):
+            for side in range(2):
+                self.pass_on(step, half, side)
 
     def finish(self):
         for block in range(self.count):
-
-            @pl.when((self.me < self.count - 1) & (block <= self.me))
-            def _():
-                self.copy(block, 0).wait_send()
-
-            @pl.when((self.me > 0) & (block >= self.me))
-            def _():
-                self.copy(block, 1).wait_send()
+            for half in range(2):
+
+                @pl.when((self.me < self.count - 1) & (block <= self.me))
+                def _():
+                    self.copy(block, half, 0).wait_send()
+
+                @pl.when((self.me > 0) & (block >= self.me))
+                def _():
+                    self.copy(block, half, 1).wait_send()
+
+
+def chain_scratch(count):
+    return [pltpu.SemaphoreType.DMA((2, 2, count)), pltpu.SemaphoreType.DMA((2, count))]
 
 
 def normalised(values):
@@ -418,6 +422,9 @@
     sin_main_hbm,
     cos_small,
     sin_small,
+    out_bias,
+    second_gain,
+    second_shift,
     first_out,
     part_all,
     cotangent_out,
@@ -432,6 +439,9 @@
     projected_out,
     mixed_out,
     summed_out,
+    out,
+    residual,
+    second,
     features,
     proj,
     cos_main,
@@ -445,6 +455,7 @@
     mixed,
     summed,
     gated,
+    held_parts,
     marks,
     load_sems,
     store_sems,
@@ -564,27 +575,43 @@
     more = store_sems.at[pl.ds(len(stores) + 3, 2)]
     stored += staged([(summed, summed_out)], more)
     gated_own[me] = gated[me]
-    for step in range(1, count):
+    wait_all(parts)
+    load = pltpu.make_async_copy(part_all, held_parts, local_sems.at[0])
+    load.start()
+    later.advance(1)
+    load.wait()
+    wait_all(swapped)
+    size = channels // (held_parts.shape[1] * 2)
+    base = tokens[...].astype(jnp.float32) + out_bias[...]
+    for block in range(count):
+        if held_parts.shape[3] == size:
+            out[block] = held_parts[block].reshape(out.shape[1:])
+        else:
+            wide = held_parts[block].astype(jnp.float32)[:, :, :size]
+            out[block] = wide.reshape(out.shape[1:]).astype(out.dtype)
+        base = base + dot_nn(gated_own[block], out[block])
+    residual[...] = base
+    hat, unused_rate = normalised(base)
+    second[...] = (hat * second_gain[...] + second_shift[...]).astype(jnp.bfloat16)
+    for step in range(2, count):
         later.advance(step)
     more = store_sems.at[pl.ds(len(stores) + 4, 1)]
     stored += staged([(cotangent_all, cotangent_out)], more)
     chain.finish()
     later.finish()
-    wait_all(parts + swapped + stored)
+    wait_all(stored)
 
 
 def middle_kernel(
-    gated,
-    out,
-    tokens,
-    out_bias,
+    second_own,
     gain,
-    shift,
+    bias,
     cotangent_hbm,
     up_hbm,
-    bias,
     down_hbm,
-    residual_out,
+    residual_hbm,
+    gated_hbm,
+    out_hbm,
     grad_residual,
     mlp_out,
     up_out,
@@ -600,6 +627,8 @@
     up,
     down,
     residual,
+    gated,
+    out,
     mlp,
     up_grad,
     down_grad,
@@ -618,16 +647,21 @@
 ):
     me = lax.axis_index("tensor")
     count = lax.axis_size("tensor")
-    shard, width = tokens.shape
+    shard, width = second_own.shape
     units = up.shape[1]
-    loads = staged([(up_hbm, up), (down_hbm, down), (cotangent_hbm, cotangent)], load_sems)
+    loads = staged(
+        [
+            (up_hbm, up),
+            (down_hbm, down),
+            (cotangent_hbm, cotangent),
+            (residual_hbm, residual),
+            (gated_hbm, gated),
+            (out_hbm, out),
+        ],
+        load_sems,
+    )
     greet(tensor_devices())
-    base = tokens[...].astype(jnp.float32) + out_bias[...]
-    for block in range(count):
-        base = base + dot_nn(gated[block], out[block])
-    residual[...] = base
-    hat, unused_rate = normalised(base)
-    second[me] = (hat * gain[...] + shift[...]).astype(jnp.bfloat16)
+    second[me] = second_own[...]
     chain = Chain(second, second_send, second_recv)
     bias_grad[...] = jnp.zeros_like(bias_grad)
 
@@ -670,7 +704,7 @@
 
         @pl.when(step == 0)
         def _():
-            wait_all(loads)
+            wait_all(loads[:3])
 
         def side(index, carry):
             block = me + step * (2 * index - 1)
@@ -684,7 +718,7 @@
         return lax.fori_loop(0, 2, side, carry)
 
     lax.fori_loop(0, count, turn, 0)
-    stored = staged([(residual, residual_out), (mlp, mlp_out)], store_sems)
+    stored = staged([(mlp, mlp_out)], store_sems)
     tokens_all = count * shard
     up_grad[...] = dot_tn(
         second[...].reshape(tokens_all, width), low[...].reshape(tokens_all, units)
@@ -692,7 +726,8 @@
     down_grad[...] = dot_tn(
         active[...].reshape(tokens_all, units), cotangent[...].reshape(tokens_all, width)
     ).astype(jnp.bfloat16)
-    stored += staged([(up_grad, up_out), (down_grad, down_out)], store_sems.at[pl.ds(2, 2)])
+    stored += staged([(up_grad, up_out), (down_grad, down_out)], store_sems.at[pl.ds(1, 2)])
+    wait_all(loads[3:])
     for peer in tensor_peers():
         remote(
             parting.at[peer],
@@ -914,8 +949,7 @@
 
 class filter_rows:
     def __init__(self, width):
-        self.inner = 0
-        self.embed = 2 * width
+        self.embed = width
         self.embed_bias = self.embed + FEAT + -FEAT % 8
         self.freq = self.embed_bias + 1
         self.inner_bias = self.embed_bias + 4
@@ -955,7 +989,7 @@
     grad_first,
     grad_low,
     mlp_sum,
-    up_part,
+    up_sum,
     down_part,
     out_part,
     filter_sums,
@@ -975,6 +1009,7 @@
     marks,
     mlp_own,
     mlp_recv,
+    up_part,
     load_sems,
     local_sems,
     gated_sems,
@@ -1008,7 +1043,8 @@
     up_row = RowReduce(up_grad, up_part, scratch[:6])
     down_row = RowReduce(down_grad, down_part, scratch[6:12])
     out_row = RowReduce(out_grad, out_part, scratch[12:21])
-    weights = (out_row, up_row, down_row)
+    weights = (up_row, down_row, out_row)
+    up_all = RowGather(up_part, up_sum, scratch[21:24])
     places = channel_rows(filter_weight.shape[0])
     filter_sums[...] = jnp.zeros_like(filter_sums)
     own = pltpu.make_async_copy(grad_blocks.at[me], grad_gated.at[me], local_sems.at[0])
@@ -1028,8 +1064,8 @@
     product = values * gate_in
     low = product.astype(jnp.bfloat16).astype(jnp.float32)
     value_main, value_small = spectra(low, marks, *transforms)
-    for weight in weights:
-        weight.plane()
+    up_row.plane()
+    out_row.plane()
     own.wait()
     wait_all(arriving)
     mlps = spread(
@@ -1051,6 +1087,7 @@
     taps_small = from_bins((real * scale, imag * scale, top * (0.5 / region)), cos_small, sin_small)
     grad_taps[:region] = taps[:region] + taps_small
     grad_taps[region:] = taps[region:]
+    down_row.plane()
     wait_all(loads[3:])
     result = filtered(
         grad_main,
@@ -1086,6 +1123,8 @@
         for k in (1, 2):
             total = total + dot_nt(grad_low[rows, k * channels : (k + 1) * channels], proj[k])
         grad_first[block] = total.astype(jnp.bfloat16)
+    up_row.finish()
+    up_all.plane()
     filter_back(
         grad_taps,
         features,
@@ -1098,7 +1137,8 @@
         filter_sums,
         channel_sums,
     )
-    for weight in weights:
+    up_all.pair()
+    for weight in (down_row, out_row):
         weight.finish()
     own_mlp.wait()
     total = mlp_own[...].astype(jnp.float32)
@@ -1106,6 +1146,7 @@
         copy.wait()
         total = total + mlp_recv[k].astype(jnp.float32)
     mlp_sum[...] = total
+    up_all.finish()
 
 
 def final_kernel(
@@ -1120,14 +1161,12 @@
     filter_sums,
     channel_sums,
     up_bias_sum,
-    up_part,
     down_part,
     out_part,
     first_hbm,
     grad_low_hbm,
     grad_tokens,
     proj_sum,
-    up_sum,
     down_sum,
     out_sum,
     line_all,
@@ -1155,15 +1194,14 @@
     row = RowReduce(proj_grad, proj_part, scratch[:6])
     proj_all = RowGather(proj_part, proj_sum, scratch[6:9])
     gathers = (
-        RowGather(up_part, up_sum, scratch[9:12]),
-        RowGather(down_part, down_sum, scratch[12:15]),
-        RowGather(out_part, out_sum, scratch[15:18]),
+        RowGather(down_part, down_sum, scratch[9:12]),
+        RowGather(out_part, out_sum, scratch[12:15]),
     )
     small = SmallSums(
         (lines, filter_sums, channel_sums, up_bias_sum),
         (line_all, filter_all, channel_all, up_bias_all),
         2,
-        scratch[18:],
+        scratch[15:],
     )
     length, columns = grad_low.shape
     channels = columns // 3
@@ -1174,6 +1212,7 @@
             first[...].reshape(length, width), grad_low[:, k * channels : (k + 1) * channels]
         ).astype(jnp.bfloat16)
     row.pair()
+    row.plane()
     plain = jnp.zeros_like(gain[...])
     scaled = jnp.zeros_like(gain[...])
     for block in range(count):
@@ -1188,17 +1227,16 @@
     lines[5:6] = plain
     lines[6:8] = jnp.zeros_like(lines[6:8])
     small.pair()
-    row.plane()
+    hat, rate = normalised(tokens[...].astype(jnp.float32))
+    small.plane()
+    row.finish()
+    proj_all.plane()
     for gather in gathers:
         gather.plane()
-    small.plane()
-    hat, rate = normalised(tokens[...].astype(jnp.float32))
-    row.finish()
-    proj_all.plane()
     small.tensor()
+    proj_all.pair()
     for gather in gathers:
         gather.pair()
-    proj_all.pair()
     small.finish()
     grad = grad_first[me].astype(jnp.float32)
     for k, copy in enumerate(blocks):
@@ -1265,11 +1303,11 @@
         width = filter_out.shape[0]
         rows = filter_rows(width)
         for i in range(2):
-            inner_out[i] = filter_all[i * width : (i + 1) * width]
-        embed_out[...] = filter_all[rows.embed : rows.embed + FEAT]
-        embed_bias_out[...] = filter_all[rows.embed_bias : rows.embed_bias + 1]
-        freq_out[...] = filter_all[rows.freq : rows.freq + 3]
-        inner_bias_out[...] = filter_all[rows.inner_bias : rows.inner_bias + 2]
+            inner_out[i] = filter_all[:width, i * width : (i + 1) * width]
+        embed_out[...] = filter_all[rows.embed : rows.embed + FEAT, :width]
+        embed_bias_out[...] = filter_all[rows.embed_bias : rows.embed_bias + 1, :width]
+        freq_out[...] = filter_all[rows.freq : rows.freq + 3, :width]
+        inner_bias_out[...] = filter_all[rows.inner_bias : rows.inner_bias + 2, :width]
         rows = channel_rows(width)
         filter_out[...] = channel_all[:width]
         for lag in range(3):
@@ -1282,7 +1320,7 @@
 
 
 def finish(big, shapes):
-    steps = 8
+    steps = 4
 
     def rows(shape):
         return pl.BlockSpec((shape[0] // steps, shape[1]), lambda i: (i, 0))
@@ -1301,7 +1339,7 @@
         out_specs=out_specs,
         out_shape=shapes,
         compiler_params=pltpu.CompilerParams(
-            dimension_semantics=("arbitrary",), vmem_limit_bytes=48 * 1024 * 1024
+            dimension_semantics=("arbitrary",), vmem_limit_bytes=60 * 1024 * 1024
         ),
         name="finish",
     )(*big)
@@ -1385,7 +1423,7 @@
     line = (1, model_width)
     (
         first_all,
-        out_all,
+        unused_parts,
         all_cotangent,
         pre,
         main_re,
@@ -1398,6 +1436,9 @@
         projected,
         mixed,
         summed,
+        out_all,
+        residual,
+        second,
     ) = communicate(
         front_kernel,
         [
@@ -1415,6 +1456,9 @@
             shaped((length, proj_columns)),
             shaped((length, proj_columns)),
             shaped((length, channels)),
+            shaped((groups, channels, model_width), low),
+            shaped((shard_len, model_width)),
+            shaped((shard_len, model_width), low),
         ],
         [
             tokens[0],
@@ -1440,6 +1484,9 @@
             sin_main,
             cos_small,
             sin_small,
+            out_bias[None],
+            norm2_gain[None],
+            norm2_bias[None],
         ],
         ((3, 17, 18, 19, 20), (0, 1, 2, 3, 4, 5, 11, 12, 13)),
         [
@@ -1456,14 +1503,13 @@
             vmem((length, proj_columns), single),
             vmem((length, channels), single),
             vmem(swapped, low),
+            vmem((groups, chips, 2) + out_part.shape, low),
             vmem((length, 8), jnp.int32),
             semaphores((4,)),
             semaphores((8,)),
             semaphores((1,)),
-            semaphores((2, groups)),
-            semaphores((groups,)),
-            semaphores((2, groups)),
-            semaphores((groups,)),
+            *chain_scratch(groups),
+            *chain_scratch(groups),
             semaphores((2, groups - 1)),
             semaphores((2, chips - 1)),
             semaphores((2, 1)),
@@ -1472,9 +1518,7 @@
         0,
         "front",
     )
-    out_all = out_all[..., :channel_slice, :].reshape(groups, channels, model_width)
     (
-        residual,
         grad_residual,
         mlp_partial,
         up_grad,
@@ -1490,7 +1534,6 @@
         middle_kernel,
         [
             shaped((shard_len, model_width)),
-            shaped((shard_len, model_width)),
             shaped(blocked, low),
             shaped((model_width, units), low),
             shaped((units, model_width), low),
@@ -1503,23 +1546,24 @@
             shaped(line),
         ],
         [
+            second,
+            norm2_gain[None],
+            up_bias[None],
+            all_cotangent,
+            up_weight,
+            down_weight,
+            residual,
             gated_own,
             out_all,
-            tokens[0],
-            out_bias[None],
-            norm2_gain[None],
-            norm2_bias[None],
-            all_cotangent,
-            up_weight,
-            up_bias[None],
-            down_weight,
         ],
-        ((6, 7, 9), (0, 2, 3, 4)),
+        ((3, 4, 5, 6, 7, 8), (1, 2, 3)),
         [
             vmem(blocked, low),
             vmem((model_width, units), low),
             vmem((units, model_width), low),
             vmem((shard_len, model_width), single),
+            vmem(swapped, low),
+            vmem((groups, channels, model_width), low),
             vmem(blocked, low),
             vmem((model_width, units), low),
             vmem((units, model_width), low),
@@ -1529,10 +1573,9 @@
             vmem(blocked, low),
             vmem(blocked, low),
             vmem((shard_len, model_width), single),
+            semaphores((6,)),
             semaphores((3,)),
-            semaphores((4,)),
-            semaphores((2, groups)),
-            semaphores((groups,)),
+            *chain_scratch(groups),
             semaphores((groups,)),
             semaphores((groups,)),
         ],
@@ -1542,13 +1585,13 @@
     fold = max(1, 32 * chips // channels)
     out_grad = out_grad.reshape(groups, channels * fold, model_width // fold)
     out_size = (channels * fold // rows, model_width // fold)
-    filter_shape = (filter_rows(width).size, width)
+    filter_shape = (filter_rows(width).size, 2 * width)
     channel_shape = (channel_rows(width).size, channels)
     (
         grad_first,
         grad_low,
         mlp_out,
-        up_part,
+        up_sum,
         down_part,
         out_part,
         filter_sums,
@@ -1559,7 +1602,7 @@
             shaped(blocked, low),
             shaped((length, proj_columns), low),
             shaped((shard_len, model_width)),
-            shaped((model_width // rows, units), low),
+            shaped(up_grad.shape, low),
             shaped((units // rows, model_width), low),
             shaped(out_size, low),
             shaped(filter_shape),
@@ -1596,7 +1639,7 @@
             features,
             pre,
         ],
-        ((0, 1, 2, 3, 4, 19, 20, 21, 22, 23, 24, 25, 26, 27, 28), ()),
+        ((0, 1, 2, 3, 4, 19, 20, 21, 22, 23, 24, 25, 26, 27, 28), (3,)),
         [
             vmem((length, proj_columns), single),
             vmem(cos_main.shape, low),
@@ -1613,6 +1656,7 @@
             vmem((length, 8), jnp.int32),
             vmem((shard_len, model_width), low),
             vmem((groups - 1, shard_len, model_width), low),
+            vmem((model_width // rows, units), low),
             semaphores((10,)),
             semaphores((2,)),
             semaphores((2, groups - 1)),
@@ -1620,14 +1664,14 @@
         ]
         + row_reduce_scratch(up_grad.shape, chips)
         + row_reduce_scratch(down_grad.shape, chips)
-        + row_reduce_scratch(out_grad.shape, chips),
+        + row_reduce_scratch(out_grad.shape, chips)
+        + row_gather_scratch(chips),
         2,
         "back",
     )
     (
         grad_tokens,
         proj_sum,
-        up_sum,
         down_sum,
         out_sum,
         line_all,
@@ -1639,7 +1683,6 @@
         [
             shaped((shard_len, model_width)),
             shaped((3 * model_width, channels), low),
-            shaped(up_grad.shape, low),
             shaped(down_grad.shape, low),
             shaped(out_grad.shape[1:], low),
             shaped((8, model_width)),
@@ -1659,13 +1702,12 @@
             filter_sums,
             channel_sums,
             grad_up_bias,
-            up_part,
             down_part,
             out_part,
             first_all,
             grad_low,
         ],
-        ((14, 15), (1, 2, 3, 4)),
+        ((13, 14), (1, 2, 3)),
         [
             vmem(blocked, low),
             vmem((length, proj_columns), low),
@@ -1677,7 +1719,7 @@
             semaphores((2, groups - 1)),
         ]
         + row_reduce_scratch((3 * model_width, channels), chips)
-        + row_gather_scratch(chips) * 4
+        + row_gather_scratch(chips) * 3
         + small_sums_scratch(
             [(8, model_width), filter_shape, channel_shape, grad_up_bias.shape], 2, chips, groups
         ),

time: 330 us -> 313 us (0.948)
  Pallas kernels: 315 us -> 305 us
  local copies, waits for them, and re-layouts: 8.39 us -> 1.68 us
    pallas_call x4, Pallas kernels: 306 us -> 295 us  [communicate(): pl.pallas_call(kernel, out_shape=shapes, in_specs=[free if i in anywhere[...]
    unnamed x24 -> x4, local copies, waits for them, and re-layouts: 7.75 us -> 1.04 us
where the time goes in v4:
time: 313 us; the launch traced here: 307 us
  Pallas kernels  305 us (97%)
    pallas_call x4, Pallas kernels, communicate(): pl.pallas_call(kernel, out_shape=shapes, in_specs=[free if i in anywhere[...  295 us
    pallas_call x1, Pallas kernels, finish(): pl.pallas_call(finish_kernel, grid=(steps,), in_specs=in_specs, out_specs...  9.88 us

profile of v4, /device:TPU:0, one launch (start us, length us, event | category | flops | bytes accessed | tf_op | source)
XLA Modules:
  0.0 307.5 jit_solution(5495416583315840369)
XLA Ops:
  0.7 0.0 copy-start
  0.7 1.0 copy-done
  1.7 0.6 constant_dynamic-slice_fusion.part
  2.3 92.2 %front.1 = (bf16[4,256,1024]{2,1,0:T(8,128)(2,1)}, bf16[4,4,2,32,1024]{4,3,2,1,0:T(8,128)(2,1)}, bf16[4,256,1024]{2,1,0:T(8,128)(2,1)}, f32[3,64,1024]{2,1,0:T(8...) custom-call(bf16[256,1024]{1,0:T(8,128)(2,1)} %bitcast.29, ...), custom_call_target="tpu_custom_call" | custom-call | bytes 200000000 | tf_op jit(solution)/shard_map/front/pallas_call | solution.py:1351
  94.5 75.4 %middle.1 = (f32[256,1024]{1,0:T(8,128)}, bf16[4,256,1024]{2,1,0:T(8,128)(2,1)}, bf16[1024,1024]{1,0:T(8,128)(2,1)}, bf16[1024,1024]{1,0:T(8,128)(2,1)}, f32[1,1...) custom-call(bf16[256,1024]{1,0:T(8,128)(2,1)} %get-tuple-element.90., ...), custom_call_target="tpu_custom_call" | custom-call | bytes 200000000 | tf_op jit(solution)/shard_map/middle/pallas_call | solution.py:1351
  169.9 67.7 %back.1 = (bf16[4,256,1024]{2,1,0:T(8,128)(2,1)}, bf16[1024,768]{1,0:T(8,128)(2,1)}, f32[256,1024]{1,0:T(8,128)}, bf16[1024,1024]{1,0:T(8,128)(2,1)}, bf16[128,1...) custom-call(bf16[4,256,256]{2,1,0:T(8,128)(2,1)} %get-tuple-element.94.grad_blocks, ...), custom_call_target="tpu_custom_call" | custom-call | bytes 200000000 | tf_op jit(solution)/shard_map/back/pallas_call | solution.py:1351
  237.6 59.5 %final.1 = (f32[256,1024]{1,0:T(8,128)}, bf16[3072,256]{1,0:T(8,128)(2,1)}, bf16[1024,1024]{1,0:T(8,128)(2,1)}, bf16[256,1024]{1,0:T(8,128)(2,1)}, f32[8,1024]{1...) custom-call(bf16[4,256,1024]{2,1,0:T(8,128)(2,1)} %get-tuple-element.110.grad_first, ...), custom_call_target="tpu_custom_call" | custom-call | bytes 200000000 | tf_op jit(solution)/shard_map/final/pallas_call | solution.py:1351
  297.1 0.0 copy-start.1
  297.1 9.9 %finish.1 = (bf16[256,1024]{1,0:T(8,128)(2,1)}, f32[256,1024]{1,0:T(8,128)}, f32[3072,256]{1,0:T(8,128)}, f32[1024,1024]{1,0:T(8,128)}, f32[1024,1024]{1,0:T(8,1...) custom-call(f32[256,1024]{1,0:T(8,128)} %get-tuple-element.89.residu, ...), custom_call_target="tpu_custom_call" | custom-call | tf_op jit(solution)/shard_map/finish/pallas_call | solution.py:1335
  307.0 0.0 copy-done.1
Async XLA Ops:
  0.7 1.1 copy-start
  297.1 9.9 %copy-start.1 = (bf16[256,1024]{1,0:T(8,128)(2,1)S(1)}, bf16[256,1024]{1,0:T(8,128)(2,1)}, u32[]{:S(2)}) copy-start(bf16[256,1024]{1,0:T(8,128)(2,1)} %param.46) | copy-start | bytes 1572868

commit v5 on v4

--- a/solution.py
+++ b/solution.py
@@ -13,6 +13,7 @@
 FEAT = 33
 SEQ = 1024
 NDOC = 8
+SLOTS = NDOC - 1
 
 
 EPS = 1e-05
@@ -118,7 +119,7 @@
     head_slot, tail_slot = marks[:region, 3:4], marks[length - region :, 4:5]
     pieces = [
         jnp.where(head_slot == d, head, 0.0) + jnp.where(tail_slot == d, tail, 0.0)
-        for d in range(NDOC)
+        for d in range(SLOTS)
     ]
     small = jnp.concatenate(pieces, axis=1)
     top = jnp.sum(small * signs(region), axis=0, keepdims=True)
@@ -153,7 +154,7 @@
 
 
 def beside(part):
-    return jnp.concatenate([part] * NDOC, axis=1)
+    return jnp.concatenate([part] * SLOTS, axis=1)
 
 
 def filtered(main_bins, small_bins, taps_main, taps_small, marks, transforms, conjugate):
@@ -166,7 +167,7 @@
     main = jnp.where(marks[:, 0:1] > 0, main, 0.0)
     head, tail = main[:region], main[length - region :]
     head_slot, tail_slot = marks[:region, 3:4], marks[length - region :, 4:5]
-    for d in range(NDOC):
+    for d in range(SLOTS):
         piece = small[:, d * channels : (d + 1) * channels]
         head = head + jnp.where(head_slot == d, piece, 0.0)
         tail = tail + jnp.where(tail_slot == d, piece, 0.0)
@@ -225,7 +226,7 @@
         same = (ids == pltpu.roll(ids, lag, 0)) & (places >= lag)
         marks[:, lag : lag + 1] = same.astype(jnp.int32)
     marks[:, 3:4] = jnp.where(inside | (places >= region), -1, ids)
-    marks[:, 4:5] = jnp.where(inside | (places < length - region), -1, ids)
+    marks[:, 4:5] = jnp.where(inside | (places < length - region), -1, ids - 1)
 
 
 BY_INDEX = pl.DeviceIdType.MESH
@@ -490,12 +491,12 @@
     )
     greet(tensor_devices() + [sibling()] + chip_devices())
 
+    cotangent_all[me] = cotangent[...]
+    later = Chain(cotangent_all, cotangent_send, cotangent_recv)
     hat, unused_rate = normalised(tokens[...].astype(jnp.float32))
     first_all[me] = (hat * gain[...] + shift[...]).astype(jnp.bfloat16)
     chain = Chain(first_all, first_send, first_recv)
     chain.advance(0)
-    cotangent_all[me] = cotangent[...]
-    later = Chain(cotangent_all, cotangent_send, cotangent_recv)
     own = pltpu.make_async_copy(part, part_all.at[me, chip, core], local_sems.at[0])
     own.start()
     parts = spread(part, part_all.at[me, chip, core], part_sems, tensor_devices())
@@ -513,7 +514,6 @@
     make_taps(
         features, embed, inner, columns, biases, filter_weight, decay, transforms, pre, taps_bins
     )
-    row_marks(segment, marks, cos_small.shape[0])
     stores = [(pre, pre_out), (main_re, main_re_out), (main_im, main_im_out)]
     stored = staged(stores, store_sems)
 
@@ -538,6 +538,7 @@
     parts = spread(held, held, chip_sems, chip_devices())
     lax.fori_loop(2, count, turn, 0)
     later.advance(0)
+    row_marks(segment, marks, cos_small.shape[0])
     more = store_sems.at[pl.ds(len(stores), 5)]
     stored += staged([(first_all, first_out), (projected, projected_out)], more)
     wait_all(parts)
@@ -557,6 +558,7 @@
     stored += staged([(mixed, mixed_out)], more)
     low = product.astype(jnp.bfloat16).astype(jnp.float32)
     main_bins, small_bins = spectra(low, marks, *transforms)
+    later.advance(1)
     result = filtered(
         main_bins,
         small_bins,
@@ -572,13 +574,13 @@
     swapped = spread(
         lambda k: gated.at[peers[k]], gated_own.at[me], gated_sems, tensor_devices()
     )
+    later.advance(2)
     more = store_sems.at[pl.ds(len(stores) + 3, 2)]
     stored += staged([(summed, summed_out)], more)
     gated_own[me] = gated[me]
     wait_all(parts)
     load = pltpu.make_async_copy(part_all, held_parts, local_sems.at[0])
     load.start()
-    later.advance(1)
     load.wait()
     wait_all(swapped)
     size = channels // (held_parts.shape[1] * 2)
@@ -593,7 +595,7 @@
     residual[...] = base
     hat, unused_rate = normalised(base)
     second[...] = (hat * second_gain[...] + second_shift[...]).astype(jnp.bfloat16)
-    for step in range(2, count):
+    for step in range(3, count):
         later.advance(step)
     more = store_sems.at[pl.ds(len(stores) + 4, 1)]
     stored += staged([(cotangent_all, cotangent_out)], more)
@@ -877,6 +879,115 @@
     ]
 
 
+class Scatter:
+    def __init__(self, blocks, refs):
+        self.blocks = blocks
+        self.relayed, self.arrived = refs[:2]
+        self.send_sems, self.recv_sems, self.relay_sems = refs[2:]
+        self.me = lax.axis_index("tensor")
+        self.count = lax.axis_size("tensor")
+
+    def far(self, block):
+        distance = jnp.abs(block - self.me)
+        return (distance > 2) & (lax.rem(distance, 2) == 1)
+
+    def joined(self, block):
+        distance = jnp.abs(block - self.me)
+        outer = self.me + jnp.where(block > self.me, -1, 1)
+        inside = (outer >= 0) & (outer < self.count)
+        return (distance > 1) & (lax.rem(distance, 2) == 0) & inside
+
+    def plain(self, block):
+        return jnp.logical_not(self.far(block) | self.joined(block))
+
+    def by_neighbour(self, block):
+        step = jnp.where(block > self.me, 1, -1)
+        return remote(
+            self.blocks.at[block],
+            self.relayed.at[lax.div(block, 2)],
+            self.send_sems.at[block],
+            self.relay_sems.at[block],
+            {"tensor": lax.rem(self.me + step + self.count, self.count)},
+        )
+
+    def direct(self, block, source):
+        return remote(
+            source,
+            self.arrived.at[lax.rem(self.me - block + self.count, self.count) - 1],
+            self.send_sems.at[block],
+            self.recv_sems.at[self.me],
+            {"tensor": block},
+        )
+
+    def start(self):
+        any_far = (self.me >= 3) | (self.me + 3 < self.count)
+        for peer in tensor_peers():
+
+            @pl.when(self.far(peer))
+            def _():
+                self.by_neighbour(peer).start()
+
+        for peer in tensor_peers():
+
+            @pl.when(self.plain(peer) & jnp.logical_not(any_far))
+            def _():
+                self.direct(peer, self.blocks.at[peer]).start()
+
+    def follow(self):
+        any_far = (self.me >= 3) | (self.me + 3 < self.count)
+        for peer in tensor_peers():
+
+            @pl.when(self.far(peer))
+            def _():
+                self.by_neighbour(peer).wait_send()
+
+        for peer in tensor_peers():
+
+            @pl.when(self.plain(peer) & any_far)
+            def _():
+                self.direct(peer, self.blocks.at[peer]).start()
+
+        for peer in tensor_peers():
+
+            @pl.when(self.joined(peer))
+            def _():
+                self.by_neighbour(peer).wait_recv()
+                held = self.relayed.at[lax.div(peer, 2)]
+                held[...] = (
+                    self.blocks[peer].astype(jnp.float32) + held[...].astype(jnp.float32)
+                ).astype(held.dtype)
+                self.direct(peer, held).start()
+
+    def finish(self, total):
+        total[...] = self.blocks[self.me].astype(jnp.float32)
+        for k, peer in enumerate(tensor_peers()):
+
+            @pl.when(self.joined(peer))
+            def _():
+                self.direct(peer, self.relayed.at[lax.div(peer, 2)]).wait_send()
+
+            @pl.when(self.plain(peer))
+            def _():
+                self.direct(peer, self.blocks.at[peer]).wait_send()
+
+            @pl.when(jnp.logical_not(self.far(peer)))
+            def _():
+                remote(
+                    self.blocks.at[peer],
+                    self.arrived.at[k],
+                    self.send_sems.at[peer],
+                    self.recv_sems.at[peer],
+                    {"tensor": peer},
+                ).wait_recv()
+                total[...] += self.arrived[k].astype(jnp.float32)
+
+
+def scatter_scratch(shape):
+    half = (shape[0] // 2,) + tuple(shape[1:])
+    rest = (shape[0] - 1,) + tuple(shape[1:])
+    return [pltpu.VMEM(half, jnp.bfloat16), pltpu.VMEM(rest, jnp.bfloat16)] + [pltpu.SemaphoreType.DMA((shape[0],))] * 3
+
+
 class SmallSums:
     def __init__(self, sources, results, wide, refs):
         self.sources, self.results, self.wide = sources, results, wide
@@ -958,7 +1069,7 @@
 
 def back_kernel(
     grad_blocks,
-    mlp,
+    mlp_hbm,
     up_grad,
     down_grad,
     out_grad,
@@ -1007,13 +1118,11 @@
     grad_gated,
     grad_taps,
     marks,
-    mlp_own,
-    mlp_recv,
+    mlp,
     up_part,
     load_sems,
     local_sems,
     gated_sems,
-    mlp_sems,
     *scratch,
 ):
     me = lax.axis_index("tensor")
@@ -1045,6 +1154,7 @@
     out_row = RowReduce(out_grad, out_part, scratch[12:21])
     weights = (up_row, down_row, out_row)
     up_all = RowGather(up_part, up_sum, scratch[21:24])
+    scatter = Scatter(mlp, scratch[24:])
     places = channel_rows(filter_weight.shape[0])
     filter_sums[...] = jnp.zeros_like(filter_sums)
     own = pltpu.make_async_copy(grad_blocks.at[me], grad_gated.at[me], local_sems.at[0])
@@ -1054,8 +1164,8 @@
     )
     for weight in weights:
         weight.pair()
-    own_mlp = pltpu.make_async_copy(mlp.at[me], mlp_own, local_sems.at[1])
-    own_mlp.start()
+    mlp_load = pltpu.make_async_copy(mlp_hbm, mlp, local_sems.at[1])
+    mlp_load.start()
     row_marks(segment, marks, region)
     wait_all(loads[:3])
     gate_out = mixed[:, :channels]
@@ -1068,9 +1178,8 @@
     out_row.plane()
     own.wait()
     wait_all(arriving)
-    mlps = spread(
-        lambda k: mlp.at[peers[k]], lambda k: mlp_recv.at[k], mlp_sems, tensor_devices()
-    )
+    mlp_load.wait()
+    scatter.start()
     grad = grad_gated[...].reshape(length, channels).astype(jnp.float32)
     grad_summed = grad * gate_out
     channel_sums[places.skip : places.skip + 1] = column_sum(grad_summed * product)
@@ -1081,12 +1190,13 @@
     taps = from_bins((real * scale, imag * scale, top * (0.5 / length)), cos_main, sin_main)
     scale = bin_scale(region)
     real, imag, top = (
-        sum(part[:, d * channels : (d + 1) * channels] for d in range(NDOC))
+        sum(part[:, d * channels : (d + 1) * channels] for d in range(SLOTS))
         for part in times(value_small, grad_small, True)
     )
     taps_small = from_bins((real * scale, imag * scale, top * (0.5 / region)), cos_small, sin_small)
     grad_taps[:region] = taps[:region] + taps_small
     grad_taps[region:] = taps[region:]
+    scatter.follow()
     down_row.plane()
     wait_all(loads[3:])
     result = filtered(
@@ -1116,6 +1226,8 @@
         row = places.proj_bias + k
         channel_sums[row : row + 1] = column_sum(running)
         grad_low[:, lanes] = running.astype(jnp.bfloat16)
+    up_row.finish()
+    up_all.plane()
     out_row.cross()
     for block in range(count):
         rows = slice(block * shard, (block + 1) * shard)
@@ -1123,8 +1235,6 @@
         for k in (1, 2):
             total = total + dot_nt(grad_low[rows, k * channels : (k + 1) * channels], proj[k])
         grad_first[block] = total.astype(jnp.bfloat16)
-    up_row.finish()
-    up_all.plane()
     filter_back(
         grad_taps,
         features,
@@ -1140,12 +1250,7 @@
     up_all.pair()
     for weight in (down_row, out_row):
         weight.finish()
-    own_mlp.wait()
-    total = mlp_own[...].astype(jnp.float32)
-    for k, copy in enumerate(mlps):
-        copy.wait()
-        total = total + mlp_recv[k].astype(jnp.float32)
-    mlp_sum[...] = total
+    scatter.finish(mlp_sum)
     up_all.finish()
 
 
@@ -1179,18 +1284,15 @@
     proj_part,
     lines,
     load_sems,
-    block_recv,
-    block_sems,
+    grad_own,
     *scratch,
 ):
-    me = lax.axis_index("tensor")
     count = lax.axis_size("tensor")
-    peers = tensor_peers()
     loads = staged([(first_hbm, first), (grad_low_hbm, grad_low)], load_sems)
     greet(tensor_devices() + [sibling()] + chip_devices())
-    blocks = spread(
-        lambda k: grad_first.at[peers[k]], lambda k: block_recv.at[k], block_sems, tensor_devices()
-    )
+    scatter = Scatter(grad_first, scratch[:5])
+    scatter.start()
+    scratch = scratch[5:]
     row = RowReduce(proj_grad, proj_part, scratch[:6])
     proj_all = RowGather(proj_part, proj_sum, scratch[6:9])
     gathers = (
@@ -1213,6 +1315,7 @@
         ).astype(jnp.bfloat16)
     row.pair()
     row.plane()
+    scatter.follow()
     plain = jnp.zeros_like(gain[...])
     scaled = jnp.zeros_like(gain[...])
     for block in range(count):
@@ -1238,11 +1341,8 @@
     for gather in gathers:
         gather.pair()
     small.finish()
-    grad = grad_first[me].astype(jnp.float32)
-    for k, copy in enumerate(blocks):
-        copy.wait()
-        grad = grad + block_recv[k].astype(jnp.float32)
-    grad_tokens[...] = norm_back(grad, gain[...], hat, rate)
+    scatter.finish(grad_own)
+    grad_tokens[...] = norm_back(grad_own[...], gain[...], hat, rate)
     for gather in gathers + (proj_all,):
         gather.finish()
 
@@ -1345,7 +1445,7 @@
     )(*big)
 
 
-def communicate(kernel, shapes, operands, anywhere, scratch, channel, name):
+def communicate(kernel, shapes, operands, anywhere, scratch, channel, name, limit=60):
     vmem = pl.BlockSpec(memory_space=pltpu.VMEM)
     free = pl.BlockSpec(memory_space=pl.ANY)
     return pl.pallas_call(
@@ -1355,7 +1455,7 @@
         out_specs=[free if i in anywhere[1] else vmem for i in range(len(shapes))],
         scratch_shapes=scratch,
         compiler_params=pltpu.CompilerParams(
-            collective_id=channel, has_side_effects=True, vmem_limit_bytes=60 * 1024 * 1024
+            collective_id=channel, has_side_effects=True, vmem_limit_bytes=limit * 1024 * 1024
         ),
         cost_estimate=pl.CostEstimate(flops=0, bytes_accessed=200_000_000, transcendentals=0),
         name=name,
@@ -1654,20 +1754,20 @@
             vmem(swapped, low),
             vmem((length, channels), single),
             vmem((length, 8), jnp.int32),
-            vmem((shard_len, model_width), low),
-            vmem((groups - 1, shard_len, model_width), low),
+            vmem(blocked, low),
             vmem((model_width // rows, units), low),
             semaphores((10,)),
             semaphores((2,)),
-            semaphores((2, groups - 1)),
             semaphores((2, groups - 1)),
         ]
         + row_reduce_scratch(up_grad.shape, chips)
         + row_reduce_scratch(down_grad.shape, chips)
         + row_reduce_scratch(out_grad.shape, chips)
-        + row_gather_scratch(chips),
+        + row_gather_scratch(chips)
+        + scatter_scratch(blocked),
         2,
         "back",
+        63,
     )
     (
         grad_tokens,
@@ -1715,9 +1815,9 @@
             vmem((3 * model_width // rows, channels), low),
             vmem((8, model_width), single),
             semaphores((2,)),
-            vmem((groups - 1, shard_len, model_width), low),
-            semaphores((2, groups - 1)),
+            vmem((shard_len, model_width), single),
         ]
+        + scatter_scratch(blocked)
         + row_reduce_scratch((3 * model_width, channels), chips)
         + row_gather_scratch(chips) * 3
         + small_sums_scratch(

time: 313 us -> 299 us (0.955)
  Pallas kernels: 305 us -> 290 us
    pallas_call x4, Pallas kernels: 295 us -> 280 us  [communicate(): pl.pallas_call(kernel, out_shape=shapes, in_specs=[free if i in anywhere[...]
where the time goes in v5:
time: 299 us; the launch traced here: 293 us
  Pallas kernels  290 us (97%)
    pallas_call x4, Pallas kernels, communicate(): pl.pallas_call(kernel, out_shape=shapes, in_specs=[free if i in anywhere[...  280 us
    pallas_call x1, Pallas kernels, finish(): pl.pallas_call(finish_kernel, grid=(steps,), in_specs=in_specs, out_specs...  9.88 us

profile of v5, /device:TPU:0, one launch (start us, length us, event | category | flops | bytes accessed | tf_op | source)
XLA Modules:
  0.0 292.9 jit_solution(5503138107692719290)
XLA Ops:
  0.7 0.0 copy-start
  0.7 1.0 copy-done
  1.7 0.6 constant_dynamic-slice_fusion.part
  2.3 92.2 %front.1 = (bf16[4,256,1024]{2,1,0:T(8,128)(2,1)}, bf16[4,4,2,32,1024]{4,3,2,1,0:T(8,128)(2,1)}, bf16[4,256,1024]{2,1,0:T(8,128)(2,1)}, f32[3,64,1024]{2,1,0:T(8...) custom-call(bf16[256,1024]{1,0:T(8,128)(2,1)} %bitcast.29, ...), custom_call_target="tpu_custom_call" | custom-call | bytes 200000000 | tf_op jit(solution)/shard_map/front/pallas_call | solution.py:1451
  94.6 75.4 %middle.1 = (f32[256,1024]{1,0:T(8,128)}, bf16[4,256,1024]{2,1,0:T(8,128)(2,1)}, bf16[1024,1024]{1,0:T(8,128)(2,1)}, bf16[1024,1024]{1,0:T(8,128)(2,1)}, f32[1,1...) custom-call(bf16[256,1024]{1,0:T(8,128)(2,1)} %get-tuple-element.90., ...), custom_call_target="tpu_custom_call" | custom-call | bytes 200000000 | tf_op jit(solution)/shard_map/middle/pallas_call | solution.py:1451
  169.9 59.0 %back.1 = (bf16[4,256,1024]{2,1,0:T(8,128)(2,1)}, bf16[1024,768]{1,0:T(8,128)(2,1)}, f32[256,1024]{1,0:T(8,128)}, bf16[1024,1024]{1,0:T(8,128)(2,1)}, bf16[128,1...) custom-call(bf16[4,256,256]{2,1,0:T(8,128)(2,1)} %get-tuple-element.94.grad_blocks, ...), custom_call_target="tpu_custom_call" | custom-call | bytes 200000000 | tf_op jit(solution)/shard_map/back/pallas_call | solution.py:1451
  229.0 53.8 %final.1 = (f32[256,1024]{1,0:T(8,128)}, bf16[3072,256]{1,0:T(8,128)(2,1)}, bf16[1024,1024]{1,0:T(8,128)(2,1)}, bf16[256,1024]{1,0:T(8,128)(2,1)}, f32[8,1024]{1...) custom-call(bf16[4,256,1024]{2,1,0:T(8,128)(2,1)} %get-tuple-element.110.grad_first, ...), custom_call_target="tpu_custom_call" | custom-call | bytes 200000000 | tf_op jit(solution)/shard_map/final/pallas_call | solution.py:1451
  282.8 0.0 copy-start.1
  282.8 9.9 %finish.1 = (bf16[256,1024]{1,0:T(8,128)(2,1)}, f32[256,1024]{1,0:T(8,128)}, f32[3072,256]{1,0:T(8,128)}, f32[1024,1024]{1,0:T(8,128)}, f32[1024,1024]{1,0:T(8,1...) custom-call(f32[256,1024]{1,0:T(8,128)} %get-tuple-element.89.residu, ...), custom_call_target="tpu_custom_call" | custom-call | tf_op jit(solution)/shard_map/finish/pallas_call | solution.py:1435
  292.7 0.0 copy-done.1
Async XLA Ops:
  0.7 1.1 copy-start
  282.8 9.9 %copy-start.1 = (bf16[256,1024]{1,0:T(8,128)(2,1)S(1)}, bf16[256,1024]{1,0:T(8,128)(2,1)}, u32[]{:S(2)}) copy-start(bf16[256,1024]{1,0:T(8,128)(2,1)} %param.46) | copy-start | bytes 1572868
